TPU v7x, 32 devices: a whole 2x2x4 slice. The times are simulated.
32 devices in a mesh: groups: 2 (over x), slab: 16 (over z, y, core).
Axes of the slice: x: 2, y: 2, z: 4, core: 2. Of those that a mesh axis runs over, the one named last changes fastest.
Arguments:
- volume: bfloat16 [32, 128, 80, 256], P(None, ('groups', 'slab')), parts along dimension 1, may hold values from -6 to 6
- weights: bfloat16 [3, 3, 3, 32, 64], replicated, may hold values from -0.21875 to 0.21875
- bias: float32 [64], replicated, may hold values from -4 to 4
- upstream: bfloat16 [64, 64, 40, 128], P(None, ('groups', 'slab')), parts along dimension 1, may hold values from -6 to 6
Outputs:
- input_grad: bfloat16 [32, 128, 80, 256], P(None, ('groups', 'slab')), parts along dimension 1
- weight_grad: float32 [6, 3, 3, 32, 64], P('groups'), parts along dimension 0
- bias_grad: float32 [128], P('groups'), parts along dimension 0
There are 2 independent parts, one for each index of `groups`. A program takes and returns all parts, laid end to end along the dimension named above; an argument that names none is the same for every part. Nothing has to cross between parts.
All inputs are finite; a program needn't handle non-finite values.
Results may differ from a plain program's by a relative error of at most 0.005.
Values may be sent and summed in bfloat16 or wider, within the bound.
No kernel may reach another device: no remote copies, remote signals or barrier semaphores. Data moves between devices by JAX's collectives and lax.ppermute only.
A program may use at most 192 MiB of HBM per device.

v0:
```python
import jax
import jax.numpy as jnp
from jax import lax
from jax.sharding import PartitionSpec as P


def shifted(x, axis, by):
    peers = lax.axis_size(axis)
    pairs = [(i, i + by) for i in range(peers) if 0 <= i + by < peers]
    return lax.ppermute(x, axis, pairs)


def forward_conv(field, kernel):
    return lax.conv_general_dilated(
        field[None],
        kernel,
        (2, 2, 2),
        ((0, 0), (1, 0), (1, 0)),
        dimension_numbers=("NCDHW", "DHWIO", "NCDHW"),
        preferred_element_type=jnp.float32,
    )[0]


def kernel_conv(field, grads):
    result = lax.conv_general_dilated(
        field[None],
        grads[None],
        (1, 1, 1),
        ((0, 0), (1, 0), (1, 0)),
        rhs_dilation=(2, 2, 2),
        dimension_numbers=("CNDHW", "IODHW", "NCDHW"),
        preferred_element_type=jnp.float32,
    )
    return jnp.transpose(result, (2, 3, 4, 0, 1))


def shards(volume, weights, bias, upstream):
    depth_in = volume.shape[1]
    below = shifted(volume[:, depth_in - 1 :], "slab", 1)
    field = jnp.concatenate([below, volume], 1)
    pre = forward_conv(field, weights)
    pre = pre + bias[:, None, None, None]
    slope = 0.2 + 0.8 * jax.nn.sigmoid(pre)
    pre_grad = (upstream.astype(jnp.float32) * slope).astype(jnp.bfloat16)
    above = shifted(pre_grad[:, 0:1], "slab", -1)
    weight_grad = kernel_conv(field, pre_grad)
    bias_grad = jnp.sum(pre_grad.astype(jnp.float32), axis=(1, 2, 3))
    weight_grad, bias_grad = lax.psum((weight_grad, bias_grad), "slab")
    extended = jnp.concatenate([pre_grad, above], 1)
    flipped = weights[::-1, ::-1, ::-1]
    total = lax.conv_general_dilated(
        extended[None],
        flipped,
        (1, 1, 1),
        ((1, 0), (1, 2), (1, 2)),
        lhs_dilation=(2, 2, 2),
        dimension_numbers=("NCDHW", "DHWOI", "NCDHW"),
        preferred_element_type=jnp.float32,
    )[0]
    input_grad = total.astype(jnp.bfloat16)
    return (input_grad, weight_grad, bias_grad)


def solution(mesh):
    placed = (
        P(None, ("groups", "slab"), None, None),
        P(),
        P(),
        P(None, ("groups", "slab"), None, None),
    )
    return jax.shard_map(
        shards,
        mesh=mesh,
        in_specs=placed,
        out_specs=(
            P(None, ("groups", "slab"), None, None),
            P("groups", None, None, None, None),
            P("groups"),
        ),
        check_vma=False,
    )
```

profile of v0, /device:TPU:0, one launch (start us, length us, event | category | flops | bytes accessed | tf_op | source)
XLA Modules:
  0.0 493.3 jit_solution(17768367693676166440)
XLA Ops:
  7.2 0.0 all-reduce.2.cloned.1.call-start
  7.2 1.5 slice.6
  8.7 3.6 collective-permute-start
  12.3 14.0 %copy.56 = bf16[32,4,80,256]{2,0,3,1:T(8,128)(2,1)} copy(bf16[32,4,80,256]{3,2,1,0:T(8,128)(2,1)} %param.4) | data formatting | bytes 10485760 | tf_op args[0]
  26.4 4.4 copy.54
  30.8 3.3 copy.55
  34.1 9.5 %fusion.8 = (bf16[1,32,5,80,256]{3,1,4,2,0:T(8,128)(2,1)}, bf16[32,5,80,1,256]{2,0,4,1,3:T(8,128)(2,1)S(1)}) fusion(bf16[32,4,80,256]{2,0,3,1:T(8,128)(2,1)} %copy.56, bf16[32,1,80,256]{2,0,3,1:T(8,128)(2,1)S(1)} %copy.55), kind=kLoop, calls=%fused_computation.12 | loop fusion | flops 3276800 | bytes 19660800 | tf_op jit(solution)/shard_map/broadcast_in_dim | solution.py:15
  43.6 5.4 %pad = bf16[32,5,80,1,272]{2,0,4,1,3:T(8,128)(2,1)} pad(bf16[32,5,80,1,256]{2,0,4,1,3:T(8,128)(2,1)S(1)} %get-tuple-element.18, bf16[]{:T(256)} %constant.10), padding=0_0x0_0x0_0x0_0x1_15 | pad | bytes 13516802 | tf_op jit(solution)/shard_map/broadcast_in_dim | solution.py:15
  49.0 31.5 %copy.58 = bf16[32,5,80,1,8,34]{0,4,5,2,1,3:T(8,128)(2,1)} copy(bf16[32,5,80,1,8,34]{2,0,5,4,1,3:T(8,128)(2,1)} %bitcast.54) | data formatting | bytes 13926400 | tf_op jit(solution)/shard_map/conv_general_dilated | solution.py:14
  80.5 1.9 slice.12
  82.5 21.7 %broadcast_select_fusion = f32[2,40,8,17,64]{4,2,3,1,0:T(8,128)} fusion(pred[8,17]{0,1:T(8,128)(4,1)S(1)} %copy-done.6, bf16[3,3,3,32,64]{4,3,2,1,0:T(8,128)(2,1)S(1)} %copy-done, bf16[32,5,80,1,7,2]{0,4,5,2,1,3:T(8,128)(2,1)S(1)} %slice.12, bf16[32,5,80,1,8,34]{0,4,5,2,1,3:T(8,128)(2,1)} %copy.58), kind=kOutput, calls=%fused_computation.33 | convolution fusion | flops 1216028672 | bytes 10217608 | tf_op jit(solution)/shard_map/conv_general_dilated | solution.py:14
  104.2 3.8 copy.59
  108.0 2.6 convert_reduce_fusion
  110.6 1.2 slice.14
  111.8 3.0 copy.60
  114.8 1.3 collective-permute-start.1
  116.1 92.3 %copy.66 = bf16[1,32,5,80,256]{1,0,4,3,2:T(2,128)(2,1)} copy(bf16[1,32,5,80,256]{3,1,4,2,0:T(8,128)(2,1)} %get-tuple-element.17) | data formatting | bytes 13107200 | tf_op jit(solution)/shard_map/broadcast_in_dim | solution.py:15
  208.4 153.2 %fusion.18 = f32[3,3,3,32,64]{4,3,2,1,0:T(8,128)} fusion(bf16[1,32,5,80,256]{1,0,4,3,2:T(2,128)(2,1)} %copy.66, bf16[1,64,2,40,128]{1,3,4,2,0:T(8,128)(2,1)S(1)} %bitcast.58), kind=kOutput, calls=%fused_computation.24 | convolution fusion | flops 1120100352 | bytes 8085504 | tf_op jit(solution)/shard_map/transpose | solution.py:34
  361.6 0.0 all-reduce.2.cloned.1.call-update
  361.6 36.0 %psum.15 = f32[64]{0:T(128)} all-reduce(f32[64]{0:T(128)S(1)} %copy-done.5), channel_id=1, replica_groups=mesh['groups'=2,'slab'=16] {'slab'}, use_global_device_ids=true, to_apply=%region_2.0 | all-reduce | flops 64 | bytes 512 | tf_op jit(solution)/shard_map/psum | solution.py:48
  397.7 2.9 copy.61
  400.6 2.2 maximum_bitcast_fusion
  402.7 0.8 pad.2
  403.5 0.5 copy.63
  404.1 0.1 slice.15
  404.1 0.9 fusion.43
  405.1 22.4 %fusion.22 = bf16[4,80,8,34,32]{4,2,3,1,0:T(8,128)(2,1)} fusion(bf16[3,3,3,32,64]{4,3,2,1,0:T(8,128)(2,1)S(1)} %copy-done, bf16[64,3,40,8,18]{0,3,4,2,1:T(8,128)(2,1)S(1)} %fusion.43), kind=kOutput, calls=%fused_computation.28 | convolution fusion | flops 1193213952 | bytes 7892992 | tf_op jit(solution)/shard_map/conv_general_dilated | solution.py:51
  427.5 26.7 %copy.64 = bf16[4,80,8,34,32]{1,4,3,2,0:T(8,128)(2,1)} copy(bf16[4,80,8,34,32]{4,2,3,1,0:T(8,128)(2,1)} %fusion.22) | data formatting | bytes 11141120 | tf_op jit(solution)/shard_map/conv_general_dilated | solution.py:51
  454.2 8.9 %select_convert_fusion = bf16[4,80,8,34,32]{1,4,3,2,0:T(8,128)(2,1)} fusion(bf16[4,80,8,34,32]{1,4,3,2,0:T(8,128)(2,1)} %copy.64, pred[8,34]{1,0:T(8,128)(4,1)S(1)} %copy-done.3), kind=kLoop, calls=%fused_computation.5 | loop fusion | flops 2785280 | bytes 11141392 | tf_op jit(solution)/shard_map/convert_element_type | solution.py:60
  463.1 8.4 %slice_bitcast_fusion = bf16[32,4,80,256]{2,0,3,1:T(8,128)(2,1)} fusion(bf16[4,80,1,272,32]{1,4,3,0,2:T(8,128)(2,1)} %bitcast.55), kind=kLoop, calls=%fused_computation.10 | loop fusion | bytes 10485760 | tf_op jit(solution)/shard_map/convert_element_type | solution.py:60
  471.5 13.1 %copy.68 = bf16[32,4,80,256]{3,2,1,0:T(8,128)(2,1)} copy(bf16[32,4,80,256]{2,0,3,1:T(8,128)(2,1)} %slice_bitcast_fusion) | data formatting | bytes 10485760
  484.6 1.8 copy.74
  (17 shorter events, 0.0 us)
Async XLA Ops:
  7.2 75.3 %copy-start = (bf16[3,3,3,32,64]{4,3,2,1,0:T(8,128)(2,1)S(1)}, bf16[3,3,3,32,64]{4,3,2,1,0:T(8,128)(2,1)}, u32[]{:S(2)}) copy-start(bf16[3,3,3,32,64]{4,3,2,1,0:T(8,128)(2,1)} %param.5) | copy-start | bytes 331780
  7.2 477.4 %all-reduce.2.cloned.1.call-start = ((), (), s32[]{:S(2)}) async-start(), calls=%async_computation | async-start | bytes 884736 | tf_op jit(solution)/shard_map/psum | solution.py:48
  8.7 17.7 %copy-start.2 = (bf16[64,2,40,128]{3,2,1,0:T(8,128)(2,1)S(1)}, bf16[64,2,40,128]{3,2,1,0:T(8,128)(2,1)}, u32[]{:S(2)}) copy-start(bf16[64,2,40,128]{3,2,1,0:T(8,128)(2,1)} %param.7) | copy-start | bytes 3932164
  8.7 22.1 %collective-permute-start = (bf16[32,1,80,256]{3,2,1,0:T(8,128)(2,1)S(1)}, bf16[32,1,80,256]{3,2,1,0:T(8,128)(2,1)}, u32[]{:S(2)}, u32[]{:S(2)}) collective-permute-start(bf16[32,1,80,256]{3,2,1,0:T(8,128)(2,1)S(1)} %slice.6), channel_id=1, source_target_pairs={{0,1},{1,2},{2,3},{3,4},{4,5},{5,6},{6,7},{7,8},{8,9},{9,10},{10,1... | collective-permute-start | bytes 3932168 | tf_op jit(solution)/shard_map/ppermute | solution.py:10
  49.0 33.5 %copy-start.6 = (pred[8,17]{0,1:T(8,128)(4,1)S(1)}, pred[8,17]{0,1:T(8,128)(4,1)}, u32[]{:S(2)}) copy-start(pred[8,17]{0,1:T(8,128)(4,1)} %constant.19) | copy-start | bytes 412
  104.2 3.8 copy-start.1
  104.2 3.8 copy-start.4
  114.8 282.9 %collective-permute-start.1 = (bf16[64,1,40,128]{3,2,1,0:T(8,128)(2,1)}, bf16[64,1,40,128]{3,2,1,0:T(8,128)(2,1)}, u32[]{:S(2)}, u32[]{:S(2)}) collective-permute-start(bf16[64,1,40,128]{3,2,1,0:T(8,128)(2,1)} %copy.60), channel_id=1, source_target_pairs={{1,0},{2,1},{3,2},{4,3},{5,4},{6,5},{7,6},{8,7},{9,8},{10,9},{11,1... | collective-permute-start | bytes 1966088 | tf_op jit(solution)/shard_map/ppermute | solution.py:10
  208.4 153.3 %copy-start.5 = (f32[64]{0:T(128)S(1)}, f32[64]{0:T(128)}, u32[]{:S(2)}) copy-start(f32[64]{0:T(128)} %get-tuple-element.15) | copy-start | bytes 772
  427.5 26.7 %copy-start.3 = (pred[8,34]{1,0:T(8,128)(4,1)S(1)}, pred[8,34]{1,0:T(8,128)(4,1)}, u32[]{:S(2)}) copy-start(pred[8,34]{1,0:T(8,128)(4,1)} %constant.18) | copy-start | bytes 820
Sparse Core Ops, SparseCore 0:
  361.7 93.1 all-reduce.1
where the time goes:
time: 502 us; the launch traced here: 493 us
  local copies, waits for them, and re-layouts  217 us (43%)
  matrix products  197 us (39%)
  blocking collectives  36 us (7%)
  other arithmetic  24.1 us (5%)
  between operations  14.2 us (3%)
    transpose x1, matrix products, kernel_conv(): return jnp.transpose(result, (2, 3, 4, 0, 1))  153 us
    broadcast_in_dim x2, local copies, waits for them, and re-layouts, forward_conv(): field[None]  97.7 us
    conv_general_dilated x3, local copies, waits for them, and re-layouts, forward_conv(): lax.conv_general_dilated(field[None], kernel, (2, 2, 2), ((0, 0), (1, 0),...  37.3 us
    psum x1, blocking collectives, shards(): weight_grad, bias_grad = lax.psum((weight_grad, bias_grad), 'slab')  36 us
    unnamed x18, local copies, waits for them, and re-layouts  33.4 us
    conv_general_dilated x3, local copies, waits for them, and re-layouts, shards(): lax.conv_general_dilated(extended[None], flipped, (1, 1, 1), ((1, 0), (1,...  27.3 us
    conv_general_dilated x1, matrix products, shards(): lax.conv_general_dilated(extended[None], flipped, (1, 1, 1), ((1, 0), (1,...  22.4 us
    conv_general_dilated x1, matrix products, forward_conv(): lax.conv_general_dilated(field[None], kernel, (2, 2, 2), ((0, 0), (1, 0),...  21.7 us
  transfers between devices with their start and end apart: 3, of which 0 were waited for; matrix products, arithmetic and copies ran while one was open for 71% of the time, Pallas kernels for 0%

commit v1 on v0

v1 whole, which is shorter than its diff:
```python
import functools

import jax
import jax.numpy as jnp
from jax import lax
from jax.experimental import pallas as pl
from jax.experimental.pallas import tpu as pltpu
from jax.sharding import PartitionSpec as P

BF = jnp.bfloat16
F32 = jnp.float32
VMEM = pl.BlockSpec(memory_space=pltpu.VMEM)
PARAMS = pltpu.CompilerParams(vmem_limit_bytes=50 * 2**20)


def shape(*dims, dtype=BF):
    return jax.ShapeDtypeStruct(dims, dtype)


def cost(flops, size):
    return pl.CostEstimate(flops=flops, bytes_accessed=size, transcendentals=0)


def picks(half, inverse):
    if inverse:
        row = lax.broadcasted_iota(jnp.int32, (2 * half, 2 * half), 0)
        col = lax.broadcasted_iota(jnp.int32, (2 * half, 2 * half), 1)
        hit = jnp.where(row < half, 2 * row, 2 * (row - half) + 1) == col
    else:
        row = lax.broadcasted_iota(jnp.int32, (2 * half, 3 * half), 0)
        col = lax.broadcasted_iota(jnp.int32, (2 * half, 3 * half), 1)
        early = 2 * col - 1
        even = 2 * (col - half)
        odd = 2 * (col - 2 * half) + 1
        hit = jnp.where(col < half, early, jnp.where(col < 2 * half, even, odd)) == row
    return jnp.where(hit, 1.0, 0.0).astype(BF)


def split_plane(read, lines, table):
    rows, channels, half = lines.shape
    channels //= 3
    lines[0] = jnp.zeros((3 * channels, half), BF)

    def step(t, carry):
        block = jnp.swapaxes(read(pl.multiple_of(t * 16, 16)), 0, 1)
        flat = block.reshape(16 * channels, 2 * half)
        taps = jnp.dot(flat, table, preferred_element_type=F32).astype(BF)
        taps = taps.reshape(16, channels, 3 * half)
        for e in range(3):
            lines[pl.ds(1 + t * 16, 16), e * channels : (e + 1) * channels, :] = taps[
                :, :, e * half : (e + 1) * half
            ]
        return carry

    lax.fori_loop(0, (rows - 1) // 16, step, 0)


def turn_upstream(upstream, turned):
    for o in range(0, upstream.shape[0], 8):
        block = upstream[o : o + 8].astype(F32)
        turned[:, o : o + 8, :] = jnp.swapaxes(block, 0, 1)


def earlier(values):
    cells = values.shape[-1]
    lane = lax.broadcasted_iota(jnp.int32, values.shape, values.ndim - 1)
    return jnp.where(lane == cells - 1, 0.0, pltpu.roll(values, cells - 1, values.ndim - 1))


def store_grads(pre, upstream, grads, j):
    slope = 0.2 + 0.8 * jax.nn.sigmoid(pre)
    value = (upstream * slope).astype(BF)
    cout = value.shape[0]
    grads[j, :cout, :] = value
    grads[j, cout:, :] = earlier(value.astype(F32)).astype(BF)


def window(planes, j, count):
    parts = [plane[pl.ds(2 * j, count)].reshape(-1, plane.shape[-1]) for plane in planes]
    return parts[0] if len(parts) == 1 else jnp.concatenate(parts, 0)


def weight_terms(planes, grads):
    cells = grads.shape[-1]
    cout = grads.shape[1] // 2
    left, right = [], []
    ones = jnp.ones((16, cells), BF)
    for j in range(grads.shape[0] - 1):
        lines = [p[1 + 2 * j : 3 + 2 * j].reshape(-1, cells) for p in planes]
        left.append(jnp.concatenate(lines + [ones], 0))
        right.append(jnp.concatenate([grads[j, :cout], grads[j + 1, :cout]], 0))
    return lax.dot_general(
        jnp.concatenate(left, 1),
        jnp.concatenate(right, 1),
        (((1,), (1,)), ((), ())),
        preferred_element_type=F32,
    )


def first_kernel(
    volume, weights, bias, upstream,
    lines_out, pre_out, grads, terms, back, front,
    extra, turned, turned_weights,
):
    cin, depth = volume.shape[0], volume.shape[1]
    cout = bias.shape[0]
    half = volume.shape[3] // 2
    ny = upstream.shape[2]
    table = picks(half, False)
    planes = [lines_out.at[0], lines_out.at[1], extra.at[0], extra.at[1]]
    for z in range(4):
        split_plane(lambda y, z=z: volume[:, z, pl.ds(y, 16), :], planes[z], table)
    for a in range(3):
        for b in range(3):
            block = jnp.concatenate([weights[a, b, e] for e in range(3)], 0)
            turned_weights[:, a, b * 3 * cin : (b + 1) * 3 * cin] = block.T
    front[...] = turned_weights[:, 0, :]
    blank = jnp.zeros((cin, cout), BF)
    for a in range(3):
        for px in range(2):
            for py in range(2):
                row = []
                for dy in range(2):
                    for dx in range(2):
                        b, e = py + 1 - 2 * dy, px + 1 - 2 * dx
                        row.append(weights[a, b, e] if b >= 0 and e >= 0 else blank)
                at = (px * 2 + py) * cin
                back[a, at : at + cin, :] = jnp.concatenate(row, 1)
    turn_upstream(upstream.at[:, 1], turned)
    full = jnp.concatenate([turned_weights[:, a, :] for a in range(3)], 1)
    late = jnp.concatenate([turned_weights[:, a, :] for a in (1, 2)], 1)
    offset = bias[...]

    def upper(t, carry):
        field = jnp.concatenate([window(planes[1:], t * 8 + q, 3) for q in range(8)], 1)
        pre = jnp.dot(full, field, preferred_element_type=F32)
        for q in range(8):
            j = t * 8 + q
            store_grads(pre[:, q * half : (q + 1) * half] + offset, turned[j], grads, j)
        return carry

    def lower(t, carry):
        field = jnp.concatenate([window(planes[:2], t * 8 + q, 3) for q in range(8)], 1)
        pre = jnp.dot(late, field, preferred_element_type=F32)
        for q in range(8):
            pre_out[t * 8 + q] = pre[:, q * half : (q + 1) * half] + offset
        return carry

    lax.fori_loop(0, ny // 8, upper, 0)
    grads[ny] = jnp.zeros(grads.shape[1:], BF)
    terms[...] = weight_terms(planes[1:], grads)
    lax.fori_loop(0, ny // 8, lower, 0)


def second_kernel(
    halo, lines, pre_in, upstream, front, terms_in,
    grads, packed,
    below, turned,
):
    half = below.shape[-1]
    cout = front.shape[0]
    ny = pre_in.shape[0]
    table = picks(half, False)
    split_plane(lambda y: halo[:, 0, pl.ds(y, 16), :], below, table)
    turn_upstream(upstream.at[:, 0], turned)

    def body(t, carry):
        field = jnp.concatenate([window([below], t * 8 + q, 3) for q in range(8)], 1)
        pre = jnp.dot(front[...], field, preferred_element_type=F32)
        for q in range(8):
            j = t * 8 + q
            store_grads(pre[:, q * half : (q + 1) * half] + pre_in[j], turned[j], grads, j)
        return carry

    lax.fori_loop(0, ny // 8, body, 0)
    grads[ny] = jnp.zeros(grads.shape[1:], BF)
    terms = terms_in[...] + weight_terms([below, lines.at[0], lines.at[1]], grads)
    count = below.shape[1]
    for a in range(3):
        packed[a * count : (a + 1) * count] = terms[(2 * a + 1) * count : (2 * a + 2) * count]
    middle = jnp.concatenate([terms[2 * a * count : (2 * a + 1) * count, :cout] for a in range(3)], 0)
    rows = middle.shape[0] // 2
    packed[3 * count : 3 * count + rows] = jnp.concatenate([middle[:rows], middle[rows:]], 1)
    packed[3 * count + rows :] = jnp.concatenate(
        [terms[6 * count :][:, :cout], jnp.zeros((16, cout), F32)], 1
    )


def finish_kernel(packed, weight_grad, bias_grad):
    count = weight_grad.shape[2]
    cout = weight_grad.shape[3]
    for a in range(3):
        block = packed[a * count : (a + 1) * count]
        weight_grad[a, 2] = block[:, :cout]
        weight_grad[a, 0] = block[:, cout:]
    rows = 3 * count // 2
    middle = packed[3 * count : 3 * count + rows]
    middle = jnp.concatenate([middle[:, :cout], middle[:, cout:]], 0)
    for a in range(3):
        weight_grad[a, 1] = middle[a * count : (a + 1) * count]
    bias_grad[...] = packed[3 * count + rows :][:1, :cout]


def back_kernel(odd, fresh, aliased, *refs):
    refs = refs[1:] if aliased else refs
    if odd:
        back, grads, above, out = refs[:4]
        left = jnp.concatenate([back[2], back[0]], 1)
    else:
        back, grads, out = refs[:3]
        left = back[1]
    if fresh:
        shifted = refs[4]
        cout = above.shape[1]
        shifted[:, :cout, :] = above[...]
        shifted[:, cout:, :] = earlier(above[...].astype(F32)).astype(BF)
        above = None
    cin = out.shape[0]
    half = out.shape[3] // 2
    ny = grads.shape[0] - 1
    table = picks(half, True)

    def pair(ref, j):
        return ref[pl.ds(j, 2)].reshape(-1, half)

    def step(t, carry):
        columns = []
        for q in range(8):
            j = t * 8 + q
            parts = [pair(grads, j)]
            if fresh:
                parts.append(shifted[j])
                nxt = shifted[jnp.minimum(j + 1, ny - 1)]
                parts.append(nxt if q < 7 else jnp.where(j + 1 < ny, nxt, jnp.zeros_like(nxt)))
            elif odd:
                parts.append(pair(above, j))
            columns.append(jnp.concatenate(parts, 0))
        total = jnp.dot(left, jnp.concatenate(columns, 1), preferred_element_type=F32)
        total = total.astype(BF)
        rows = []
        for q in range(8):
            for py in range(2):
                lanes = slice(q * half, (q + 1) * half)
                even = total[py * cin : (py + 1) * cin, lanes]
                odds = total[(2 + py) * cin : (3 + py) * cin, lanes]
                rows.append(jnp.concatenate([even, odds], 1))
        merged = jnp.dot(jnp.concatenate(rows, 0), table, preferred_element_type=F32)
        merged = merged.astype(BF).reshape(16, cin, 2 * half)
        out[:, 0, pl.ds(pl.multiple_of(t * 16, 16), 16), :] = jnp.swapaxes(merged, 0, 1)
        return carry

    lax.fori_loop(0, ny // 8, step, 0)


def back_plane(z, total, full, back, grads, above=None, fresh=False):
    cin, depth, height, width = full
    args = [back, grads] + ([above] if above is not None else [])
    aliased = total is not None
    specs = [pl.BlockSpec(a.shape, lambda g, n=a.ndim: (0,) * n) for a in args]
    if aliased:
        args = [total] + args
        specs = [pl.BlockSpec(memory_space=pl.ANY)] + specs
    scratch = [pltpu.VMEM((above.shape[0], 2 * above.shape[1], above.shape[2]), BF)] if fresh else []
    return pl.pallas_call(
        functools.partial(back_kernel, above is not None, fresh, aliased),
        grid=(1,),
        in_specs=specs,
        out_specs=pl.BlockSpec((cin, 1, height, width), lambda g: (0, z, 0, 0)),
        out_shape=shape(*full),
        scratch_shapes=scratch,
        input_output_aliases={0: 0} if aliased else {},
        compiler_params=PARAMS,
        cost_estimate=cost(4 * 10**9, 4 * 2**20),
    )(*args)


def all_sum(value, axis):
    peers = lax.axis_size(axis)
    if peers & (peers - 1):
        return lax.psum(value, axis)
    if peers == 1:
        return value
    swap = [(i, i ^ 1) for i in range(peers)]
    odd = lax.axis_index(axis) & 1
    rows = value.shape[0] // 2
    halves = value.reshape(2, rows, value.shape[1])
    mine = lax.dynamic_index_in_dim(halves, odd, 0, False)
    other = lax.dynamic_index_in_dim(halves, 1 - odd, 0, False)
    mine = mine + lax.ppermute(other, axis, swap)
    step = 2
    while step < peers:
        mine = mine + lax.ppermute(mine, axis, [(i, i ^ step) for i in range(peers)])
        step *= 2
    other = lax.ppermute(mine, axis, swap)
    low = jnp.where(odd == 0, mine, other)
    high = jnp.where(odd == 0, other, mine)
    return jnp.concatenate([low, high], 0)


def shifted(x, axis, by):
    peers = lax.axis_size(axis)
    pairs = [(i, i + by) for i in range(peers) if 0 <= i + by < peers]
    return lax.ppermute(x, axis, pairs)


def shards(volume, weights, bias, upstream):
    cin, depth, height, width = volume.shape
    cout = bias.shape[0]
    ny, half = height // 2, width // 2
    rows, count = height + 1, 3 * cin
    halo = shifted(volume[:, depth - 1 :], "slab", 1)
    lines, pre, upper, terms, back, front = pl.pallas_call(
        first_kernel,
        in_specs=[VMEM] * 4,
        out_specs=[VMEM] * 6,
        out_shape=[
            shape(2, rows, count, half),
            shape(ny, cout, half, dtype=F32),
            shape(ny + 1, 2 * cout, half),
            shape(6 * count + 16, 2 * cout, dtype=F32),
            shape(3, 4 * cin, 4 * cout),
            shape(cout, 3 * count),
        ],
        scratch_shapes=[
            pltpu.VMEM((2, rows, count, half), BF),
            pltpu.VMEM((ny, cout, half), F32),
            pltpu.VMEM((cout, 3, 3 * count), BF),
        ],
        compiler_params=PARAMS,
        cost_estimate=cost(10 * 10**9, 20 * 2**20),
    )(volume, weights, bias.reshape(cout, 1), upstream)
    full = volume.shape
    total = back_plane(2, None, full, back, upper)
    total, halo = lax.optimization_barrier((total, halo))
    lower, packed = pl.pallas_call(
        second_kernel,
        in_specs=[VMEM] * 6,
        out_specs=[VMEM] * 2,
        out_shape=[
            shape(ny + 1, 2 * cout, half),
            shape(9 * count // 2 + 16, 2 * cout, dtype=F32),
        ],
        scratch_shapes=[
            pltpu.VMEM((rows, count, half), BF),
            pltpu.VMEM((ny, cout, half), F32),
        ],
        compiler_params=PARAMS,
        cost_estimate=cost(5 * 10**9, 10 * 2**20),
    )(halo, lines, pre, upstream, front, terms)
    above = shifted(lower[:ny, :cout], "slab", -1)
    packed = all_sum(packed, "slab")
    total = back_plane(0, total, full, back, lower)
    total = back_plane(1, total, full, back, lower, upper)
    total = back_plane(3, total, full, back, upper, above, True)
    weight_grad, bias_grad = pl.pallas_call(
        finish_kernel,
        in_specs=[VMEM],
        out_specs=[VMEM] * 2,
        out_shape=[shape(3, 3, count, cout, dtype=F32), shape(1, cout, dtype=F32)],
        compiler_params=PARAMS,
    )(packed)
    return (
        total,
        weight_grad.reshape(3, 3, 3, cin, cout),
        bias_grad.reshape(cout),
    )


def solution(mesh):
    placed = (
        P(None, ("groups", "slab"), None, None),
        P(),
        P(),
        P(None, ("groups", "slab"), None, None),
    )
    return jax.shard_map(
        shards,
        mesh=mesh,
        in_specs=placed,
        out_specs=(
            P(None, ("groups", "slab"), None, None),
            P("groups", None, None, None, None),
            P("groups"),
        ),
        check_vma=False,
    )
```

time: 502 us -> 75.6 us (0.15)
  the two profiles are of different devices: /device:TPU:0 before, /device:TPU:1 now
where the time goes in v1:
time: 75.6 us; the launch traced here: 75.2 us
  Pallas kernels  41.6 us (55%)
  starting transfers between devices  14 us (19%)
  waiting for transfers between devices  11.6 us (15%)
  local copies, waits for them, and re-layouts  7.14 us (9%)
  between operations  0.76 us (1%)
    pallas_call x1, Pallas kernels, shards(): pl.pallas_call(first_kernel, in_specs=[VMEM] * 4, out_specs=[VMEM] * 6, o...  18.4 us
    pallas_call x4, Pallas kernels, back_plane(): pl.pallas_call(functools.partial(back_kernel, above is not None, fresh, a...  14.3 us
    ppermute x2, starting transfers between devices, shifted(): return lax.ppermute(x, axis, pairs)  8.84 us
    pallas_call x1, Pallas kernels, shards(): pl.pallas_call(second_kernel, in_specs=[VMEM] * 6, out_specs=[VMEM] * 2,...  7.97 us
    ppermute x3, waiting for transfers between devices, all_sum(): lax.ppermute(mine, axis, [(i, i ^ step) for i in range(peers)])  5.71 us
    ppermute x3, starting transfers between devices, all_sum(): lax.ppermute(mine, axis, [(i, i ^ step) for i in range(peers)])  5.04 us
    unnamed x12, local copies, waits for them, and re-layouts  4.91 us
    ppermute x2, waiting for transfers between devices, shifted(): return lax.ppermute(x, axis, pairs)  4.6 us
  transfers between devices with their start and end apart: 7, of which 4 were waited for; matrix products, arithmetic and copies ran while one was open for 1% of the time, Pallas kernels for 39%

profile of v1, /device:TPU:1, one launch (start us, length us, event | category | flops | bytes accessed | tf_op | source)
XLA Modules:
  0.0 75.2 jit_solution(12987026334867716807)
XLA Ops:
  0.6 1.4 %slice.6 = bf16[32,1,80,256]{3,2,1,0:T(8,128)(2,1)S(1)} slice(bf16[32,4,80,256]{3,2,1,0:T(8,128)(2,1)} %volume.1), slice={[0:32], [3:4], [0:80], [0:256]} | slice | bytes 2621440 | tf_op jit(solution)/shard_map/slice | solution.py:311
  2.0 4.5 %collective-permute-start = (bf16[32,1,80,256]{3,2,1,0:T(8,128)(2,1)S(1)}, bf16[32,1,80,256]{3,2,1,0:T(8,128)(2,1)S(1)}, u32[]{:S(2)}, u32[]{:S(2)}) collective-permute-start(bf16[32,1,80,256]{3,2,1,0:T(8,128)(2,1)S(1)} %slice.6), channel_id=1, source_target_pairs={{0,1},{1,2},{2,3},{3,4},{4,5},{5,6},{6,7},{7,8},{8,9},{9,10},{10,1... | collective-permute-start | bytes 3932168 | tf_op jit(solution)/shard_map/ppermute | solution.py:303
  6.6 0.7 copy.10.bias
  7.3 0.0 copy-start.2
  7.3 1.3 %copy-done.2 = bf16[64,2,40,128]{3,2,1,0:T(8,128)(2,1)S(1)} copy-done((bf16[64,2,40,128]{3,2,1,0:T(8,128)(2,1)S(1)}, bf16[64,2,40,128]{3,2,1,0:T(8,128)(2,1)}, u32[]{:S(2)}) %copy-start.2) | copy-done | bytes 1310744
  8.7 0.0 copy-start.3
  8.7 0.9 %copy-done.3 = bf16[3,3,3,32,64]{4,3,2,1,0:T(8,128)(2,1)S(1)} copy-done((bf16[3,3,3,32,64]{4,3,2,1,0:T(8,128)(2,1)S(1)}, bf16[3,3,3,32,64]{4,3,2,1,0:T(8,128)(2,1)}, u32[]{:S(2)}) %copy-start.3) | copy-done | bytes 110616
  9.6 18.4 %shard_map.67 = (bf16[2,81,96,128]{3,2,1,0:T(8,128)(2,1)}, f32[40,64,128]{2,1,0:T(8,128)S(1)}, bf16[41,128,128]{2,1,0:T(8,128)(2,1)}, f32[592,128]{1,0:T(8,128)S...) custom-call(bf16[32,4,80,256]{3,2,1,0:T(8,128)(2,1)} %volume.1, ...), custom_call_target="tpu_custom_call" | custom-call | flops 10000000000 | bytes 20971520 | tf_op jit(solution)/shard_map/pallas_call | solution.py:312
  28.0 1.3 %copy-done.4 = bf16[41,128,128]{2,1,0:T(8,128)(2,1)S(1)} copy-done((bf16[41,128,128]{2,1,0:T(8,128)(2,1)S(1)}, bf16[41,128,128]{2,1,0:T(8,128)(2,1)}, u32[]{:S(2)}) %copy-start.4) | copy-done | bytes 1343512
  29.4 3.3 %shard_map.68.refs_0_ = bf16[32,4,80,256]{3,2,1,0:T(8,128)(2,1)} custom-call(bf16[3,128,256]{2,1,0:T(8,128)(2,1)S(1)} %get-tuple-element.15.refs_0_.refs_1_, bf16[41,128,128]{2,1,0:T(8,128)(2,1)S(1)} %copy-done.4), custom_call_target="tpu_custom_call" | custom-call | flops 4000000000 | bytes 4194304 | tf_op jit(solution)/shard_map/pallas_call | solution.py:264
  32.7 0.0 collective-permute-done.halo
  32.7 8.0 %shard_map.69 = (bf16[41,128,128]{2,1,0:T(8,128)(2,1)}, f32[448,128]{1,0:T(8,128)S(1)}) custom-call(bf16[32,1,80,256]{3,2,1,0:T(8,128)(2,1)S(1)} %collective-permute-done.halo, bf16[2,81,96,128]{3,2,1,0:T(8,128)(2,1)} %get-tuple-element.19.lines, f32[40,64,128]{2,1,0:T(8,128)S(1)} %get-tuple-element.20.pre_in, bf16[64,2,40,128]{3,2,1,0:T(8,128)(2,1)} %upstream.3, ...), custom_call_target="tpu_custom_call" | custom-call | flops 5000000000 | bytes 10485760 | tf_op jit(solution)/shard_map/pallas_call | solution.py:335
  40.7 0.1 collective-permute-start.2
  40.8 1.3 %collective-permute-done.2 = f32[224,128]{1,0:T(8,128)S(1)} collective-permute-done((f32[224,128]{1,0:T(8,128)S(1)}, f32[224,128]{1,0:T(8,128)S(1)}, u32[]{:S(2)}, u32[]{:S(2)}) %collective-permute-start.2) | collective-permute-done | bytes 114720 | tf_op jit(solution)/shard_map/ppermute | solution.py:289
  42.1 1.3 %collective-permute-start.3 = (f32[224,128]{1,0:T(8,128)S(1)}, f32[224,128]{1,0:T(8,128)S(1)}, u32[]{:S(2)}, u32[]{:S(2)}) collective-permute-start(f32[224,128]{1,0:T(8,128)S(1)} %bitcast_add_fusion), channel_id=1, source_target_pairs={{0,2},{1,3},{2,0},{3,1},{4,6},{5,7},{6,4},{7,5},{8,10},{9,11},{10,... | collective-permute-start | bytes 344072 | tf_op jit(solution)/shard_map/ppermute | solution.py:292
  43.4 3.4 %collective-permute-done.3 = f32[224,128]{1,0:T(8,128)S(1)} collective-permute-done((f32[224,128]{1,0:T(8,128)S(1)}, f32[224,128]{1,0:T(8,128)S(1)}, u32[]{:S(2)}, u32[]{:S(2)}) %collective-permute-start.3) | collective-permute-done | bytes 114720 | tf_op jit(solution)/shard_map/ppermute | solution.py:292
  46.8 1.4 %collective-permute-start.4 = (f32[224,128]{1,0:T(8,128)S(1)}, f32[224,128]{1,0:T(8,128)S(1)}, u32[]{:S(2)}, u32[]{:S(2)}) collective-permute-start(f32[224,128]{1,0:T(8,128)S(1)} %add.23), channel_id=1, source_target_pairs={{0,4},{1,5},{2,6},{3,7},{4,0},{5,1},{6,2},{7,3},{8,12},{9,13},{10,... | collective-permute-start | bytes 344072 | tf_op jit(solution)/shard_map/ppermute | solution.py:292
  48.1 2.4 %collective-permute-done.4 = f32[224,128]{1,0:T(8,128)S(1)} collective-permute-done((f32[224,128]{1,0:T(8,128)S(1)}, f32[224,128]{1,0:T(8,128)S(1)}, u32[]{:S(2)}, u32[]{:S(2)}) %collective-permute-start.4) | collective-permute-done | bytes 114720 | tf_op jit(solution)/shard_map/ppermute | solution.py:292
  50.5 2.4 %collective-permute-start.5 = (f32[224,128]{1,0:T(8,128)S(1)}, f32[224,128]{1,0:T(8,128)S(1)}, u32[]{:S(2)}, u32[]{:S(2)}) collective-permute-start(f32[224,128]{1,0:T(8,128)S(1)} %add.24), channel_id=1, source_target_pairs={{0,8},{1,9},{2,10},{3,11},{4,12},{5,13},{6,14},{7,15},{8,0},{9,1},... | collective-permute-start | bytes 344072 | tf_op jit(solution)/shard_map/ppermute | solution.py:292
  52.9 1.3 %copy-done = bf16[41,128,128]{2,1,0:T(8,128)(2,1)S(1)} copy-done((bf16[41,128,128]{2,1,0:T(8,128)(2,1)S(1)}, bf16[41,128,128]{2,1,0:T(8,128)(2,1)}, u32[]{:S(2)}) %copy-start) | copy-done | bytes 1343512
  54.2 3.3 %shard_map.70.refs_0_ = bf16[32,4,80,256]{3,2,1,0:T(8,128)(2,1)} custom-call(bf16[32,4,80,256]{3,2,1,0:T(8,128)(2,1)} %shard_map.68.refs_0_, bf16[3,128,256]{2,1,0:T(8,128)(2,1)S(1)} %get-tuple-element.15.refs_0_.refs_1_, bf16[41,128,128]{2,1,0:T(8,128)(2,1)S(1)} %copy-done), custom_call_target="tpu_custom_call", output_to_operand_aliasing={{}: (0, {})} | custom-call | flops 4000000000 | bytes 4194304 | tf_op jit(solution)/shard_map/pallas_call | solution.py:264
  57.6 0.1 slice.7
  57.6 4.3 %collective-permute-start.1 = (bf16[40,64,128]{2,1,0:T(8,128)(2,1)S(1)}, bf16[40,64,128]{2,1,0:T(8,128)(2,1)S(1)}, u32[]{:S(2)}, u32[]{:S(2)}) collective-permute-start(bf16[40,64,128]{2,1,0:T(8,128)(2,1)S(1)} %slice.7), channel_id=1, source_target_pairs={{1,0},{2,1},{3,2},{4,3},{5,4},{6,5},{7,6},{8,7},{9,8},{10,9},{11,1... | collective-permute-start | bytes 1966088 | tf_op jit(solution)/shard_map/ppermute | solution.py:303
  62.0 0.0 collective-permute-done.5
  62.0 0.1 collective-permute-start.6
  62.1 0.0 copy-done.1
  62.1 0.0 copy-done.5
  62.1 3.7 %shard_map.71.refs_0_ = bf16[32,4,80,256]{3,2,1,0:T(8,128)(2,1)} custom-call(bf16[32,4,80,256]{3,2,1,0:T(8,128)(2,1)} %shard_map.70.refs_0_, bf16[3,128,256]{2,1,0:T(8,128)(2,1)S(1)} %get-tuple-element.15.refs_0_.refs_1_, bf16[41,128,128]{2,1,0:T(8,128)(2,1)S(1)} %copy-done.1, bf16[41,128,128]{2,1,0:T(8,128)(2,1)S(1)} %copy-done.5), custom_call_target="tpu_custom_call", output_to_operand_aliasing={{}: (0, {})} | custom-call | flops 4000000000 | bytes 4194304 | tf_op jit(solution)/shard_map/pallas_call | solution.py:264
  65.8 0.0 collective-permute-done.6
  65.8 0.9 %shard_map.73 = (f32[3,3,96,64]{3,2,1,0:T(8,128)}, f32[1,64]{1,0:T(1,128)}) custom-call(f32[448,128]{1,0:T(8,128)S(1)} %pad_maximum_fusion.packed), custom_call_target="tpu_custom_call" | custom-call | tf_op jit(solution)/shard_map/pallas_call | solution.py:355
  66.7 4.6 %collective-permute-done.1.refs_3_ = bf16[40,64,128]{2,1,0:T(8,128)(2,1)S(1)} collective-permute-done((bf16[40,64,128]{2,1,0:T(8,128)(2,1)S(1)}, bf16[40,64,128]{2,1,0:T(8,128)(2,1)S(1)}, u32[]{:S(2)}, u32[]{:S(2)}) %collective-permute-start.1) | collective-permute-done | bytes 655392 | tf_op jit(solution)/shard_map/ppermute | solution.py:303
  71.3 3.9 %shard_map.72 = bf16[32,4,80,256]{3,2,1,0:T(8,128)(2,1)} custom-call(bf16[32,4,80,256]{3,2,1,0:T(8,128)(2,1)} %shard_map.71.refs_0_, bf16[3,128,256]{2,1,0:T(8,128)(2,1)S(1)} %get-tuple-element.15.refs_0_.refs_1_, bf16[41,128,128]{2,1,0:T(8,128)(2,1)S(1)} %copy-done.5, ...), custom_call_target="tpu_custom_call", output_to_operand_aliasing={{}: (0, {})} | custom-call | flops 4000000000 | bytes 4194304 | tf_op jit(solution)/shard_map/pallas_call | solution.py:264
  (11 shorter events, 0.1 us)
Async XLA Ops:
  2.0 30.7 %collective-permute-start = (bf16[32,1,80,256]{3,2,1,0:T(8,128)(2,1)S(1)}, bf16[32,1,80,256]{3,2,1,0:T(8,128)(2,1)S(1)}, u32[]{:S(2)}, u32[]{:S(2)}) collective-permute-start(bf16[32,1,80,256]{3,2,1,0:T(8,128)(2,1)S(1)} %slice.6), channel_id=1, source_target_pairs={{0,1},{1,2},{2,3},{3,4},{4,5},{5,6},{6,7},{7,8},{8,9},{9,10},{10,1... | collective-permute-start | bytes 3932168 | tf_op jit(solution)/shard_map/ppermute | solution.py:303
  7.3 1.3 %copy-start.2 = (bf16[64,2,40,128]{3,2,1,0:T(8,128)(2,1)S(1)}, bf16[64,2,40,128]{3,2,1,0:T(8,128)(2,1)}, u32[]{:S(2)}) copy-start(bf16[64,2,40,128]{3,2,1,0:T(8,128)(2,1)} %upstream.3) | copy-start | bytes 3932164
  8.7 0.9 %copy-start.3 = (bf16[3,3,3,32,64]{4,3,2,1,0:T(8,128)(2,1)S(1)}, bf16[3,3,3,32,64]{4,3,2,1,0:T(8,128)(2,1)}, u32[]{:S(2)}) copy-start(bf16[3,3,3,32,64]{4,3,2,1,0:T(8,128)(2,1)} %weights.1) | copy-start | bytes 331780
  28.0 1.3 %copy-start.4 = (bf16[41,128,128]{2,1,0:T(8,128)(2,1)S(1)}, bf16[41,128,128]{2,1,0:T(8,128)(2,1)}, u32[]{:S(2)}) copy-start(bf16[41,128,128]{2,1,0:T(8,128)(2,1)} %get-tuple-element.16.refs_1_.refs_3_.refs_2_) | copy-start | bytes 4030468
  40.7 1.4 %collective-permute-start.2 = (f32[224,128]{1,0:T(8,128)S(1)}, f32[224,128]{1,0:T(8,128)S(1)}, u32[]{:S(2)}, u32[]{:S(2)}) collective-permute-start(f32[224,128]{1,0:T(8,128)S(1)} %dynamic-slice_bitcast_fusion), channel_id=1, source_target_pairs={{0,1},{1,0},{2,3},{3,2},{4,5},{5,4},{6,7},{7,6},{8,9},{9,8},{10,11... | collective-permute-start | bytes 344072 | tf_op jit(solution)/shard_map/ppermute | solution.py:289
  42.1 4.7 %collective-permute-start.3 = (f32[224,128]{1,0:T(8,128)S(1)}, f32[224,128]{1,0:T(8,128)S(1)}, u32[]{:S(2)}, u32[]{:S(2)}) collective-permute-start(f32[224,128]{1,0:T(8,128)S(1)} %bitcast_add_fusion), channel_id=1, source_target_pairs={{0,2},{1,3},{2,0},{3,1},{4,6},{5,7},{6,4},{7,5},{8,10},{9,11},{10,... | collective-permute-start | bytes 344072 | tf_op jit(solution)/shard_map/ppermute | solution.py:292
  46.8 3.7 %collective-permute-start.4 = (f32[224,128]{1,0:T(8,128)S(1)}, f32[224,128]{1,0:T(8,128)S(1)}, u32[]{:S(2)}, u32[]{:S(2)}) collective-permute-start(f32[224,128]{1,0:T(8,128)S(1)} %add.23), channel_id=1, source_target_pairs={{0,4},{1,5},{2,6},{3,7},{4,0},{5,1},{6,2},{7,3},{8,12},{9,13},{10,... | collective-permute-start | bytes 344072 | tf_op jit(solution)/shard_map/ppermute | solution.py:292
  50.5 11.4 %collective-permute-start.5 = (f32[224,128]{1,0:T(8,128)S(1)}, f32[224,128]{1,0:T(8,128)S(1)}, u32[]{:S(2)}, u32[]{:S(2)}) collective-permute-start(f32[224,128]{1,0:T(8,128)S(1)} %add.24), channel_id=1, source_target_pairs={{0,8},{1,9},{2,10},{3,11},{4,12},{5,13},{6,14},{7,15},{8,0},{9,1},... | collective-permute-start | bytes 344072 | tf_op jit(solution)/shard_map/ppermute | solution.py:292
  52.9 1.3 %copy-start = (bf16[41,128,128]{2,1,0:T(8,128)(2,1)S(1)}, bf16[41,128,128]{2,1,0:T(8,128)(2,1)}, u32[]{:S(2)}) copy-start(bf16[41,128,128]{2,1,0:T(8,128)(2,1)} %get-tuple-element.23.refs_2_) | copy-start | bytes 4030468
  54.2 7.8 %copy-start.1 = (bf16[41,128,128]{2,1,0:T(8,128)(2,1)S(1)}, bf16[41,128,128]{2,1,0:T(8,128)(2,1)}, u32[]{:S(2)}) copy-start(bf16[41,128,128]{2,1,0:T(8,128)(2,1)} %get-tuple-element.23.refs_2_) | copy-start | bytes 4030468
  54.2 7.8 %copy-start.5 = (bf16[41,128,128]{2,1,0:T(8,128)(2,1)S(1)}, bf16[41,128,128]{2,1,0:T(8,128)(2,1)}, u32[]{:S(2)}) copy-start(bf16[41,128,128]{2,1,0:T(8,128)(2,1)} %get-tuple-element.16.refs_1_.refs_3_.refs_2_) | copy-start | bytes 4030468
  57.6 13.7 %collective-permute-start.1 = (bf16[40,64,128]{2,1,0:T(8,128)(2,1)S(1)}, bf16[40,64,128]{2,1,0:T(8,128)(2,1)S(1)}, u32[]{:S(2)}, u32[]{:S(2)}) collective-permute-start(bf16[40,64,128]{2,1,0:T(8,128)(2,1)S(1)} %slice.7), channel_id=1, source_target_pairs={{1,0},{2,1},{3,2},{4,3},{5,4},{6,5},{7,6},{8,7},{9,8},{10,9},{11,1... | collective-permute-start | bytes 1966088 | tf_op jit(solution)/shard_map/ppermute | solution.py:303
  62.0 3.8 %collective-permute-start.6 = (f32[224,128]{1,0:T(8,128)S(1)}, f32[224,128]{1,0:T(8,128)S(1)}, u32[]{:S(2)}, u32[]{:S(2)}) collective-permute-start(f32[224,128]{1,0:T(8,128)S(1)} %add.25), channel_id=1, source_target_pairs={{0,1},{1,0},{2,3},{3,2},{4,5},{5,4},{6,7},{7,6},{8,9},{9,8},{10,11... | collective-permute-start | bytes 344072 | tf_op jit(solution)/shard_map/ppermute | solution.py:294

commit v2 on v1

v2 whole, which is shorter than its diff:
```python
import functools

import jax
import jax.numpy as jnp
from jax import lax
from jax.experimental import pallas as pl
from jax.experimental.pallas import tpu as pltpu
from jax.sharding import PartitionSpec as P

BF = jnp.bfloat16
F32 = jnp.float32
VMEM = pl.BlockSpec(memory_space=pltpu.VMEM)
ANY = pl.BlockSpec(memory_space=pl.ANY)
PARAMS = pltpu.CompilerParams(vmem_limit_bytes=40 * 2**20)


def shape(*dims, dtype=BF):
    return jax.ShapeDtypeStruct(dims, dtype)


def cost(flops, size):
    return pl.CostEstimate(flops=flops, bytes_accessed=size, transcendentals=0)


def picks(half, inverse):
    if inverse:
        row = lax.broadcasted_iota(jnp.int32, (2 * half, 2 * half), 0)
        col = lax.broadcasted_iota(jnp.int32, (2 * half, 2 * half), 1)
        hit = jnp.where(row < half, 2 * row, 2 * (row - half) + 1) == col
    else:
        row = lax.broadcasted_iota(jnp.int32, (2 * half, 3 * half), 0)
        col = lax.broadcasted_iota(jnp.int32, (2 * half, 3 * half), 1)
        early = 2 * col - 1
        even = 2 * (col - half)
        odd = 2 * (col - 2 * half) + 1
        hit = jnp.where(col < half, early, jnp.where(col < 2 * half, even, odd)) == row
    return jnp.where(hit, 1.0, 0.0).astype(BF)


def split_plane(read, lines, table):
    rows, channels, half = lines.shape
    channels //= 3

    def step(t, carry):
        block = jnp.swapaxes(read(pl.multiple_of(t * 16, 16)), 0, 1)
        flat = block.reshape(16 * channels, 2 * half)
        taps = jnp.dot(flat, table, preferred_element_type=F32).astype(BF)
        taps = taps.reshape(16, channels, 3 * half)
        for e in range(3):
            lines[pl.ds(1 + t * 16, 16), e * channels : (e + 1) * channels, :] = taps[
                :, :, e * half : (e + 1) * half
            ]
        return carry

    lax.fori_loop(0, (rows - 1) // 16, step, 0, unroll=True)


def turn_upstream(upstream, turned):
    for o in range(0, upstream.shape[0], 8):
        block = upstream[o : o + 8].astype(F32)
        turned[:, o : o + 8, :] = jnp.swapaxes(block, 0, 1).astype(turned.dtype)


def earlier(values):
    cells = values.shape[-1]
    lane = lax.broadcasted_iota(jnp.int32, values.shape, values.ndim - 1)
    return jnp.where(lane == cells - 1, 0.0, pltpu.roll(values, cells - 1, values.ndim - 1))


def store_grads(pre, upstream, grads, j):
    slope = 0.6 + 0.4 * jnp.tanh(0.5 * pre)
    value = (upstream * slope).astype(BF)
    cout = value.shape[0]
    grads[j, :cout, :] = value
    grads[j, cout:, :] = earlier(value.astype(F32)).astype(BF)


def window(planes, j, count):
    parts = [plane[2 * j : 2 * j + count].reshape(-1, plane.shape[-1]) for plane in planes]
    return parts[0] if len(parts) == 1 else jnp.concatenate(parts, 0)


def weight_terms(cells):
    left, right = [], []
    for lines, grads in cells:
        flat = [line.reshape(-1, line.shape[-1]) for line in lines]
        ones = jnp.ones((16, flat[0].shape[-1]), BF)
        left.append(jnp.concatenate(flat + [ones], 0))
        right.append(jnp.concatenate(grads, 0))
    return lax.dot_general(
        jnp.concatenate(left, 1),
        jnp.concatenate(right, 1),
        (((1,), (1,)), ((), ())),
        preferred_element_type=F32,
    )


class Copies:
    def __init__(self, semaphores):
        self.semaphores, self.used, self.pending = semaphores, 0, []

    def start(self, source, target):
        copy = pltpu.make_async_copy(source, target, self.semaphores.at[self.used])
        self.used += 1
        copy.start()
        self.pending.append(copy)
        return copy

    def wait(self, *copies):
        for copy in copies or list(self.pending):
            copy.wait()
            self.pending.remove(copy)


def spans(total, size):
    return [(at, min(at + size, total)) for at in range(0, total, size)]


def first_kernel(
    volume, weights, bias, upstream,
    lines_out, pre_out, turned_out, grads_out, terms, back, front,
    field, lines, inputs, turned, turned_late, pre, grads, turned_weights, semaphores,
):
    cin = volume.shape[0]
    cout = bias.shape[0]
    half = volume.shape[3] // 2
    ny = upstream.shape[2]
    copies = Copies(semaphores)
    ins = [copies.start(volume.at[:, z], field.at[z]) for z in range(2)]
    ups = [copies.start(upstream.at[:, k], inputs.at[k]) for k in range(2)]
    ins += [copies.start(volume.at[:, z], field.at[z]) for z in range(2, 4)]
    table = picks(half, False)
    planes = [lines.at[z] for z in range(4)]
    for a in range(3):
        for b in range(3):
            block = jnp.concatenate([weights[a, b, e] for e in range(3)], 0)
            turned_weights[:, a, b * 3 * cin : (b + 1) * 3 * cin] = block.T
    front[...] = turned_weights[:, 0, :]
    blank = jnp.zeros((cin, cout), BF)
    for a in range(3):
        for px in range(2):
            for py in range(2):
                row = []
                for dy in range(2):
                    for dx in range(2):
                        b, e = py + 1 - 2 * dy, px + 1 - 2 * dx
                        row.append(weights[a, b, e] if b >= 0 and e >= 0 else blank)
                at = (px * 2 + py) * cin
                back[a, at : at + cin, :] = jnp.concatenate(row, 1)
    full = jnp.concatenate([turned_weights[:, a, :] for a in range(3)], 1)
    late = jnp.concatenate([turned_weights[:, a, :] for a in (1, 2)], 1)
    offset = bias[...]

    def split(z):
        planes[z][0] = jnp.zeros(planes[z].shape[1:], BF)
        copies.wait(ins[z])
        split_plane(lambda y: field[z, :, pl.ds(y, 16), :], planes[z], table)

    for z in range(2):
        split(z)
        copies.start(lines.at[z], lines_out.at[z])
    for lo, hi in spans(ny, 8):
        block = jnp.concatenate([window(planes[:2], j, 3) for j in range(lo, hi)], 1)
        sums = jnp.dot(late, block, preferred_element_type=F32)
        for j in range(lo, hi):
            pre[j] = sums[:, (j - lo) * half : (j - lo + 1) * half] + offset
    copies.start(pre, pre_out)
    copies.wait(*ups)
    turn_upstream(inputs.at[0], turned_late)
    copies.start(turned_late, turned_out)
    turn_upstream(inputs.at[1], turned)
    for z in range(2, 4):
        split(z)
    for lo, hi in spans(ny, 8):
        block = jnp.concatenate([window(planes[1:], j, 3) for j in range(lo, hi)], 1)
        sums = jnp.dot(full, block, preferred_element_type=F32)
        for j in range(lo, hi):
            at = (j - lo) * half
            store_grads(sums[:, at : at + half] + offset, turned[j], grads, j)
    grads[ny] = jnp.zeros(grads.shape[1:], BF)
    copies.start(grads, grads_out)
    terms[...] = weight_terms(
        [
            (
                [plane[1 + 2 * j : 3 + 2 * j] for plane in planes[1:]],
                [grads[j, :cout], grads[j + 1, :cout]],
            )
            for j in range(ny)
        ]
    )
    copies.wait()


def halo_kernel(first, last, *refs):
    halo, lines, pre_in, turned_in, front, terms_in = refs[:6]
    refs = refs[6:]
    if not first:
        before, grads_in = refs[:2]
        refs = refs[2:]
    grads_out, raw_out = refs[:2]
    refs = refs[2:]
    if last:
        packed = refs[0]
        refs = refs[1:]
    else:
        terms_out, carry_out = refs[:2]
        refs = refs[2:]
    below, own, pre, turned, grads, raw, held, semaphores = refs
    half = below.shape[-1]
    cout = front.shape[0]
    count = raw.shape[0]
    ny = pre_in.shape[0]
    start = 0 if first else ny - count
    rows = 2 * count
    lead = 0 if first else 2
    copies = Copies(semaphores)
    early = [
        copies.start(pre_in.at[start : start + count], pre),
        copies.start(turned_in.at[start : start + count], turned),
    ]
    begin = 2 * start + 1 - lead
    late = [
        copies.start(lines.at[:, begin : 2 * start + 1 + rows], own.at[:, 0 : rows + lead])
    ]
    if first:
        below[0] = jnp.zeros(below.shape[1:], BF)
    else:
        late.append(copies.start(grads_in.at[start - 1], held.at[0]))
        below[0] = before[1]
    table = picks(half, False)
    split_plane(lambda y: halo[:, 0, pl.ds(y, 16), :], below, table)
    copies.wait(*early)
    for lo, hi in spans(count, 8):
        block = jnp.concatenate([window([below], j, 3) for j in range(lo, hi)], 1)
        sums = jnp.dot(front[...], block, preferred_element_type=F32)
        for j in range(lo, hi):
            at = (j - lo) * half
            store_grads(sums[:, at : at + half] + pre[j], turned[j].astype(F32), grads, j)
            raw[j] = grads[j, :cout, :]
    size = count
    if last:
        grads[count] = jnp.zeros(grads.shape[1:], BF)
        size += 1
    copies.start(raw, raw_out)
    copies.start(grads.at[0:size], grads_out.at[start : start + size])
    copies.wait(*late)
    cells = []
    if not first:
        cells.append(
            (
                [before[...], own[0, 0:2], own[1, 0:2]],
                [held[0, :cout], grads[0, :cout]],
            )
        )
    for j in range(count if last else count - 1):
        at = 2 * j + lead
        cells.append(
            (
                [below[2 * j + 1 : 2 * j + 3], own[0, at : at + 2], own[1, at : at + 2]],
                [grads[j, :cout], grads[j + 1, :cout]],
            )
        )
    terms = terms_in[...] + weight_terms(cells)
    if last:
        pack(terms, packed, below.shape[1], cout)
    else:
        terms_out[...] = terms
        carry_out[...] = below[rows - 1 : rows + 1]
    copies.wait()


def pack(terms, packed, count, cout):
    for a in range(3):
        packed[a * count : (a + 1) * count] = terms[(2 * a + 1) * count : (2 * a + 2) * count]
    middle = jnp.concatenate([terms[2 * a * count : (2 * a + 1) * count, :cout] for a in range(3)], 0)
    rows = middle.shape[0] // 2
    packed[3 * count : 3 * count + rows] = jnp.concatenate([middle[:rows], middle[rows:]], 1)
    packed[3 * count + rows :] = jnp.concatenate(
        [terms[6 * count :][:, :cout], jnp.zeros((16, cout), F32)], 1
    )


def finish_kernel(packed, weight_grad, bias_grad):
    count = weight_grad.shape[2]
    cout = weight_grad.shape[3]
    for a in range(3):
        block = packed[a * count : (a + 1) * count]
        weight_grad[a, 2] = block[:, :cout]
        weight_grad[a, 0] = block[:, cout:]
    rows = 3 * count // 2
    middle = packed[3 * count : 3 * count + rows]
    middle = jnp.concatenate([middle[:, :cout], middle[:, cout:]], 0)
    for a in range(3):
        weight_grad[a, 1] = middle[a * count : (a + 1) * count]
    bias_grad[...] = packed[3 * count + rows :][:1, :cout]


def back_kernel(z, odd, fresh, aliased, *refs):
    refs = refs[1:] if aliased else refs
    back, grads_in = refs[:2]
    above_in = refs[2 : 2 + (2 if fresh else odd)]
    refs = refs[2 + len(above_in) :]
    total, grads, above, plane, semaphores = refs[:5]
    ny = grads.shape[0] - 1
    cout = grads.shape[1] // 2
    copies = Copies(semaphores)
    loads = []
    for lo, hi in spans(ny, 8):
        top = ny + 1 if hi == ny else hi
        part = [copies.start(grads_in.at[lo:top], grads.at[lo:top])]
        if odd and not fresh:
            part.append(copies.start(above_in[0].at[lo:top], above.at[lo:top]))
        loads.append(part)
    if fresh:
        at = 0
        for ref in above_in:
            for j in range(ref.shape[0]):
                above[at + j, :cout, :] = ref[j]
                above[at + j, cout:, :] = earlier(ref[j].astype(F32)).astype(BF)
            at += ref.shape[0]
        above[ny] = jnp.zeros(above.shape[1:], BF)
    left = jnp.concatenate([back[2], back[0]], 1) if odd else back[1]
    cin = plane.shape[0]
    half = plane.shape[2] // 2
    table = picks(half, True)
    copies.wait(*loads[0])
    for n, (lo, hi) in enumerate(spans(ny, 8)):
        if n + 1 < len(loads):
            copies.wait(*loads[n + 1])
        columns = []
        for j in range(lo, hi):
            parts = [grads[j : j + 2].reshape(-1, half)]
            if odd:
                parts.append(above[j : j + 2].reshape(-1, half))
            columns.append(jnp.concatenate(parts, 0))
        sums = jnp.dot(left, jnp.concatenate(columns, 1), preferred_element_type=F32)
        sums = sums.astype(BF)
        rows = []
        for j in range(hi - lo):
            for py in range(2):
                lanes = slice(j * half, (j + 1) * half)
                even = sums[py * cin : (py + 1) * cin, lanes]
                odds = sums[(2 + py) * cin : (3 + py) * cin, lanes]
                rows.append(jnp.concatenate([even, odds], 1))
        merged = jnp.dot(jnp.concatenate(rows, 0), table, preferred_element_type=F32)
        merged = merged.astype(BF).reshape(2 * (hi - lo), cin, 2 * half)
        plane[:, 2 * lo : 2 * hi, :] = jnp.swapaxes(merged, 0, 1)
        copies.start(plane.at[:, 2 * lo : 2 * hi], total.at[:, z, 2 * lo : 2 * hi])
    copies.wait()


def back_plane(z, total, full, back, grads, above=()):
    cin, depth, height, width = full
    fresh = len(above) == 2
    args = [back, grads, *above]
    specs = [VMEM, ANY] + [VMEM if fresh else ANY] * len(above)
    aliased = total is not None
    if aliased:
        args = [total] + args
        specs = [ANY] + specs
    return pl.pallas_call(
        functools.partial(back_kernel, z, len(above) > 0, fresh, aliased),
        in_specs=specs,
        out_specs=ANY,
        out_shape=shape(*full),
        scratch_shapes=[
            pltpu.VMEM(grads.shape, BF),
            pltpu.VMEM(grads.shape if above else (16, 128), BF),
            pltpu.VMEM((cin, height, width), BF),
            pltpu.SemaphoreType.DMA((3 * (height // 16),)),
        ],
        input_output_aliases={0: 0} if aliased else {},
        compiler_params=PARAMS,
        cost_estimate=cost(3 * 10**9, 4 * 2**20),
    )(*args)


def all_sum(value, axis):
    peers = lax.axis_size(axis)
    if peers & (peers - 1):
        return lax.psum(value, axis)
    if peers == 1:
        return value
    swap = [(i, i ^ 1) for i in range(peers)]
    odd = lax.axis_index(axis) & 1
    rows = value.shape[0] // 2
    halves = value.reshape(2, rows, value.shape[1])
    mine = lax.dynamic_index_in_dim(halves, odd, 0, False)
    other = lax.dynamic_index_in_dim(halves, 1 - odd, 0, False)
    mine = mine + lax.ppermute(other, axis, swap)
    step = 2
    while step < peers:
        mine = mine + lax.ppermute(mine, axis, [(i, i ^ step) for i in range(peers)])
        step *= 2
    other = lax.ppermute(mine, axis, swap)
    low = jnp.where(odd == 0, mine, other)
    high = jnp.where(odd == 0, other, mine)
    return jnp.concatenate([low, high], 0)


def shifted(x, axis, by):
    peers = lax.axis_size(axis)
    pairs = [(i, i + by) for i in range(peers) if 0 <= i + by < peers]
    return lax.ppermute(x, axis, pairs)


def shards(volume, weights, bias, upstream):
    cin, depth, height, width = volume.shape
    cout = bias.shape[0]
    ny, half = height // 2, width // 2
    rows, count = height + 1, 3 * cin
    cut = (height // 16 + 1) // 2 * 16
    halos = [
        shifted(volume[:, depth - 1 :, :cut], "slab", 1),
        shifted(volume[:, depth - 1 :, cut:], "slab", 1),
    ]
    grads_shape = (ny + 1, 2 * cout, half)
    terms_shape = (6 * count + 16, 2 * cout)
    lines, pre, turned, upper, terms, back, front = pl.pallas_call(
        first_kernel,
        in_specs=[ANY, VMEM, VMEM, ANY],
        out_specs=[ANY] * 4 + [VMEM] * 3,
        out_shape=[
            shape(2, rows, count, half),
            shape(ny, cout, half, dtype=F32),
            shape(ny, cout, half),
            shape(*grads_shape),
            shape(*terms_shape, dtype=F32),
            shape(3, 4 * cin, 4 * cout),
            shape(cout, 3 * count),
        ],
        scratch_shapes=[
            pltpu.VMEM((4, cin, height, width), BF),
            pltpu.VMEM((4, rows, count, half), BF),
            pltpu.VMEM((2, cout, ny, half), BF),
            pltpu.VMEM((ny, cout, half), F32),
            pltpu.VMEM((ny, cout, half), BF),
            pltpu.VMEM((ny, cout, half), F32),
            pltpu.VMEM(grads_shape, BF),
            pltpu.VMEM((cout, 3, 3 * count), BF),
            pltpu.SemaphoreType.DMA((16,)),
        ],
        compiler_params=PARAMS,
        cost_estimate=cost(10 * 10**9, 20 * 2**20),
    )(volume, weights, bias.reshape(cout, 1), upstream)
    full = volume.shape

    def scratch(cells):
        return [
            pltpu.VMEM((2 * cells + 1, count, half), BF),
            pltpu.VMEM((2, 2 * cells + 2, count, half), BF),
            pltpu.VMEM((cells, cout, half), F32),
            pltpu.VMEM((cells, cout, half), BF),
            pltpu.VMEM((cells + 1, 2 * cout, half), BF),
            pltpu.VMEM((cells, cout, half), BF),
            pltpu.VMEM((1, 2 * cout, half), BF),
            pltpu.SemaphoreType.DMA((8,)),
        ]

    cells = cut // 2
    lower, raw, terms, carry = pl.pallas_call(
        functools.partial(halo_kernel, True, False),
        in_specs=[VMEM, ANY, ANY, ANY, VMEM, VMEM],
        out_specs=[ANY, ANY, VMEM, VMEM],
        out_shape=[
            shape(*grads_shape),
            shape(cells, cout, half),
            shape(*terms_shape, dtype=F32),
            shape(2, count, half),
        ],
        scratch_shapes=scratch(cells),
        compiler_params=PARAMS,
        cost_estimate=cost(3 * 10**9, 6 * 2**20),
    )(halos[0], lines, pre, turned, front, terms)
    above = [shifted(raw, "slab", -1)]
    total = back_plane(2, None, full, back, upper)
    total, late, lower = lax.optimization_barrier((total, halos[1], lower))
    cells = ny - cells
    lower, raw, packed = pl.pallas_call(
        functools.partial(halo_kernel, False, True),
        in_specs=[VMEM, ANY, ANY, ANY, VMEM, VMEM, VMEM, ANY],
        out_specs=[ANY, ANY, VMEM],
        out_shape=[
            shape(*grads_shape),
            shape(cells, cout, half),
            shape(9 * count // 2 + 16, 2 * cout, dtype=F32),
        ],
        scratch_shapes=scratch(cells),
        input_output_aliases={7: 0},
        compiler_params=PARAMS,
        cost_estimate=cost(2 * 10**9, 4 * 2**20),
    )(late, lines, pre, turned, front, terms, carry, lower)
    above.append(shifted(raw, "slab", -1))
    packed = all_sum(packed, "slab")
    total = back_plane(0, total, full, back, lower)
    total = back_plane(1, total, full, back, lower, (upper,))
    total = back_plane(3, total, full, back, upper, tuple(above))
    weight_grad, bias_grad = pl.pallas_call(
        finish_kernel,
        in_specs=[VMEM],
        out_specs=[VMEM] * 2,
        out_shape=[shape(3, 3, count, cout, dtype=F32), shape(1, cout, dtype=F32)],
        compiler_params=PARAMS,
    )(packed)
    return (
        total,
        weight_grad.reshape(3, 3, 3, cin, cout),
        bias_grad.reshape(cout),
    )


def solution(mesh):
    placed = (
        P(None, ("groups", "slab"), None, None),
        P(),
        P(),
        P(None, ("groups", "slab"), None, None),
    )
    return jax.shard_map(
        shards,
        mesh=mesh,
        in_specs=placed,
        out_specs=(
            P(None, ("groups", "slab"), None, None),
            P("groups", None, None, None, None),
            P("groups"),
        ),
        check_vma=False,
    )
```

time: 75.6 us -> 68.9 us (0.911)
  the two profiles are of different devices: /device:TPU:1 before, /device:TPU:0 now
where the time goes in v2:
time: 68.9 us; the launch traced here: 68.4 us
  Pallas kernels  32.2 us (47%)
  starting transfers between devices  15.2 us (22%)
  waiting for transfers between devices  10.7 us (16%)
  local copies, waits for them, and re-layouts  8.38 us (12%)
  other arithmetic  0.99 us (1%)
  between operations  0.83 us (1%)
    pallas_call x4, Pallas kernels, back_plane(): pl.pallas_call(functools.partial(back_kernel, z, len(above) > 0, fresh, a...  13.2 us
    pallas_call x1, Pallas kernels, shards(): pl.pallas_call(first_kernel, in_specs=[ANY, VMEM, VMEM, ANY], out_specs=[...  11.2 us
    ppermute x4, starting transfers between devices, shifted(): return lax.ppermute(x, axis, pairs)  10.4 us
    ppermute x3, waiting for transfers between devices, all_sum(): lax.ppermute(mine, axis, [(i, i ^ step) for i in range(peers)])  9.42 us
    ppermute x3, starting transfers between devices, all_sum(): lax.ppermute(mine, axis, [(i, i ^ step) for i in range(peers)])  4.74 us
    pallas_call x1, Pallas kernels, shards(): pl.pallas_call(functools.partial(halo_kernel, True, False), in_specs=[VME...  4.42 us
    unnamed x10, local copies, waits for them, and re-layouts  3.64 us
    pallas_call x1, Pallas kernels, shards(): pl.pallas_call(functools.partial(halo_kernel, False, True), in_specs=[VME...  2.48 us
  transfers between devices with their start and end apart: 9, of which 4 were waited for; matrix products, arithmetic and copies ran while one was open for 4% of the time, Pallas kernels for 42%

profile of v2, /device:TPU:0, one launch (start us, length us, event | category | flops | bytes accessed | tf_op | source)
XLA Modules:
  0.0 68.4 jit_solution(15926940903757544061)
XLA Ops:
  0.6 1.9 %slice.6 = bf16[32,1,32,256]{3,2,1,0:T(8,128)(2,1)} slice(bf16[32,4,80,256]{3,2,1,0:T(8,128)(2,1)} %volume.1), slice={[0:32], [3:4], [48:80], [0:256]} | slice | bytes 1048576 | tf_op jit(solution)/shard_map/slice | solution.py:415
  2.5 2.4 %collective-permute-start = (bf16[32,1,32,256]{3,2,1,0:T(8,128)(2,1)}, bf16[32,1,32,256]{3,2,1,0:T(8,128)(2,1)S(1)}, u32[]{:S(2)}, u32[]{:S(2)}) collective-permute-start(bf16[32,1,32,256]{3,2,1,0:T(8,128)(2,1)} %slice.6), channel_id=1, source_target_pairs={{0,1},{1,2},{2,3},{3,4},{4,5},{5,6},{6,7},{7,8},{8,9},{9,10},{10,1... | collective-permute-start | bytes 1572872 | tf_op jit(solution)/shard_map/ppermute | solution.py:404
  4.9 2.1 %slice.7 = bf16[32,1,48,256]{3,2,1,0:T(8,128)(2,1)} slice(bf16[32,4,80,256]{3,2,1,0:T(8,128)(2,1)} %volume.1), slice={[0:32], [3:4], [0:48], [0:256]} | slice | bytes 1572864 | tf_op jit(solution)/shard_map/slice | solution.py:414
  7.0 5.4 %collective-permute-start.1 = (bf16[32,1,48,256]{3,2,1,0:T(8,128)(2,1)}, bf16[32,1,48,256]{3,2,1,0:T(8,128)(2,1)}, u32[]{:S(2)}, u32[]{:S(2)}) collective-permute-start(bf16[32,1,48,256]{3,2,1,0:T(8,128)(2,1)} %slice.7), channel_id=1, source_target_pairs={{0,1},{1,2},{2,3},{3,4},{4,5},{5,6},{6,7},{7,8},{8,9},{9,10},{10,1... | collective-permute-start | bytes 2359304 | tf_op jit(solution)/shard_map/ppermute | solution.py:404
  12.4 0.7 %copy.11.bias = f32[64,1]{1,0:T(8,128)S(1)} copy(f32[64,1]{0,1:T(1,128)} %bitcast.10) | data formatting | bytes 512 | tf_op jit(solution)/shard_map/reshape | solution.py:445
  13.2 1.3 %copy-done.1 = bf16[64,2,40,128]{3,2,1,0:T(8,128)(2,1)S(1)} copy-done((bf16[64,2,40,128]{3,2,1,0:T(8,128)(2,1)S(1)}, bf16[64,2,40,128]{3,2,1,0:T(8,128)(2,1)}, u32[]{:S(2)}) %copy-start.1) | copy-done | bytes 1310744
  14.5 0.9 %copy-done.4 = bf16[3,3,3,32,64]{4,3,2,1,0:T(8,128)(2,1)S(1)} copy-done((bf16[3,3,3,32,64]{4,3,2,1,0:T(8,128)(2,1)S(1)}, bf16[3,3,3,32,64]{4,3,2,1,0:T(8,128)(2,1)}, u32[]{:S(2)}) %copy-start.4) | copy-done | bytes 110616
  15.4 11.2 %shard_map.67 = (bf16[2,81,96,128]{3,2,1,0:T(8,128)(2,1)S(1)}, f32[40,64,128]{2,1,0:T(8,128)S(1)}, bf16[40,64,128]{2,1,0:T(8,128)(2,1)S(1)}, bf16[41,128,128]{2,...) custom-call(bf16[32,4,80,256]{3,2,1,0:T(8,128)(2,1)} %volume.1, ...), custom_call_target="tpu_custom_call" | custom-call | flops 10000000000 | bytes 20971520 | tf_op jit(solution)/shard_map/pallas_call | solution.py:419
  26.6 3.0 %shard_map.68.refs_0_ = bf16[32,4,80,256]{3,2,1,0:T(8,128)(2,1)} custom-call(bf16[3,128,256]{2,1,0:T(8,128)(2,1)S(1)} %get-tuple-element.22.refs_0_.refs_1_, bf16[41,128,128]{2,1,0:T(8,128)(2,1)S(1)} %get-tuple-element.23.refs_1_.refs_3_.refs_2_), custom_call_target="tpu_custom_call" | custom-call | flops 3000000000 | bytes 4194304 | tf_op jit(solution)/shard_map/pallas_call | solution.py:361
  29.7 0.0 collective-permute-done.1.refs_0_
  29.7 4.4 %shard_map.69 = (bf16[41,128,128]{2,1,0:T(8,128)(2,1)S(1)}, bf16[24,64,128]{2,1,0:T(8,128)(2,1)S(1)}, f32[592,128]{1,0:T(8,128)S(1)}, bf16[2,96,128]{2,1,0:T(8,128)(2,1)S(1)}) custom-call(bf16[32,1,48,256]{3,2,1,0:T(8,128)(2,1)} %collective-permute-done.1.refs_0_, bf16[2,81,96,128]{3,2,1,0:T(8,128)(2,1)S(1)} %get-tuple-element.24.refs_1_, ...), custom_call_target="tpu_custom_call" | custom-call | flops 3000000000 | bytes 6291456 | tf_op jit(solution)/shard_map/pallas_call | solution.py:461
  34.1 0.0 copy-start.2
  34.1 2.5 %shard_map.70 = (bf16[41,128,128]{2,1,0:T(8,128)(2,1)S(1)}, bf16[16,64,128]{2,1,0:T(8,128)(2,1)S(1)}, f32[448,128]{1,0:T(8,128)S(1)}) custom-call(bf16[32,1,32,256]{3,2,1,0:T(8,128)(2,1)S(1)} %collective-permute-done.refs_0_, bf16[2,81,96,128]{3,2,1,0:T(8,128)(2,1)S(1)} %get-tuple-element.24.refs_1_, ...), custom_call_target="tpu_custom_call", output_to_operand_aliasing={{0}: (7, {})} | custom-call | flops 2000000000 | bytes 4194304 | tf_op jit(solution)/shard_map/pallas_call | solution.py:479
  36.6 0.7 %copy-done.3 = bf16[16,64,128]{2,1,0:T(8,128)(2,1)} copy-done((bf16[16,64,128]{2,1,0:T(8,128)(2,1)}, bf16[16,64,128]{2,1,0:T(8,128)(2,1)S(1)}, u32[]{:S(2)}) %copy-start.3) | copy-done | bytes 262168
  37.3 0.7 copy-done
  38.0 0.1 collective-permute-start.4
  38.1 1.3 %collective-permute-done.4 = f32[224,128]{1,0:T(8,128)S(1)} collective-permute-done((f32[224,128]{1,0:T(8,128)S(1)}, f32[224,128]{1,0:T(8,128)S(1)}, u32[]{:S(2)}, u32[]{:S(2)}) %collective-permute-start.4) | collective-permute-done | bytes 114720 | tf_op jit(solution)/shard_map/ppermute | solution.py:390
  39.4 0.9 %bitcast_add_fusion = f32[224,128]{1,0:T(8,128)S(1)} fusion(f32[224,128]{1,0:T(8,128)S(1)} %collective-permute-done.4, f32[2,224,128]{2,1,0:T(8,128)} %bitcast.9, s32[]{:T(128)S(6)} %select_n.20), kind=kLoop, calls=%fused_computation.1 | loop fusion | flops 28672 | bytes 344068 | tf_op jit(solution)/shard_map/add | solution.py:390
  40.3 0.7 collective-permute-start.5
  41.0 1.3 %collective-permute-start.2 = (bf16[24,64,128]{2,1,0:T(8,128)(2,1)}, bf16[24,64,128]{2,1,0:T(8,128)(2,1)S(1)}, u32[]{:S(2)}, u32[]{:S(2)}) collective-permute-start(bf16[24,64,128]{2,1,0:T(8,128)(2,1)} %copy-done.2), channel_id=1, source_target_pairs={{1,0},{2,1},{3,2},{4,3},{5,4},{6,5},{7,6},{8,7},{9,8},{10,9},{11,1... | collective-permute-start | bytes 1179656 | tf_op jit(solution)/shard_map/ppermute | solution.py:404
  42.3 1.3 %collective-permute-start.3 = (bf16[16,64,128]{2,1,0:T(8,128)(2,1)}, bf16[16,64,128]{2,1,0:T(8,128)(2,1)S(1)}, u32[]{:S(2)}, u32[]{:S(2)}) collective-permute-start(bf16[16,64,128]{2,1,0:T(8,128)(2,1)} %copy-done.3), channel_id=1, source_target_pairs={{1,0},{2,1},{3,2},{4,3},{5,4},{6,5},{7,6},{8,7},{9,8},{10,9},{11,1... | collective-permute-start | bytes 786440 | tf_op jit(solution)/shard_map/ppermute | solution.py:404
  43.6 2.0 %collective-permute-done.5 = f32[224,128]{1,0:T(8,128)S(1)} collective-permute-done((f32[224,128]{1,0:T(8,128)S(1)}, f32[224,128]{1,0:T(8,128)S(1)}, u32[]{:S(2)}, u32[]{:S(2)}) %collective-permute-start.5) | collective-permute-done | bytes 114720 | tf_op jit(solution)/shard_map/ppermute | solution.py:393
  45.6 2.3 %collective-permute-start.6 = (f32[224,128]{1,0:T(8,128)S(1)}, f32[224,128]{1,0:T(8,128)S(1)}, u32[]{:S(2)}, u32[]{:S(2)}) collective-permute-start(f32[224,128]{1,0:T(8,128)S(1)} %add.23), channel_id=1, source_target_pairs={{0,4},{1,5},{2,6},{3,7},{4,0},{5,1},{6,2},{7,3},{8,12},{9,13},{10,... | collective-permute-start | bytes 344072 | tf_op jit(solution)/shard_map/ppermute | solution.py:393
  47.9 3.0 %shard_map.71.refs_0_ = bf16[32,4,80,256]{3,2,1,0:T(8,128)(2,1)} custom-call(bf16[32,4,80,256]{3,2,1,0:T(8,128)(2,1)} %shard_map.68.refs_0_, bf16[3,128,256]{2,1,0:T(8,128)(2,1)S(1)} %get-tuple-element.22.refs_0_.refs_1_, bf16[41,128,128]{2,1,0:T(8,128)(2,1)S(1)} %get-tuple-element.35.refs_2_), custom_call_target="tpu_custom_call", output_to_operand_aliasing={{}: (0, {})} | custom-call | flops 3000000000 | bytes 4194304 | tf_op jit(solution)/shard_map/pallas_call | solution.py:361
  50.9 6.8 %collective-permute-done.6 = f32[224,128]{1,0:T(8,128)S(1)} collective-permute-done((f32[224,128]{1,0:T(8,128)S(1)}, f32[224,128]{1,0:T(8,128)S(1)}, u32[]{:S(2)}, u32[]{:S(2)}) %collective-permute-start.6) | collective-permute-done | bytes 114720 | tf_op jit(solution)/shard_map/ppermute | solution.py:393
  57.7 1.8 %collective-permute-start.7 = (f32[224,128]{1,0:T(8,128)S(1)}, f32[224,128]{1,0:T(8,128)S(1)}, u32[]{:S(2)}, u32[]{:S(2)}) collective-permute-start(f32[224,128]{1,0:T(8,128)S(1)} %add.24), channel_id=1, source_target_pairs={{0,8},{1,9},{2,10},{3,11},{4,12},{5,13},{6,14},{7,15},{8,0},{9,1},... | collective-permute-start | bytes 344072 | tf_op jit(solution)/shard_map/ppermute | solution.py:393
  59.5 3.6 %shard_map.72.refs_0_ = bf16[32,4,80,256]{3,2,1,0:T(8,128)(2,1)} custom-call(bf16[32,4,80,256]{3,2,1,0:T(8,128)(2,1)} %shard_map.71.refs_0_, bf16[3,128,256]{2,1,0:T(8,128)(2,1)S(1)} %get-tuple-element.22.refs_0_.refs_1_, bf16[41,128,128]{2,1,0:T(8,128)(2,1)S(1)} %get-tuple-element.35.refs_2_, ...), custom_call_target="tpu_custom_call", output_to_operand_aliasing={{}: (0, {})} | custom-call | flops 3000000000 | bytes 4194304 | tf_op jit(solution)/shard_map/pallas_call | solution.py:361
  63.0 0.6 collective-permute-done.7
  63.7 0.1 collective-permute-start.8
  63.8 0.0 collective-permute-done.3.refs_4_
  63.8 3.7 %shard_map.73 = bf16[32,4,80,256]{3,2,1,0:T(8,128)(2,1)} custom-call(bf16[32,4,80,256]{3,2,1,0:T(8,128)(2,1)} %shard_map.72.refs_0_, bf16[3,128,256]{2,1,0:T(8,128)(2,1)S(1)} %get-tuple-element.22.refs_0_.refs_1_, bf16[41,128,128]{2,1,0:T(8,128)(2,1)S(1)} %get-tuple-element.23.refs_1_.refs_3_.refs_2_, ...), custom_call_target="tpu_custom_call", output_to_operand_aliasing={{}: (0, {})} | custom-call | flops 3000000000 | bytes 4194304 | tf_op jit(solution)/shard_map/pallas_call | solution.py:361
  67.5 0.9 %shard_map.74 = (f32[3,3,96,64]{3,2,1,0:T(8,128)}, f32[1,64]{1,0:T(1,128)}) custom-call(f32[448,128]{1,0:T(8,128)S(1)} %pad_maximum_fusion.packed), custom_call_target="tpu_custom_call" | custom-call | tf_op jit(solution)/shard_map/pallas_call | solution.py:498
  (14 shorter events, 0.1 us)
Async XLA Ops:
  2.5 31.6 %collective-permute-start = (bf16[32,1,32,256]{3,2,1,0:T(8,128)(2,1)}, bf16[32,1,32,256]{3,2,1,0:T(8,128)(2,1)S(1)}, u32[]{:S(2)}, u32[]{:S(2)}) collective-permute-start(bf16[32,1,32,256]{3,2,1,0:T(8,128)(2,1)} %slice.6), channel_id=1, source_target_pairs={{0,1},{1,2},{2,3},{3,4},{4,5},{5,6},{6,7},{7,8},{8,9},{9,10},{10,1... | collective-permute-start | bytes 1572872 | tf_op jit(solution)/shard_map/ppermute | solution.py:404
  7.0 22.7 %collective-permute-start.1 = (bf16[32,1,48,256]{3,2,1,0:T(8,128)(2,1)}, bf16[32,1,48,256]{3,2,1,0:T(8,128)(2,1)}, u32[]{:S(2)}, u32[]{:S(2)}) collective-permute-start(bf16[32,1,48,256]{3,2,1,0:T(8,128)(2,1)} %slice.7), channel_id=1, source_target_pairs={{0,1},{1,2},{2,3},{3,4},{4,5},{5,6},{6,7},{7,8},{8,9},{9,10},{10,1... | collective-permute-start | bytes 2359304 | tf_op jit(solution)/shard_map/ppermute | solution.py:404
  13.2 1.3 %copy-start.1 = (bf16[64,2,40,128]{3,2,1,0:T(8,128)(2,1)S(1)}, bf16[64,2,40,128]{3,2,1,0:T(8,128)(2,1)}, u32[]{:S(2)}) copy-start(bf16[64,2,40,128]{3,2,1,0:T(8,128)(2,1)} %upstream.1) | copy-start | bytes 3932164
  14.5 0.9 %copy-start.4 = (bf16[3,3,3,32,64]{4,3,2,1,0:T(8,128)(2,1)S(1)}, bf16[3,3,3,32,64]{4,3,2,1,0:T(8,128)(2,1)}, u32[]{:S(2)}) copy-start(bf16[3,3,3,32,64]{4,3,2,1,0:T(8,128)(2,1)} %weights.1) | copy-start | bytes 331780
  34.1 2.5 %copy-start.2 = (bf16[24,64,128]{2,1,0:T(8,128)(2,1)}, bf16[24,64,128]{2,1,0:T(8,128)(2,1)S(1)}, u32[]{:S(2)}) copy-start(bf16[24,64,128]{2,1,0:T(8,128)(2,1)S(1)} %get-tuple-element.36) | copy-start | bytes 1179652
  36.6 0.7 %copy-start.3 = (bf16[16,64,128]{2,1,0:T(8,128)(2,1)}, bf16[16,64,128]{2,1,0:T(8,128)(2,1)S(1)}, u32[]{:S(2)}) copy-start(bf16[16,64,128]{2,1,0:T(8,128)(2,1)S(1)} %get-tuple-element.37) | copy-start | bytes 786436
  37.3 0.7 copy-start
  38.0 1.4 %collective-permute-start.4 = (f32[224,128]{1,0:T(8,128)S(1)}, f32[224,128]{1,0:T(8,128)S(1)}, u32[]{:S(2)}, u32[]{:S(2)}) collective-permute-start(f32[224,128]{1,0:T(8,128)S(1)} %dynamic-slice_bitcast_fusion), channel_id=1, source_target_pairs={{0,1},{1,0},{2,3},{3,2},{4,5},{5,4},{6,7},{7,6},{8,9},{9,8},{10,11... | collective-permute-start | bytes 344072 | tf_op jit(solution)/shard_map/ppermute | solution.py:390
  40.3 5.3 %collective-permute-start.5 = (f32[224,128]{1,0:T(8,128)S(1)}, f32[224,128]{1,0:T(8,128)S(1)}, u32[]{:S(2)}, u32[]{:S(2)}) collective-permute-start(f32[224,128]{1,0:T(8,128)S(1)} %bitcast_add_fusion), channel_id=1, source_target_pairs={{0,2},{1,3},{2,0},{3,1},{4,6},{5,7},{6,4},{7,5},{8,10},{9,11},{10,... | collective-permute-start | bytes 344072 | tf_op jit(solution)/shard_map/ppermute | solution.py:393
  41.0 22.8 %collective-permute-start.2 = (bf16[24,64,128]{2,1,0:T(8,128)(2,1)}, bf16[24,64,128]{2,1,0:T(8,128)(2,1)S(1)}, u32[]{:S(2)}, u32[]{:S(2)}) collective-permute-start(bf16[24,64,128]{2,1,0:T(8,128)(2,1)} %copy-done.2), channel_id=1, source_target_pairs={{1,0},{2,1},{3,2},{4,3},{5,4},{6,5},{7,6},{8,7},{9,8},{10,9},{11,1... | collective-permute-start | bytes 1179656 | tf_op jit(solution)/shard_map/ppermute | solution.py:404
  42.3 21.5 %collective-permute-start.3 = (bf16[16,64,128]{2,1,0:T(8,128)(2,1)}, bf16[16,64,128]{2,1,0:T(8,128)(2,1)S(1)}, u32[]{:S(2)}, u32[]{:S(2)}) collective-permute-start(bf16[16,64,128]{2,1,0:T(8,128)(2,1)} %copy-done.3), channel_id=1, source_target_pairs={{1,0},{2,1},{3,2},{4,3},{5,4},{6,5},{7,6},{8,7},{9,8},{10,9},{11,1... | collective-permute-start | bytes 786440 | tf_op jit(solution)/shard_map/ppermute | solution.py:404
  45.6 12.1 %collective-permute-start.6 = (f32[224,128]{1,0:T(8,128)S(1)}, f32[224,128]{1,0:T(8,128)S(1)}, u32[]{:S(2)}, u32[]{:S(2)}) collective-permute-start(f32[224,128]{1,0:T(8,128)S(1)} %add.23), channel_id=1, source_target_pairs={{0,4},{1,5},{2,6},{3,7},{4,0},{5,1},{6,2},{7,3},{8,12},{9,13},{10,... | collective-permute-start | bytes 344072 | tf_op jit(solution)/shard_map/ppermute | solution.py:393
  57.7 6.0 %collective-permute-start.7 = (f32[224,128]{1,0:T(8,128)S(1)}, f32[224,128]{1,0:T(8,128)S(1)}, u32[]{:S(2)}, u32[]{:S(2)}) collective-permute-start(f32[224,128]{1,0:T(8,128)S(1)} %add.24), channel_id=1, source_target_pairs={{0,8},{1,9},{2,10},{3,11},{4,12},{5,13},{6,14},{7,15},{8,0},{9,1},... | collective-permute-start | bytes 344072 | tf_op jit(solution)/shard_map/ppermute | solution.py:393
  63.7 3.8 %collective-permute-start.8 = (f32[224,128]{1,0:T(8,128)S(1)}, f32[224,128]{1,0:T(8,128)S(1)}, u32[]{:S(2)}, u32[]{:S(2)}) collective-permute-start(f32[224,128]{1,0:T(8,128)S(1)} %add.25), channel_id=1, source_target_pairs={{0,1},{1,0},{2,3},{3,2},{4,5},{5,4},{6,7},{7,6},{8,9},{9,8},{10,11... | collective-permute-start | bytes 344072 | tf_op jit(solution)/shard_map/ppermute | solution.py:395

commit v3 on v2

v3 whole, which is shorter than its diff:
```python
import functools

import jax
import jax.numpy as jnp
from jax import lax
from jax.experimental import pallas as pl
from jax.experimental.pallas import tpu as pltpu
from jax.sharding import PartitionSpec as P

BF = jnp.bfloat16
F32 = jnp.float32
VMEM = pl.BlockSpec(memory_space=pltpu.VMEM)
ANY = pl.BlockSpec(memory_space=pl.ANY)
HBM = pl.BlockSpec(memory_space=pltpu.HBM)
SMEM = pl.BlockSpec(memory_space=pltpu.SMEM)
PARAMS = pltpu.CompilerParams(vmem_limit_bytes=40 * 2**20)


def shape(*dims, dtype=BF):
    return jax.ShapeDtypeStruct(dims, dtype)


def cost(flops, size):
    return pl.CostEstimate(flops=flops, bytes_accessed=size, transcendentals=0)


def picks(half, inverse):
    if inverse:
        row = lax.broadcasted_iota(jnp.int32, (2 * half, 2 * half), 0)
        col = lax.broadcasted_iota(jnp.int32, (2 * half, 2 * half), 1)
        hit = jnp.where(row < half, 2 * row, 2 * (row - half) + 1) == col
    else:
        row = lax.broadcasted_iota(jnp.int32, (2 * half, 3 * half), 0)
        col = lax.broadcasted_iota(jnp.int32, (2 * half, 3 * half), 1)
        early = 2 * col - 1
        even = 2 * (col - half)
        odd = 2 * (col - 2 * half) + 1
        hit = jnp.where(col < half, early, jnp.where(col < 2 * half, even, odd)) == row
    return jnp.where(hit, 1.0, 0.0).astype(BF)


def split_plane(read, lines, table):
    rows, channels, half = lines.shape
    channels //= 3

    def step(t, carry):
        block = jnp.swapaxes(read(pl.multiple_of(t * 16, 16)), 0, 1)
        flat = block.reshape(16 * channels, 2 * half)
        taps = jnp.dot(flat, table, preferred_element_type=F32).astype(BF)
        taps = taps.reshape(16, channels, 3 * half)
        for e in range(3):
            lines[pl.ds(1 + t * 16, 16), e * channels : (e + 1) * channels, :] = taps[
                :, :, e * half : (e + 1) * half
            ]
        return carry

    lax.fori_loop(0, (rows - 1) // 16, step, 0, unroll=True)


def turn_upstream(upstream, turned):
    for o in range(0, upstream.shape[0], 8):
        block = upstream[o : o + 8].astype(F32)
        turned[:, o : o + 8, :] = jnp.swapaxes(block, 0, 1).astype(turned.dtype)


def earlier(values):
    cells = values.shape[-1]
    lane = lax.broadcasted_iota(jnp.int32, values.shape, values.ndim - 1)
    return jnp.where(lane == cells - 1, 0.0, pltpu.roll(values, cells - 1, values.ndim - 1))


def store_grads(pre, upstream, grads, j):
    slope = 0.6 + 0.4 * jnp.tanh(0.5 * pre)
    value = (upstream * slope).astype(BF)
    cout = value.shape[0]
    grads[j, :cout, :] = value
    grads[j, cout:, :] = earlier(value.astype(F32)).astype(BF)


def window(planes, j, count):
    parts = [plane[2 * j : 2 * j + count].reshape(-1, plane.shape[-1]) for plane in planes]
    return parts[0] if len(parts) == 1 else jnp.concatenate(parts, 0)


def weight_terms(cells):
    left, right = [], []
    for lines, grads in cells:
        flat = [line.reshape(-1, line.shape[-1]) for line in lines]
        ones = jnp.ones((16, flat[0].shape[-1]), BF)
        left.append(jnp.concatenate(flat + [ones], 0))
        right.append(jnp.concatenate(grads, 0))
    return lax.dot_general(
        jnp.concatenate(left, 1),
        jnp.concatenate(right, 1),
        (((1,), (1,)), ((), ())),
        preferred_element_type=F32,
    )


class Copies:
    def __init__(self, semaphores):
        self.semaphores, self.used, self.pending = semaphores, 0, []

    def start(self, source, target):
        copy = pltpu.make_async_copy(source, target, self.semaphores.at[self.used])
        self.used += 1
        copy.start()
        self.pending.append(copy)
        return copy

    def wait(self, *copies):
        for copy in copies or list(self.pending):
            copy.wait()
            self.pending.remove(copy)


def spans(total, size):
    return [(at, min(at + size, total)) for at in range(0, total, size)]


def column(bias):
    cout = bias.shape[1]
    row = lax.broadcasted_iota(jnp.int32, (cout, cout), 0)
    col = lax.broadcasted_iota(jnp.int32, (cout, cout), 1)
    return jnp.sum(jnp.where(row == col, bias[...], 0.0), axis=1, keepdims=True)


def lower_kernel(
    volume, weights_in, bias, upstream,
    lines, pre, late, full, back,
    field, inputs, weights, semaphores,
):
    cin = volume.shape[0]
    cout = bias.shape[1]
    half = volume.shape[3] // 2
    ny = upstream.shape[2]
    copies = Copies(semaphores)
    kernel = copies.start(weights_in, weights)
    ins = [copies.start(volume.at[:, z], field.at[z]) for z in range(2)]
    ups = copies.start(upstream.at[:, 0], inputs)
    table = picks(half, False)
    copies.wait(kernel)
    for a in range(3):
        for b in range(3):
            block = jnp.concatenate([weights[a, b, e] for e in range(3)], 0)
            at = (3 * a + b) * 3 * cin
            full[:, at : at + 3 * cin] = block.T
    blank = jnp.zeros((cin, cout), BF)
    for a in range(3):
        for px in range(2):
            for py in range(2):
                row = []
                for dy in range(2):
                    for dx in range(2):
                        b, e = py + 1 - 2 * dy, px + 1 - 2 * dx
                        row.append(weights[a, b, e] if b >= 0 and e >= 0 else blank)
                at = (px * 2 + py) * cin
                back[a, at : at + cin, :] = jnp.concatenate(row, 1)
    planes = [lines.at[z] for z in range(2)]
    for z in range(2):
        planes[z][0] = jnp.zeros(planes[z].shape[1:], BF)
        copies.wait(ins[z])
        split_plane(lambda y, z=z: field[z, :, pl.ds(y, 16), :], planes[z], table)
    copies.wait(ups)
    turn_upstream(inputs, late)
    taps = full[:, 9 * cin :]
    offset = column(bias)
    for lo, hi in spans(ny, 8):
        block = jnp.concatenate([window(planes, j, 3) for j in range(lo, hi)], 1)
        sums = jnp.dot(taps, block, preferred_element_type=F32)
        for j in range(lo, hi):
            pre[j] = sums[:, (j - lo) * half : (j - lo + 1) * half] + offset


def upper_kernel(
    volume, lines, full, bias, upstream,
    grads, terms,
    field, middle, top, inputs, turned, semaphores,
):
    cout = bias.shape[1]
    half = volume.shape[3] // 2
    ny = upstream.shape[2]
    copies = Copies(semaphores)
    ins = [copies.start(volume.at[:, 2 + z], field.at[z]) for z in range(2)]
    ups = copies.start(upstream.at[:, 1], inputs)
    table = picks(half, False)
    planes = [lines.at[1], middle, top]
    for z in range(2):
        planes[1 + z][0] = jnp.zeros(top.shape[1:], BF)
        copies.wait(ins[z])
        split_plane(lambda y, z=z: field[z, :, pl.ds(y, 16), :], planes[1 + z], table)
    copies.wait(ups)
    turn_upstream(inputs, turned)
    offset = column(bias)
    for lo, hi in spans(ny, 8):
        block = jnp.concatenate([window(planes, j, 3) for j in range(lo, hi)], 1)
        sums = jnp.dot(full[...], block, preferred_element_type=F32)
        for j in range(lo, hi):
            at = (j - lo) * half
            store_grads(sums[:, at : at + half] + offset, turned[j], grads, j)
    grads[ny] = jnp.zeros(grads.shape[1:], BF)
    terms[...] = plane_terms(planes, grads)


def plane_terms(planes, grads):
    cout = grads.shape[1] // 2
    return weight_terms(
        [
            (
                [plane[1 + 2 * j : 3 + 2 * j] for plane in planes],
                [grads[j, :cout], grads[j + 1, :cout]],
            )
            for j in range(grads.shape[0] - 1)
        ]
    )


def halo_kernel(halo, pre, upstream, full, grads, raw, below):
    half = below.shape[-1]
    cout, ny = full.shape[0], pre.shape[0]
    below[0] = jnp.zeros(below.shape[1:], BF)
    split_plane(lambda y: halo[:, 0, pl.ds(y, 16), :], below, picks(half, False))
    front = full[:, : full.shape[1] // 3]
    for lo, hi in spans(ny, 8):
        block = jnp.concatenate([window([below], j, 3) for j in range(lo, hi)], 1)
        sums = jnp.dot(front, block, preferred_element_type=F32)
        for j in range(lo, hi):
            at = (j - lo) * half
            store_grads(sums[:, at : at + half] + pre[j], upstream[j].astype(F32), grads, j)
            raw[j] = grads[j, :cout, :]
    grads[ny] = jnp.zeros(grads.shape[1:], BF)


def terms_kernel(below, lines, grads, terms_in, packed):
    terms = terms_in[...] + plane_terms([below, lines.at[0], lines.at[1]], grads)
    pack(terms, packed, below.shape[1], grads.shape[1] // 2)


def pack(terms, packed, count, cout):
    for a in range(3):
        packed[a * count : (a + 1) * count] = terms[(2 * a + 1) * count : (2 * a + 2) * count]
    middle = jnp.concatenate([terms[2 * a * count : (2 * a + 1) * count, :cout] for a in range(3)], 0)
    rows = middle.shape[0] // 2
    packed[3 * count : 3 * count + rows] = jnp.concatenate([middle[:rows], middle[rows:]], 1)
    packed[3 * count + rows :] = jnp.concatenate(
        [terms[6 * count :][:, :cout], jnp.zeros((16, cout), F32)], 1
    )


def finish_kernel(mine, got, weight_grad, bias_grad):
    packed = mine[...].astype(F32) + got[...].astype(F32)
    count = weight_grad.shape[2]
    cout = weight_grad.shape[3]
    for a in range(3):
        block = packed[a * count : (a + 1) * count]
        weight_grad[a, 2] = block[:, :cout]
        weight_grad[a, 0] = block[:, cout:]
    rows = 3 * count // 2
    middle = packed[3 * count : 3 * count + rows]
    middle = jnp.concatenate([middle[:, :cout], middle[:, cout:]], 0)
    for a in range(3):
        weight_grad[a, 1] = middle[a * count : (a + 1) * count]
    bias_grad[...] = packed[3 * count + rows :][:1, :cout]


def back_kernel(z, odd, fresh, aliased, *refs):
    refs = refs[1:] if aliased else refs
    back, grads_in = refs[:2]
    above_in = refs[2 : 2 + odd]
    refs = refs[2 + len(above_in) :]
    total, grads, above, plane, semaphores = refs[:5]
    ny = grads.shape[0] - 1
    cout = grads.shape[1] // 2
    copies = Copies(semaphores)
    loads = []
    for lo, hi in spans(ny, 8):
        top = ny + 1 if hi == ny else hi
        part = [copies.start(grads_in.at[lo:top], grads.at[lo:top])]
        if odd and not fresh:
            part.append(copies.start(above_in[0].at[lo:top], above.at[lo:top]))
        loads.append(part)
    if fresh:
        for j in range(ny):
            value = above_in[0][j]
            above[j, :cout, :] = value
            above[j, cout:, :] = earlier(value.astype(F32)).astype(BF)
        above[ny] = jnp.zeros(above.shape[1:], BF)
    left = jnp.concatenate([back[2], back[0]], 1) if odd else back[1]
    cin = plane.shape[0]
    half = plane.shape[2] // 2
    table = picks(half, True)
    copies.wait(*loads[0])
    for n, (lo, hi) in enumerate(spans(ny, 8)):
        if n + 1 < len(loads):
            copies.wait(*loads[n + 1])
        columns = []
        for j in range(lo, hi):
            parts = [grads[j : j + 2].reshape(-1, half)]
            if odd:
                parts.append(above[j : j + 2].reshape(-1, half))
            columns.append(jnp.concatenate(parts, 0))
        sums = jnp.dot(left, jnp.concatenate(columns, 1), preferred_element_type=F32)
        sums = sums.astype(BF)
        rows = []
        for j in range(hi - lo):
            for py in range(2):
                lanes = slice(j * half, (j + 1) * half)
                even = sums[py * cin : (py + 1) * cin, lanes]
                odds = sums[(2 + py) * cin : (3 + py) * cin, lanes]
                rows.append(jnp.concatenate([even, odds], 1))
        merged = jnp.dot(jnp.concatenate(rows, 0), table, preferred_element_type=F32)
        merged = merged.astype(BF).reshape(2 * (hi - lo), cin, 2 * half)
        plane[:, 2 * lo : 2 * hi, :] = jnp.swapaxes(merged, 0, 1)
        copies.start(plane.at[:, 2 * lo : 2 * hi], total.at[:, z, 2 * lo : 2 * hi])
    copies.wait()


def back_plane(z, total, full, back, grads, above=()):
    cin, depth, height, width = full
    fresh = len(above) > 0 and above[0].shape != grads.shape
    args = [back, grads, *above]
    specs = [VMEM, ANY] + [VMEM if fresh else ANY] * len(above)
    aliased = total is not None
    if aliased:
        args = [total] + args
        specs = [ANY] + specs
    return pl.pallas_call(
        functools.partial(back_kernel, z, len(above) > 0, fresh, aliased),
        in_specs=specs,
        out_specs=ANY,
        out_shape=shape(*full),
        scratch_shapes=[
            pltpu.VMEM(grads.shape, BF),
            pltpu.VMEM(grads.shape if above else (16, 128), BF),
            pltpu.VMEM((cin, height, width), BF),
            pltpu.SemaphoreType.DMA((3 * (height // 16),)),
        ],
        input_output_aliases={0: 0} if aliased else {},
        compiler_params=PARAMS,
        cost_estimate=cost(3 * 10**9, 4 * 2**20),
    )(*args)


def all_sum(value, axis, total, above, works):
    peers = lax.axis_size(axis)
    works = list(works)
    got = lax.ppermute(value, axis, [(i, i ^ 1) for i in range(peers)])
    step = 2
    while step < peers:
        sent, total = lax.optimization_barrier(
            ((value.astype(F32) + got.astype(F32)).astype(BF), total)
        )
        value = sent
        got = lax.ppermute(sent, axis, [(i, i ^ step) for i in range(peers)])
        if works:
            total, above = works.pop(0)(total, above)
        got, total = lax.optimization_barrier((got, total))
        step *= 2
    for work in works:
        total, above = work(total, above)
    return value, got, total


def shifted(x, axis, by):
    peers = lax.axis_size(axis)
    pairs = [(i, i + by) for i in range(peers) if 0 <= i + by < peers]
    return lax.ppermute(x, axis, pairs)


def shards(volume, weights, bias, upstream):
    cin, depth, height, width = volume.shape
    cout = bias.shape[0]
    ny, half = height // 2, width // 2
    rows, count = height + 1, 3 * cin
    halo = shifted(volume[:, depth - 1 :], "slab", 1)
    grads_shape = (ny + 1, 2 * cout, half)
    terms_shape = (6 * count + 16, 2 * cout)
    bias = bias.reshape(1, cout)
    pinned = pltpu.with_memory_space_constraint(volume, pltpu.HBM)
    lines, pre, late, taps, back = pl.pallas_call(
        lower_kernel,
        in_specs=[ANY, ANY, VMEM, ANY],
        out_specs=[VMEM] * 5,
        out_shape=[
            shape(2, rows, count, half),
            shape(ny, cout, half, dtype=F32),
            shape(ny, cout, half),
            shape(cout, 9 * count),
            shape(3, 4 * cin, 4 * cout),
        ],
        scratch_shapes=[
            pltpu.VMEM((2, cin, height, width), BF),
            pltpu.VMEM((cout, ny, half), BF),
            pltpu.VMEM(weights.shape, BF),
            pltpu.SemaphoreType.DMA((4,)),
        ],
        compiler_params=PARAMS,
        cost_estimate=cost(5 * 10**9, 10 * 2**20),
    )(pinned, weights, bias, upstream)
    upper, terms = pl.pallas_call(
        upper_kernel,
        in_specs=[ANY, VMEM, VMEM, VMEM, ANY],
        out_specs=[VMEM] * 2,
        out_shape=[shape(*grads_shape), shape(*terms_shape, dtype=F32)],
        scratch_shapes=[
            pltpu.VMEM((2, cin, height, width), BF),
            pltpu.VMEM((rows, count, half), BF),
            pltpu.VMEM((rows, count, half), BF),
            pltpu.VMEM((cout, ny, half), BF),
            pltpu.VMEM((ny, cout, half), F32),
            pltpu.SemaphoreType.DMA((3,)),
        ],
        compiler_params=PARAMS,
        cost_estimate=cost(6 * 10**9, 10 * 2**20),
    )(pinned, lines, taps, bias, upstream)
    full = volume.shape

    total = back_plane(2, None, full, back, upper)
    total, halo = lax.optimization_barrier((total, halo))
    lower, raw, below = pl.pallas_call(
        halo_kernel,
        in_specs=[VMEM] * 4,
        out_specs=[VMEM] * 3,
        out_shape=[shape(*grads_shape), shape(ny, cout, half), shape(rows, count, half)],
        compiler_params=PARAMS,
        cost_estimate=cost(3 * 10**9, 6 * 2**20),
    )(halo, pre, late, taps)
    above = shifted(raw, "slab", -1)
    packed = pl.pallas_call(
        terms_kernel,
        in_specs=[VMEM] * 4,
        out_specs=VMEM,
        out_shape=shape(9 * count // 2 + 16, 2 * cout, dtype=F32),
        compiler_params=PARAMS,
        cost_estimate=cost(10**8, 10**5),
    )(below, lines, lower, terms)

    def middle(total, above):
        total, above = lax.optimization_barrier((total, above))
        return back_plane(1, total, full, back, lower, (upper,)), above

    packed, got, total = all_sum(
        packed,
        "slab",
        total,
        above,
        [
            lambda t, g: (back_plane(0, t, full, back, lower), g),
            middle,
            lambda t, g: (back_plane(3, t, full, back, upper, (g,)), g),
        ],
    )
    weight_grad, bias_grad = pl.pallas_call(
        finish_kernel,
        in_specs=[VMEM] * 2,
        out_specs=[VMEM] * 2,
        out_shape=[shape(3, 3, count, cout, dtype=F32), shape(1, cout, dtype=F32)],
        compiler_params=PARAMS,
    )(packed, got)
    return (
        total,
        weight_grad.reshape(3, 3, 3, cin, cout),
        bias_grad.reshape(cout),
    )


def solution(mesh):
    placed = (
        P(None, ("groups", "slab"), None, None),
        P(),
        P(),
        P(None, ("groups", "slab"), None, None),
    )
    return jax.shard_map(
        shards,
        mesh=mesh,
        in_specs=placed,
        out_specs=(
            P(None, ("groups", "slab"), None, None),
            P("groups", None, None, None, None),
            P("groups"),
        ),
        check_vma=False,
    )
```

time: 68.9 us -> 55.1 us (0.80)
  local copies, waits for them, and re-layouts: 8.38 us -> 1.54 us
  Pallas kernels: 32.2 us -> 29.2 us
  waiting for transfers between devices: 10.7 us -> 8.49 us
  other arithmetic: 0.99 us -> 0.1 us
    ppermute x4 -> x2, starting transfers between devices: 10.4 us -> 3.72 us  [shifted(): return lax.ppermute(x, axis, pairs)]
    ppermute x5 -> x4, starting transfers between devices: 4.88 us -> 11 us  [the longest x3 8.41 us: all_sum(): got = lax.ppermute(sent, axis, [(i, i ^ step) for i in range(peers)])]
    unnamed x10 -> x6, local copies, waits for them, and re-layouts: 3.64 us -> 0.01 us
    pallas_call x4 -> x5, Pallas kernels: 19 us -> 15.8 us  [the longest x1 6.45 us: shards(): pl.pallas_call(upper_kernel, in_specs=[ANY, VMEM, VMEM, VMEM, ANY], out_s...]
    slice x2 -> x1, local copies, waits for them, and re-layouts: 3.99 us -> 1.52 us  [shards(): halo = shifted(volume[:, depth - 1:], 'slab', 1)]
    ppermute x5 -> x4, waiting for transfers between devices: 10.7 us -> 8.48 us  [the longest x3 8.48 us: all_sum(): got = lax.ppermute(sent, axis, [(i, i ^ step) for i in range(peers)])]
    add x4 -> x0, other arithmetic: 0.95 us -> none  [the longest x1 0.91 us: all_sum(): mine = mine + lax.ppermute(other, axis, swap)]
    reshape x1 -> x0, local copies, waits for them, and re-layouts: 0.74 us -> none  [shards(): bias.reshape(cout, 1)]
  transfers between devices with their start and end apart: 9 -> 6, of which waited for: 4 -> 2; matrix products, arithmetic and copies ran while one was open for 4% -> 0% of each run, Pallas kernels for 42% -> 45%
where the time goes in v3:
time: 55.1 us; the launch traced here: 54.9 us
  Pallas kernels  29.2 us (53%)
  starting transfers between devices  14.8 us (27%)
  waiting for transfers between devices  8.49 us (15%)
  local copies, waits for them, and re-layouts  1.54 us (3%)
  between operations  0.8 us (1%)
    pallas_call x4, Pallas kernels, back_plane(): pl.pallas_call(functools.partial(back_kernel, z, len(above) > 0, fresh, a...  13.4 us
    ppermute x3, waiting for transfers between devices, all_sum(): got = lax.ppermute(sent, axis, [(i, i ^ step) for i in range(peers)])  8.48 us
    ppermute x3, starting transfers between devices, all_sum(): got = lax.ppermute(sent, axis, [(i, i ^ step) for i in range(peers)])  8.41 us
    pallas_call x1, Pallas kernels, shards(): pl.pallas_call(upper_kernel, in_specs=[ANY, VMEM, VMEM, VMEM, ANY], out_s...  6.45 us
    pallas_call x1, Pallas kernels, shards(): pl.pallas_call(lower_kernel, in_specs=[ANY, ANY, VMEM, ANY], out_specs=[V...  4.91 us
    ppermute x2, starting transfers between devices, shifted(): return lax.ppermute(x, axis, pairs)  3.72 us
    ppermute x1, starting transfers between devices, all_sum(): got = lax.ppermute(value, axis, [(i, i ^ 1) for i in range(peers)])  2.62 us
    pallas_call x1, Pallas kernels, shards(): pl.pallas_call(terms_kernel, in_specs=[VMEM] * 4, out_specs=VMEM, out_sha...  1.78 us
  transfers between devices with their start and end apart: 6, of which 2 were waited for; matrix products, arithmetic and copies ran while one was open for 0% of the time, Pallas kernels for 45%

profile of v3, /device:TPU:0, one launch (start us, length us, event | category | flops | bytes accessed | tf_op | source)
XLA Modules:
  0.0 54.9 jit_solution(14301161966364630031)
XLA Ops:
  0.6 0.0 copy-start
  0.6 0.0 copy-start.2
  0.7 0.0 copy-start.1
  0.7 1.5 %slice.3 = bf16[32,1,80,256]{3,2,1,0:T(8,128)(2,1)S(1)} slice(bf16[32,4,80,256]{3,2,1,0:T(8,128)(2,1)} %volume.3), slice={[0:32], [3:4], [0:80], [0:256]} | slice | bytes 2621440 | tf_op jit(solution)/shard_map/slice | solution.py:375
  2.2 2.4 %collective-permute-start = (bf16[32,1,80,256]{3,2,1,0:T(8,128)(2,1)S(1)}, bf16[32,1,80,256]{3,2,1,0:T(8,128)(2,1)S(1)}, u32[]{:S(2)}, u32[]{:S(2)}) collective-permute-start(bf16[32,1,80,256]{3,2,1,0:T(8,128)(2,1)S(1)} %slice.3), channel_id=1, source_target_pairs={{0,1},{1,2},{2,3},{3,4},{4,5},{5,6},{6,7},{7,8},{8,9},{9,10},{10,1... | collective-permute-start | bytes 3932168 | tf_op jit(solution)/shard_map/ppermute | solution.py:367
  4.6 0.0 copy-done
  4.6 0.0 copy-done.2
  4.7 0.0 copy-done.1
  4.7 4.9 %shard_map.67 = (bf16[2,81,96,128]{3,2,1,0:T(8,128)(2,1)S(1)}, f32[40,64,128]{2,1,0:T(8,128)S(1)}, bf16[40,64,128]{2,1,0:T(8,128)(2,1)S(1)}, bf16[64,864]{1,0:T(8,128)(2,1)S(1)}, bf16[3,128,256]{2,1,0:T(8,128)(2,1)S(1)}) custom-call(bf16[32,4,80,256]{3,2,1,0:T(8,128)(2,1)} %volume.3, bf16[3,3,3,32,64]{4,3,2,1,0:T(8,128)(2,1)S(1)} %copy-done.1, ...), custom_call_target="tpu_custom_call" | custom-call | flops 5000000000 | bytes 10485760 | tf_op jit(solution)/shard_map/pallas_call | solution.py:380
  9.6 6.4 %shard_map.68 = (bf16[41,128,128]{2,1,0:T(8,128)(2,1)S(1)}, f32[592,128]{1,0:T(8,128)S(1)}) custom-call(bf16[32,4,80,256]{3,2,1,0:T(8,128)(2,1)} %volume.3, bf16[2,81,96,128]{3,2,1,0:T(8,128)(2,1)S(1)} %get-tuple-element.32.lines, bf16[64,864]{1,0:T(8,128)(2,1)S(1)} %get-tuple-element.33.full, f32[1,64]{1,0:T(1,128)S(1)} %bitcast.4, ...), custom_call_target="tpu_custom_call" | custom-call | flops 6000000000 | bytes 10485760 | tf_op jit(solution)/shard_map/pallas_call | solution.py:400
  16.0 3.2 %shard_map.69.refs_0_ = bf16[32,4,80,256]{3,2,1,0:T(8,128)(2,1)} custom-call(bf16[3,128,256]{2,1,0:T(8,128)(2,1)S(1)} %get-tuple-element.31.refs_0_.refs_1_, bf16[41,128,128]{2,1,0:T(8,128)(2,1)S(1)} %get-tuple-element.34.refs_1_.refs_3_.refs_2_), custom_call_target="tpu_custom_call" | custom-call | flops 3000000000 | bytes 4194304 | tf_op jit(solution)/shard_map/pallas_call | solution.py:327
  19.2 0.0 collective-permute-done.halo
  19.2 1.8 %shard_map.70 = (bf16[41,128,128]{2,1,0:T(8,128)(2,1)S(1)}, bf16[40,64,128]{2,1,0:T(8,128)(2,1)S(1)}, bf16[81,96,128]{2,1,0:T(8,128)(2,1)S(1)}) custom-call(bf16[32,1,80,256]{3,2,1,0:T(8,128)(2,1)S(1)} %collective-permute-done.halo, f32[40,64,128]{2,1,0:T(8,128)S(1)} %get-tuple-element.36.pre, bf16[40,64,128]{2,1,0:T(8,128)(2,1)S(1)} %get-tuple-element.37.upstream, ...), custom_call_target="tpu_custom_call" | custom-call | flops 3000000000 | bytes 6291456 | tf_op jit(solution)/shard_map/pallas_call | solution.py:420
  21.0 1.8 %shard_map.71 = f32[448,128]{1,0:T(8,128)S(1)} custom-call(bf16[81,96,128]{2,1,0:T(8,128)(2,1)S(1)} %get-tuple-element.38.below, bf16[2,81,96,128]{3,2,1,0:T(8,128)(2,1)S(1)} %get-tuple-element.32.lines, bf16[41,128,128]{2,1,0:T(8,128)(2,1)S(1)} %get-tuple-element.39.grads.refs_2_, f32[592,128]{1,0:T(8,128)S(1)} %get-tuple-element.40.terms_in), custom_call_target="tpu_custom_call" | custom-call | flops 100000000 | bytes 100000 | tf_op jit(solution)/shard_map/pallas_call | solution.py:429
  22.8 2.6 %collective-permute-start.1 = (f32[448,128]{1,0:T(8,128)S(1)}, f32[448,128]{1,0:T(8,128)S(1)}, u32[]{:S(2)}, u32[]{:S(2)}) collective-permute-start(f32[448,128]{1,0:T(8,128)S(1)} %shard_map.71), channel_id=1, source_target_pairs={{0,1},{1,0},{2,3},{3,2},{4,5},{5,4},{6,7},{7,6},{8,9},{9,8},{10,11... | collective-permute-start | bytes 688136 | tf_op jit(solution)/shard_map/ppermute | solution.py:347
  25.4 1.3 %collective-permute-start.4 = (bf16[40,64,128]{2,1,0:T(8,128)(2,1)S(1)}, bf16[40,64,128]{2,1,0:T(8,128)(2,1)S(1)}, u32[]{:S(2)}, u32[]{:S(2)}) collective-permute-start(bf16[40,64,128]{2,1,0:T(8,128)(2,1)S(1)} %get-tuple-element.48), channel_id=1, source_target_pairs={{1,0},{2,1},{3,2},{4,3},{5,4},{6,5},{7,6},{8,7},{9,8},{10,9},{11,1... | collective-permute-start | bytes 1966088 | tf_op jit(solution)/shard_map/ppermute | solution.py:367
  26.7 0.0 collective-permute-done.1
  26.8 3.0 %collective-permute-start.2 = (bf16[448,128]{1,0:T(8,128)(2,1)S(1)}, bf16[448,128]{1,0:T(8,128)(2,1)S(1)}, u32[]{:S(2)}, u32[]{:S(2)}) collective-permute-start(bf16[448,128]{1,0:T(8,128)(2,1)S(1)} %add_convert_fusion.2), channel_id=1, source_target_pairs={{0,2},{1,3},{2,0},{3,1},{4,6},{5,7},{6,4},{7,5},{8,10},{9,11},{10,... | collective-permute-start | bytes 344072 | tf_op jit(solution)/shard_map/ppermute | solution.py:354
  29.7 3.0 %shard_map.72.refs_0_ = bf16[32,4,80,256]{3,2,1,0:T(8,128)(2,1)} custom-call(bf16[32,4,80,256]{3,2,1,0:T(8,128)(2,1)} %shard_map.69.refs_0_, bf16[3,128,256]{2,1,0:T(8,128)(2,1)S(1)} %get-tuple-element.31.refs_0_.refs_1_, bf16[41,128,128]{2,1,0:T(8,128)(2,1)S(1)} %get-tuple-element.39.grads.refs_2_), custom_call_target="tpu_custom_call", output_to_operand_aliasing={{}: (0, {})} | custom-call | flops 3000000000 | bytes 4194304 | tf_op jit(solution)/shard_map/pallas_call | solution.py:327
  32.7 7.8 %collective-permute-done.2 = bf16[448,128]{1,0:T(8,128)(2,1)S(1)} collective-permute-done((bf16[448,128]{1,0:T(8,128)(2,1)S(1)}, bf16[448,128]{1,0:T(8,128)(2,1)S(1)}, u32[]{:S(2)}, u32[]{:S(2)}) %collective-permute-start.2) | collective-permute-done | bytes 114720 | tf_op jit(solution)/shard_map/ppermute | solution.py:354
  40.6 2.8 %collective-permute-start.3 = (bf16[448,128]{1,0:T(8,128)(2,1)S(1)}, bf16[448,128]{1,0:T(8,128)(2,1)S(1)}, u32[]{:S(2)}, u32[]{:S(2)}) collective-permute-start(bf16[448,128]{1,0:T(8,128)(2,1)S(1)} %add_convert_fusion.1), channel_id=1, source_target_pairs={{0,4},{1,5},{2,6},{3,7},{4,0},{5,1},{6,2},{7,3},{8,12},{9,13},{10,... | collective-permute-start | bytes 344072 | tf_op jit(solution)/shard_map/ppermute | solution.py:354
  43.4 0.0 collective-permute-done.4.refs_3_
  43.4 3.6 %shard_map.73.refs_0_ = bf16[32,4,80,256]{3,2,1,0:T(8,128)(2,1)} custom-call(bf16[32,4,80,256]{3,2,1,0:T(8,128)(2,1)} %shard_map.72.refs_0_, bf16[3,128,256]{2,1,0:T(8,128)(2,1)S(1)} %get-tuple-element.31.refs_0_.refs_1_, bf16[41,128,128]{2,1,0:T(8,128)(2,1)S(1)} %get-tuple-element.39.grads.refs_2_, ...), custom_call_target="tpu_custom_call", output_to_operand_aliasing={{}: (0, {})} | custom-call | flops 3000000000 | bytes 4194304 | tf_op jit(solution)/shard_map/pallas_call | solution.py:327
  46.9 0.0 collective-permute-done.3
  47.0 2.7 %collective-permute-start.5 = (bf16[448,128]{1,0:T(8,128)(2,1)S(1)}, bf16[448,128]{1,0:T(8,128)(2,1)S(1)}, u32[]{:S(2)}, u32[]{:S(2)}) collective-permute-start(bf16[448,128]{1,0:T(8,128)(2,1)S(1)} %add_convert_fusion.mine), channel_id=1, source_target_pairs={{0,8},{1,9},{2,10},{3,11},{4,12},{5,13},{6,14},{7,15},{8,0},{9,1},... | collective-permute-start | bytes 344072 | tf_op jit(solution)/shard_map/ppermute | solution.py:354
  49.7 3.7 %shard_map.74 = bf16[32,4,80,256]{3,2,1,0:T(8,128)(2,1)} custom-call(bf16[32,4,80,256]{3,2,1,0:T(8,128)(2,1)} %shard_map.73.refs_0_, bf16[3,128,256]{2,1,0:T(8,128)(2,1)S(1)} %get-tuple-element.31.refs_0_.refs_1_, bf16[41,128,128]{2,1,0:T(8,128)(2,1)S(1)} %get-tuple-element.34.refs_1_.refs_3_.refs_2_, ...), custom_call_target="tpu_custom_call", output_to_operand_aliasing={{}: (0, {})} | custom-call | flops 3000000000 | bytes 4194304 | tf_op jit(solution)/shard_map/pallas_call | solution.py:327
  53.3 0.7 %collective-permute-done.5.got = bf16[448,128]{1,0:T(8,128)(2,1)S(1)} collective-permute-done((bf16[448,128]{1,0:T(8,128)(2,1)S(1)}, bf16[448,128]{1,0:T(8,128)(2,1)S(1)}, u32[]{:S(2)}, u32[]{:S(2)}) %collective-permute-start.5) | collective-permute-done | bytes 114720 | tf_op jit(solution)/shard_map/ppermute | solution.py:354
  54.0 0.9 %shard_map.75 = (f32[3,3,96,64]{3,2,1,0:T(8,128)}, f32[1,64]{1,0:T(1,128)}) custom-call(bf16[448,128]{1,0:T(8,128)(2,1)S(1)} %add_convert_fusion.mine, bf16[448,128]{1,0:T(8,128)(2,1)S(1)} %collective-permute-done.5.got), custom_call_target="tpu_custom_call" | custom-call | tf_op jit(solution)/shard_map/pallas_call | solution.py:453
  (3 shorter events, 0.1 us)
Async XLA Ops:
  0.6 4.0 %copy-start = (bf16[64,2,40,128]{3,2,1,0:T(8,128)(2,1)S(1)}, bf16[64,2,40,128]{3,2,1,0:T(8,128)(2,1)}, u32[]{:S(2)}) copy-start(bf16[64,2,40,128]{3,2,1,0:T(8,128)(2,1)} %upstream.3) | copy-start | bytes 3932164
  0.6 4.0 %copy-start.2 = (f32[64]{0:T(128)S(1)}, f32[64]{0:T(128)}, u32[]{:S(2)}) copy-start(f32[64]{0:T(128)} %param.6) | copy-start | bytes 772
  0.7 4.0 %copy-start.1 = (bf16[3,3,3,32,64]{4,3,2,1,0:T(8,128)(2,1)S(1)}, bf16[3,3,3,32,64]{4,3,2,1,0:T(8,128)(2,1)}, u32[]{:S(2)}) copy-start(bf16[3,3,3,32,64]{4,3,2,1,0:T(8,128)(2,1)} %weights_in.1) | copy-start | bytes 331780
  2.2 17.0 %collective-permute-start = (bf16[32,1,80,256]{3,2,1,0:T(8,128)(2,1)S(1)}, bf16[32,1,80,256]{3,2,1,0:T(8,128)(2,1)S(1)}, u32[]{:S(2)}, u32[]{:S(2)}) collective-permute-start(bf16[32,1,80,256]{3,2,1,0:T(8,128)(2,1)S(1)} %slice.3), channel_id=1, source_target_pairs={{0,1},{1,2},{2,3},{3,4},{4,5},{5,6},{6,7},{7,8},{8,9},{9,10},{10,1... | collective-permute-start | bytes 3932168 | tf_op jit(solution)/shard_map/ppermute | solution.py:367
  22.8 3.9 %collective-permute-start.1 = (f32[448,128]{1,0:T(8,128)S(1)}, f32[448,128]{1,0:T(8,128)S(1)}, u32[]{:S(2)}, u32[]{:S(2)}) collective-permute-start(f32[448,128]{1,0:T(8,128)S(1)} %shard_map.71), channel_id=1, source_target_pairs={{0,1},{1,0},{2,3},{3,2},{4,5},{5,4},{6,7},{7,6},{8,9},{9,8},{10,11... | collective-permute-start | bytes 688136 | tf_op jit(solution)/shard_map/ppermute | solution.py:347
  25.4 18.0 %collective-permute-start.4 = (bf16[40,64,128]{2,1,0:T(8,128)(2,1)S(1)}, bf16[40,64,128]{2,1,0:T(8,128)(2,1)S(1)}, u32[]{:S(2)}, u32[]{:S(2)}) collective-permute-start(bf16[40,64,128]{2,1,0:T(8,128)(2,1)S(1)} %get-tuple-element.48), channel_id=1, source_target_pairs={{1,0},{2,1},{3,2},{4,3},{5,4},{6,5},{7,6},{8,7},{9,8},{10,9},{11,1... | collective-permute-start | bytes 1966088 | tf_op jit(solution)/shard_map/ppermute | solution.py:367
  26.8 13.8 %collective-permute-start.2 = (bf16[448,128]{1,0:T(8,128)(2,1)S(1)}, bf16[448,128]{1,0:T(8,128)(2,1)S(1)}, u32[]{:S(2)}, u32[]{:S(2)}) collective-permute-start(bf16[448,128]{1,0:T(8,128)(2,1)S(1)} %add_convert_fusion.2), channel_id=1, source_target_pairs={{0,2},{1,3},{2,0},{3,1},{4,6},{5,7},{6,4},{7,5},{8,10},{9,11},{10,... | collective-permute-start | bytes 344072 | tf_op jit(solution)/shard_map/ppermute | solution.py:354
  40.6 6.3 %collective-permute-start.3 = (bf16[448,128]{1,0:T(8,128)(2,1)S(1)}, bf16[448,128]{1,0:T(8,128)(2,1)S(1)}, u32[]{:S(2)}, u32[]{:S(2)}) collective-permute-start(bf16[448,128]{1,0:T(8,128)(2,1)S(1)} %add_convert_fusion.1), channel_id=1, source_target_pairs={{0,4},{1,5},{2,6},{3,7},{4,0},{5,1},{6,2},{7,3},{8,12},{9,13},{10,... | collective-permute-start | bytes 344072 | tf_op jit(solution)/shard_map/ppermute | solution.py:354
  47.0 7.0 %collective-permute-start.5 = (bf16[448,128]{1,0:T(8,128)(2,1)S(1)}, bf16[448,128]{1,0:T(8,128)(2,1)S(1)}, u32[]{:S(2)}, u32[]{:S(2)}) collective-permute-start(bf16[448,128]{1,0:T(8,128)(2,1)S(1)} %add_convert_fusion.mine), channel_id=1, source_target_pairs={{0,8},{1,9},{2,10},{3,11},{4,12},{5,13},{6,14},{7,15},{8,0},{9,1},... | collective-permute-start | bytes 344072 | tf_op jit(solution)/shard_map/ppermute | solution.py:354

commit v4 on v3

--- a/solution.py
+++ b/solution.py
@@ -233,17 +233,22 @@
 
 def terms_kernel(below, lines, grads, terms_in, packed):
     terms = terms_in[...] + plane_terms([below, lines.at[0], lines.at[1]], grads)
-    pack(terms, packed, below.shape[1], grads.shape[1] // 2)
-
-
-def pack(terms, packed, count, cout):
+    pack(terms, packed, below.shape[1], grads.shape[1] // 2, lax.axis_index("slab"))
+
+
+def pack(terms, packed, count, cout, place):
     for a in range(3):
         packed[a * count : (a + 1) * count] = terms[(2 * a + 1) * count : (2 * a + 2) * count]
     middle = jnp.concatenate([terms[2 * a * count : (2 * a + 1) * count, :cout] for a in range(3)], 0)
     rows = middle.shape[0] // 2
     packed[3 * count : 3 * count + rows] = jnp.concatenate([middle[:rows], middle[rows:]], 1)
-    packed[3 * count + rows :] = jnp.concatenate(
-        [terms[6 * count :][:, :cout], jnp.zeros((16, cout), F32)], 1
+    total = terms[6 * count : 6 * count + 8, :cout]
+    high = total.astype(BF).astype(F32)
+    both = jnp.concatenate([high, total - high], 1)
+    slots = packed.shape[0] - 3 * count - rows
+    row = lax.broadcasted_iota(jnp.int32, (slots, 2 * cout), 0)
+    packed[3 * count + rows :] = jnp.where(
+        row == place, jnp.broadcast_to(both[:1], (slots, 2 * cout)), 0.0
     )
 
 
@@ -260,7 +265,8 @@
     middle = jnp.concatenate([middle[:, :cout], middle[:, cout:]], 0)
     for a in range(3):
         weight_grad[a, 1] = middle[a * count : (a + 1) * count]
-    bias_grad[...] = packed[3 * count + rows :][:1, :cout]
+    total = jnp.sum(packed[3 * count + rows :], axis=0, keepdims=True)
+    bias_grad[...] = total[:, :cout] + total[:, cout:]
 
 
 def back_kernel(z, odd, fresh, aliased, *refs):
@@ -337,14 +343,17 @@
         ],
         input_output_aliases={0: 0} if aliased else {},
         compiler_params=PARAMS,
-        cost_estimate=cost(3 * 10**9, 4 * 2**20),
+        cost_estimate=cost(10**6, 10**3),
     )(*args)
 
 
 def all_sum(value, axis, total, above, works):
     peers = lax.axis_size(axis)
     works = list(works)
+    value, total = lax.optimization_barrier((value, total))
     got = lax.ppermute(value, axis, [(i, i ^ 1) for i in range(peers)])
+    total, above = works.pop(0)(total, above)
+    got, total = lax.optimization_barrier((got, total))
     step = 2
     while step < peers:
         sent, total = lax.optimization_barrier(
@@ -354,7 +363,7 @@
         got = lax.ppermute(sent, axis, [(i, i ^ step) for i in range(peers)])
         if works:
             total, above = works.pop(0)(total, above)
-        got, total = lax.optimization_barrier((got, total))
+        got, total, above = lax.optimization_barrier((got, total, above))
         step *= 2
     for work in works:
         total, above = work(total, above)
@@ -425,19 +434,16 @@
         compiler_params=PARAMS,
         cost_estimate=cost(3 * 10**9, 6 * 2**20),
     )(halo, pre, late, taps)
+    slots = (lax.axis_size("slab") + 15) // 16 * 16
     above = shifted(raw, "slab", -1)
     packed = pl.pallas_call(
         terms_kernel,
         in_specs=[VMEM] * 4,
         out_specs=VMEM,
-        out_shape=shape(9 * count // 2 + 16, 2 * cout, dtype=F32),
+        out_shape=shape(9 * count // 2 + slots, 2 * cout, dtype=F32),
         compiler_params=PARAMS,
         cost_estimate=cost(10**8, 10**5),
     )(below, lines, lower, terms)
-
-    def middle(total, above):
-        total, above = lax.optimization_barrier((total, above))
-        return back_plane(1, total, full, back, lower, (upper,)), above
 
     packed, got, total = all_sum(
         packed,
@@ -446,7 +452,7 @@
         above,
         [
             lambda t, g: (back_plane(0, t, full, back, lower), g),
-            middle,
+            lambda t, g: (back_plane(1, t, full, back, lower, (upper,)), g),
             lambda t, g: (back_plane(3, t, full, back, upper, (g,)), g),
         ],
     )

time: 55.1 us -> 53.4 us (0.969)
  waiting for transfers between devices: 8.49 us -> 7.3 us
    ppermute x3, waiting for transfers between devices: 8.48 us -> 7.29 us  [all_sum(): got = lax.ppermute(sent, axis, [(i, i ^ step) for i in range(peers)])]
    ppermute x3, starting transfers between devices: 8.41 us -> 7.23 us  [all_sum(): got = lax.ppermute(sent, axis, [(i, i ^ step) for i in range(peers)])]
    ppermute x1, starting transfers between devices: 2.62 us -> 3.31 us  [all_sum(): got = lax.ppermute(value, axis, [(i, i ^ 1) for i in range(peers)])]
  transfers between devices with their start and end apart: 6 -> 6, of which waited for: 2 -> 2; matrix products, arithmetic and copies ran while one was open for 0% -> 0% of each run, Pallas kernels for 45% -> 50%
where the time goes in v4:
time: 53.4 us; the launch traced here: 53.2 us
  Pallas kernels  29 us (54%)
  starting transfers between devices  14.4 us (27%)
  waiting for transfers between devices  7.3 us (14%)
  local copies, waits for them, and re-layouts  1.54 us (3%)
  between operations  0.79 us (1%)
    pallas_call x4, Pallas kernels, back_plane(): pl.pallas_call(functools.partial(back_kernel, z, len(above) > 0, fresh, a...  13.2 us
    ppermute x3, waiting for transfers between devices, all_sum(): got = lax.ppermute(sent, axis, [(i, i ^ step) for i in range(peers)])  7.29 us
    ppermute x3, starting transfers between devices, all_sum(): got = lax.ppermute(sent, axis, [(i, i ^ step) for i in range(peers)])  7.23 us
    pallas_call x1, Pallas kernels, shards(): pl.pallas_call(upper_kernel, in_specs=[ANY, VMEM, VMEM, VMEM, ANY], out_s...  6.45 us
    pallas_call x1, Pallas kernels, shards(): pl.pallas_call(lower_kernel, in_specs=[ANY, ANY, VMEM, ANY], out_specs=[V...  4.92 us
    ppermute x2, starting transfers between devices, shifted(): return lax.ppermute(x, axis, pairs)  3.91 us
    ppermute x1, starting transfers between devices, all_sum(): got = lax.ppermute(value, axis, [(i, i ^ 1) for i in range(peers)])  3.31 us
    pallas_call x1, Pallas kernels, shards(): pl.pallas_call(terms_kernel, in_specs=[VMEM] * 4, out_specs=VMEM, out_sha...  1.81 us
  transfers between devices with their start and end apart: 6, of which 2 were waited for; matrix products, arithmetic and copies ran while one was open for 0% of the time, Pallas kernels for 50%

profile of v4, /device:TPU:0, one launch (start us, length us, event | category | flops | bytes accessed | tf_op | source)
XLA Modules:
  0.0 53.2 jit_solution(16252578995540381382)
XLA Ops:
  0.6 0.0 copy-start
  0.6 0.0 copy-start.2
  0.7 0.0 copy-start.1
  0.7 1.5 %slice.3 = bf16[32,1,80,256]{3,2,1,0:T(8,128)(2,1)S(1)} slice(bf16[32,4,80,256]{3,2,1,0:T(8,128)(2,1)} %volume.3), slice={[0:32], [3:4], [0:80], [0:256]} | slice | bytes 2621440 | tf_op jit(solution)/shard_map/slice | solution.py:384
  2.2 2.4 %collective-permute-start = (bf16[32,1,80,256]{3,2,1,0:T(8,128)(2,1)S(1)}, bf16[32,1,80,256]{3,2,1,0:T(8,128)(2,1)S(1)}, u32[]{:S(2)}, u32[]{:S(2)}) collective-permute-start(bf16[32,1,80,256]{3,2,1,0:T(8,128)(2,1)S(1)} %slice.3), channel_id=1, source_target_pairs={{0,1},{1,2},{2,3},{3,4},{4,5},{5,6},{6,7},{7,8},{8,9},{9,10},{10,1... | collective-permute-start | bytes 3932168 | tf_op jit(solution)/shard_map/ppermute | solution.py:376
  4.6 0.0 copy-done
  4.6 0.0 copy-done.2
  4.7 0.0 copy-done.1
  4.7 4.9 %shard_map.67 = (bf16[2,81,96,128]{3,2,1,0:T(8,128)(2,1)S(1)}, f32[40,64,128]{2,1,0:T(8,128)S(1)}, bf16[40,64,128]{2,1,0:T(8,128)(2,1)S(1)}, bf16[64,864]{1,0:T(8,128)(2,1)S(1)}, bf16[3,128,256]{2,1,0:T(8,128)(2,1)S(1)}) custom-call(bf16[32,4,80,256]{3,2,1,0:T(8,128)(2,1)} %volume.3, bf16[3,3,3,32,64]{4,3,2,1,0:T(8,128)(2,1)S(1)} %copy-done.1, ...), custom_call_target="tpu_custom_call" | custom-call | flops 5000000000 | bytes 10485760 | tf_op jit(solution)/shard_map/pallas_call | solution.py:389
  9.6 6.4 %shard_map.68 = (bf16[41,128,128]{2,1,0:T(8,128)(2,1)S(1)}, f32[592,128]{1,0:T(8,128)S(1)}) custom-call(bf16[32,4,80,256]{3,2,1,0:T(8,128)(2,1)} %volume.3, bf16[2,81,96,128]{3,2,1,0:T(8,128)(2,1)S(1)} %get-tuple-element.35.lines, bf16[64,864]{1,0:T(8,128)(2,1)S(1)} %get-tuple-element.36.full, f32[1,64]{1,0:T(1,128)S(1)} %bitcast.4, ...), custom_call_target="tpu_custom_call" | custom-call | flops 6000000000 | bytes 10485760 | tf_op jit(solution)/shard_map/pallas_call | solution.py:409
  16.0 3.0 %shard_map.69.refs_0_ = bf16[32,4,80,256]{3,2,1,0:T(8,128)(2,1)} custom-call(bf16[3,128,256]{2,1,0:T(8,128)(2,1)S(1)} %get-tuple-element.34.refs_0_.refs_1_, bf16[41,128,128]{2,1,0:T(8,128)(2,1)S(1)} %get-tuple-element.37.refs_1_.refs_3_.refs_2_), custom_call_target="tpu_custom_call" | custom-call | flops 1000000 | bytes 1000 | tf_op jit(solution)/shard_map/pallas_call | solution.py:333
  19.1 0.0 collective-permute-done.halo
  19.1 1.8 %shard_map.70 = (bf16[41,128,128]{2,1,0:T(8,128)(2,1)S(1)}, bf16[40,64,128]{2,1,0:T(8,128)(2,1)S(1)}, bf16[81,96,128]{2,1,0:T(8,128)(2,1)S(1)}) custom-call(bf16[32,1,80,256]{3,2,1,0:T(8,128)(2,1)S(1)} %collective-permute-done.halo, f32[40,64,128]{2,1,0:T(8,128)S(1)} %get-tuple-element.39.pre, bf16[40,64,128]{2,1,0:T(8,128)(2,1)S(1)} %get-tuple-element.40.upstream, ...), custom_call_target="tpu_custom_call" | custom-call | flops 3000000000 | bytes 6291456 | tf_op jit(solution)/shard_map/pallas_call | solution.py:429
  20.8 1.5 %collective-permute-start.3 = (bf16[40,64,128]{2,1,0:T(8,128)(2,1)S(1)}, bf16[40,64,128]{2,1,0:T(8,128)(2,1)S(1)}, u32[]{:S(2)}, u32[]{:S(2)}) collective-permute-start(bf16[40,64,128]{2,1,0:T(8,128)(2,1)S(1)} %get-tuple-element.51), channel_id=1, source_target_pairs={{1,0},{2,1},{3,2},{4,3},{5,4},{6,5},{7,6},{8,7},{9,8},{10,9},{11,1... | collective-permute-start | bytes 1966088 | tf_op jit(solution)/shard_map/ppermute | solution.py:376
  22.3 1.8 %shard_map.71 = f32[448,128]{1,0:T(8,128)S(1)} custom-call(bf16[81,96,128]{2,1,0:T(8,128)(2,1)S(1)} %get-tuple-element.41.below, bf16[2,81,96,128]{3,2,1,0:T(8,128)(2,1)S(1)} %get-tuple-element.35.lines, bf16[41,128,128]{2,1,0:T(8,128)(2,1)S(1)} %get-tuple-element.42.grads.refs_2_, f32[592,128]{1,0:T(8,128)S(1)} %get-tuple-element.43.terms_in), custom_call_target="tpu_custom_call" | custom-call | flops 100000000 | bytes 100000 | tf_op jit(solution)/shard_map/pallas_call | solution.py:439
  24.1 3.3 %collective-permute-start.1 = (f32[448,128]{1,0:T(8,128)S(1)}, f32[448,128]{1,0:T(8,128)S(1)}, u32[]{:S(2)}, u32[]{:S(2)}) collective-permute-start(f32[448,128]{1,0:T(8,128)S(1)} %shard_map.71), channel_id=1, source_target_pairs={{0,1},{1,0},{2,3},{3,2},{4,5},{5,4},{6,7},{7,6},{8,9},{9,8},{10,11... | collective-permute-start | bytes 688136 | tf_op jit(solution)/shard_map/ppermute | solution.py:354
  27.4 3.0 %shard_map.72.refs_0_ = bf16[32,4,80,256]{3,2,1,0:T(8,128)(2,1)} custom-call(bf16[32,4,80,256]{3,2,1,0:T(8,128)(2,1)} %shard_map.69.refs_0_, bf16[3,128,256]{2,1,0:T(8,128)(2,1)S(1)} %get-tuple-element.34.refs_0_.refs_1_, bf16[41,128,128]{2,1,0:T(8,128)(2,1)S(1)} %get-tuple-element.42.grads.refs_2_), custom_call_target="tpu_custom_call", output_to_operand_aliasing={{}: (0, {})} | custom-call | flops 1000000 | bytes 1000 | tf_op jit(solution)/shard_map/pallas_call | solution.py:333
  30.4 0.0 collective-permute-done.1
  30.5 2.9 %collective-permute-start.2 = (bf16[448,128]{1,0:T(8,128)(2,1)S(1)}, bf16[448,128]{1,0:T(8,128)(2,1)S(1)}, u32[]{:S(2)}, u32[]{:S(2)}) collective-permute-start(bf16[448,128]{1,0:T(8,128)(2,1)S(1)} %add_convert_fusion.2), channel_id=1, source_target_pairs={{0,2},{1,3},{2,0},{3,1},{4,6},{5,7},{6,4},{7,5},{8,10},{9,11},{10,... | collective-permute-start | bytes 344072 | tf_op jit(solution)/shard_map/ppermute | solution.py:363
  33.4 3.6 %shard_map.73.refs_0_ = bf16[32,4,80,256]{3,2,1,0:T(8,128)(2,1)} custom-call(bf16[32,4,80,256]{3,2,1,0:T(8,128)(2,1)} %shard_map.72.refs_0_, bf16[3,128,256]{2,1,0:T(8,128)(2,1)S(1)} %get-tuple-element.34.refs_0_.refs_1_, bf16[41,128,128]{2,1,0:T(8,128)(2,1)S(1)} %get-tuple-element.42.grads.refs_2_, ...), custom_call_target="tpu_custom_call", output_to_operand_aliasing={{}: (0, {})} | custom-call | flops 1000000 | bytes 1000 | tf_op jit(solution)/shard_map/pallas_call | solution.py:333
  37.0 1.8 %collective-permute-done.2 = bf16[448,128]{1,0:T(8,128)(2,1)S(1)} collective-permute-done((bf16[448,128]{1,0:T(8,128)(2,1)S(1)}, bf16[448,128]{1,0:T(8,128)(2,1)S(1)}, u32[]{:S(2)}, u32[]{:S(2)}) %collective-permute-start.2) | collective-permute-done | bytes 114720 | tf_op jit(solution)/shard_map/ppermute | solution.py:363
  38.8 0.0 collective-permute-done.3.refs_3_
  38.8 1.6 %collective-permute-start.4 = (bf16[448,128]{1,0:T(8,128)(2,1)S(1)}, bf16[448,128]{1,0:T(8,128)(2,1)S(1)}, u32[]{:S(2)}, u32[]{:S(2)}) collective-permute-start(bf16[448,128]{1,0:T(8,128)(2,1)S(1)} %add_convert_fusion.1), channel_id=1, source_target_pairs={{0,4},{1,5},{2,6},{3,7},{4,0},{5,1},{6,2},{7,3},{8,12},{9,13},{10,... | collective-permute-start | bytes 344072 | tf_op jit(solution)/shard_map/ppermute | solution.py:363
  40.4 3.7 %shard_map.74 = bf16[32,4,80,256]{3,2,1,0:T(8,128)(2,1)} custom-call(bf16[32,4,80,256]{3,2,1,0:T(8,128)(2,1)} %shard_map.73.refs_0_, bf16[3,128,256]{2,1,0:T(8,128)(2,1)S(1)} %get-tuple-element.34.refs_0_.refs_1_, bf16[41,128,128]{2,1,0:T(8,128)(2,1)S(1)} %get-tuple-element.37.refs_1_.refs_3_.refs_2_, ...), custom_call_target="tpu_custom_call", output_to_operand_aliasing={{}: (0, {})} | custom-call | flops 1000000 | bytes 1000 | tf_op jit(solution)/shard_map/pallas_call | solution.py:333
  44.1 0.0 collective-permute-done.4
  44.2 2.7 %collective-permute-start.5 = (bf16[448,128]{1,0:T(8,128)(2,1)S(1)}, bf16[448,128]{1,0:T(8,128)(2,1)S(1)}, u32[]{:S(2)}, u32[]{:S(2)}) collective-permute-start(bf16[448,128]{1,0:T(8,128)(2,1)S(1)} %add_convert_fusion.mine), channel_id=1, source_target_pairs={{0,8},{1,9},{2,10},{3,11},{4,12},{5,13},{6,14},{7,15},{8,0},{9,1},... | collective-permute-start | bytes 344072 | tf_op jit(solution)/shard_map/ppermute | solution.py:363
  46.8 5.5 %collective-permute-done.5.got = bf16[448,128]{1,0:T(8,128)(2,1)S(1)} collective-permute-done((bf16[448,128]{1,0:T(8,128)(2,1)S(1)}, bf16[448,128]{1,0:T(8,128)(2,1)S(1)}, u32[]{:S(2)}, u32[]{:S(2)}) %collective-permute-start.5) | collective-permute-done | bytes 114720 | tf_op jit(solution)/shard_map/ppermute | solution.py:363
  52.3 0.9 %shard_map.75 = (f32[3,3,96,64]{3,2,1,0:T(8,128)}, f32[1,64]{1,0:T(1,128)}) custom-call(bf16[448,128]{1,0:T(8,128)(2,1)S(1)} %add_convert_fusion.mine, bf16[448,128]{1,0:T(8,128)(2,1)S(1)} %collective-permute-done.5.got), custom_call_target="tpu_custom_call" | custom-call | tf_op jit(solution)/shard_map/pallas_call | solution.py:459
  (3 shorter events, 0.1 us)
Async XLA Ops:
  0.6 4.0 %copy-start = (bf16[64,2,40,128]{3,2,1,0:T(8,128)(2,1)S(1)}, bf16[64,2,40,128]{3,2,1,0:T(8,128)(2,1)}, u32[]{:S(2)}) copy-start(bf16[64,2,40,128]{3,2,1,0:T(8,128)(2,1)} %upstream.3) | copy-start | bytes 3932164
  0.6 4.0 %copy-start.2 = (f32[64]{0:T(128)S(1)}, f32[64]{0:T(128)}, u32[]{:S(2)}) copy-start(f32[64]{0:T(128)} %param.6) | copy-start | bytes 772
  0.7 4.0 %copy-start.1 = (bf16[3,3,3,32,64]{4,3,2,1,0:T(8,128)(2,1)S(1)}, bf16[3,3,3,32,64]{4,3,2,1,0:T(8,128)(2,1)}, u32[]{:S(2)}) copy-start(bf16[3,3,3,32,64]{4,3,2,1,0:T(8,128)(2,1)} %weights_in.1) | copy-start | bytes 331780
  2.2 16.9 %collective-permute-start = (bf16[32,1,80,256]{3,2,1,0:T(8,128)(2,1)S(1)}, bf16[32,1,80,256]{3,2,1,0:T(8,128)(2,1)S(1)}, u32[]{:S(2)}, u32[]{:S(2)}) collective-permute-start(bf16[32,1,80,256]{3,2,1,0:T(8,128)(2,1)S(1)} %slice.3), channel_id=1, source_target_pairs={{0,1},{1,2},{2,3},{3,4},{4,5},{5,6},{6,7},{7,8},{8,9},{9,10},{10,1... | collective-permute-start | bytes 3932168 | tf_op jit(solution)/shard_map/ppermute | solution.py:376
  20.8 17.9 %collective-permute-start.3 = (bf16[40,64,128]{2,1,0:T(8,128)(2,1)S(1)}, bf16[40,64,128]{2,1,0:T(8,128)(2,1)S(1)}, u32[]{:S(2)}, u32[]{:S(2)}) collective-permute-start(bf16[40,64,128]{2,1,0:T(8,128)(2,1)S(1)} %get-tuple-element.51), channel_id=1, source_target_pairs={{1,0},{2,1},{3,2},{4,3},{5,4},{6,5},{7,6},{8,7},{9,8},{10,9},{11,1... | collective-permute-start | bytes 1966088 | tf_op jit(solution)/shard_map/ppermute | solution.py:376
  24.1 6.3 %collective-permute-start.1 = (f32[448,128]{1,0:T(8,128)S(1)}, f32[448,128]{1,0:T(8,128)S(1)}, u32[]{:S(2)}, u32[]{:S(2)}) collective-permute-start(f32[448,128]{1,0:T(8,128)S(1)} %shard_map.71), channel_id=1, source_target_pairs={{0,1},{1,0},{2,3},{3,2},{4,5},{5,4},{6,7},{7,6},{8,9},{9,8},{10,11... | collective-permute-start | bytes 688136 | tf_op jit(solution)/shard_map/ppermute | solution.py:354
  30.5 8.3 %collective-permute-start.2 = (bf16[448,128]{1,0:T(8,128)(2,1)S(1)}, bf16[448,128]{1,0:T(8,128)(2,1)S(1)}, u32[]{:S(2)}, u32[]{:S(2)}) collective-permute-start(bf16[448,128]{1,0:T(8,128)(2,1)S(1)} %add_convert_fusion.2), channel_id=1, source_target_pairs={{0,2},{1,3},{2,0},{3,1},{4,6},{5,7},{6,4},{7,5},{8,10},{9,11},{10,... | collective-permute-start | bytes 344072 | tf_op jit(solution)/shard_map/ppermute | solution.py:363
  38.8 5.3 %collective-permute-start.4 = (bf16[448,128]{1,0:T(8,128)(2,1)S(1)}, bf16[448,128]{1,0:T(8,128)(2,1)S(1)}, u32[]{:S(2)}, u32[]{:S(2)}) collective-permute-start(bf16[448,128]{1,0:T(8,128)(2,1)S(1)} %add_convert_fusion.1), channel_id=1, source_target_pairs={{0,4},{1,5},{2,6},{3,7},{4,0},{5,1},{6,2},{7,3},{8,12},{9,13},{10,... | collective-permute-start | bytes 344072 | tf_op jit(solution)/shard_map/ppermute | solution.py:363
  44.2 8.2 %collective-permute-start.5 = (bf16[448,128]{1,0:T(8,128)(2,1)S(1)}, bf16[448,128]{1,0:T(8,128)(2,1)S(1)}, u32[]{:S(2)}, u32[]{:S(2)}) collective-permute-start(bf16[448,128]{1,0:T(8,128)(2,1)S(1)} %add_convert_fusion.mine), channel_id=1, source_target_pairs={{0,8},{1,9},{2,10},{3,11},{4,12},{5,13},{6,14},{7,15},{8,0},{9,1},... | collective-permute-start | bytes 344072 | tf_op jit(solution)/shard_map/ppermute | solution.py:363

commit v5 on v4

--- a/solution.py
+++ b/solution.py
@@ -231,9 +231,14 @@
     grads[ny] = jnp.zeros(grads.shape[1:], BF)
 
 
-def terms_kernel(below, lines, grads, terms_in, packed):
+def terms_kernel(below, lines, grads, terms_in, kept, sent, packed):
+    place = lax.axis_index("slab")
     terms = terms_in[...] + plane_terms([below, lines.at[0], lines.at[1]], grads)
-    pack(terms, packed, below.shape[1], grads.shape[1] // 2, lax.axis_index("slab"))
+    pack(terms, packed, below.shape[1], grads.shape[1] // 2, place)
+    rows = kept.shape[0]
+    low, high = packed[:rows], packed[rows:]
+    kept[...] = jnp.where(place % 2 == 0, low, high)
+    sent[...] = jnp.where(place % 2 == 0, high, low)
 
 
 def pack(terms, packed, count, cout, place):
@@ -253,7 +258,10 @@
 
 
 def finish_kernel(mine, got, weight_grad, bias_grad):
-    packed = mine[...].astype(F32) + got[...].astype(F32)
+    even = lax.axis_index("slab") % 2 == 0
+    low = jnp.where(even, mine[...], got[...])
+    high = jnp.where(even, got[...], mine[...])
+    packed = jnp.concatenate([low, high], 0)
     count = weight_grad.shape[2]
     cout = weight_grad.shape[3]
     for a in range(3):
@@ -347,27 +355,27 @@
     )(*args)
 
 
-def all_sum(value, axis, total, above, works):
+def all_sum(kept, sent, axis, total, above, works):
     peers = lax.axis_size(axis)
     works = list(works)
-    value, total = lax.optimization_barrier((value, total))
-    got = lax.ppermute(value, axis, [(i, i ^ 1) for i in range(peers)])
+    swap = [(i, i ^ 1) for i in range(peers)]
+    kept, sent, total = lax.optimization_barrier((kept, sent, total))
+    got = lax.ppermute(sent, axis, swap)
     total, above = works.pop(0)(total, above)
     got, total = lax.optimization_barrier((got, total))
+    value = kept + got
     step = 2
     while step < peers:
-        sent, total = lax.optimization_barrier(
-            ((value.astype(F32) + got.astype(F32)).astype(BF), total)
-        )
-        value = sent
-        got = lax.ppermute(sent, axis, [(i, i ^ step) for i in range(peers)])
+        value, total = lax.optimization_barrier((value.astype((BF if 2 * step == peers else F32)), total))
+        got = lax.ppermute(value, axis, [(i, i ^ step) for i in range(peers)])
         if works:
             total, above = works.pop(0)(total, above)
         got, total, above = lax.optimization_barrier((got, total, above))
+        value = value.astype(F32) + got.astype(F32)
         step *= 2
     for work in works:
         total, above = work(total, above)
-    return value, got, total
+    return value, lax.ppermute(value, axis, swap), total
 
 
 def shifted(x, axis, by):
@@ -436,17 +444,20 @@
     )(halo, pre, late, taps)
     slots = (lax.axis_size("slab") + 15) // 16 * 16
     above = shifted(raw, "slab", -1)
-    packed = pl.pallas_call(
+    packed_rows = 9 * count // 2 + slots
+    kept, sent = pl.pallas_call(
         terms_kernel,
         in_specs=[VMEM] * 4,
-        out_specs=VMEM,
-        out_shape=shape(9 * count // 2 + slots, 2 * cout, dtype=F32),
+        out_specs=[VMEM] * 2,
+        out_shape=[shape(packed_rows // 2, 2 * cout, dtype=F32)] * 2,
+        scratch_shapes=[pltpu.VMEM((packed_rows, 2 * cout), F32)],
         compiler_params=PARAMS,
         cost_estimate=cost(10**8, 10**5),
     )(below, lines, lower, terms)
 
-    packed, got, total = all_sum(
-        packed,
+    mine, got, total = all_sum(
+        kept,
+        sent,
         "slab",
         total,
         above,
@@ -462,7 +473,7 @@
         out_specs=[VMEM] * 2,
         out_shape=[shape(3, 3, count, cout, dtype=F32), shape(1, cout, dtype=F32)],
         compiler_params=PARAMS,
-    )(packed, got)
+    )(mine, got)
     return (
         total,
         weight_grad.reshape(3, 3, 3, cin, cout),

time: 53.4 us -> 51.8 us (0.970)
  waiting for transfers between devices: 7.3 us -> 5.6 us
    ppermute x4 -> x5, waiting for transfers between devices: 7.29 us -> 5.6 us  [the longest x3 4.28 us: all_sum(): got = lax.ppermute(value, axis, [(i, i ^ step) for i in range(peers)])]
    ppermute x4 -> x5, starting transfers between devices: 10.5 us -> 10.6 us  [the longest x3 7.23 us: all_sum(): got = lax.ppermute(value, axis, [(i, i ^ step) for i in range(peers)])]
  transfers between devices with their start and end apart: 6 -> 7, of which waited for: 2 -> 3; matrix products, arithmetic and copies ran while one was open for 0% -> 0% of each run, Pallas kernels for 50% -> 51%
where the time goes in v5:
time: 51.8 us; the launch traced here: 51.6 us
  Pallas kernels  29 us (56%)
  starting transfers between devices  14.5 us (28%)
  waiting for transfers between devices  5.6 us (11%)
  local copies, waits for them, and re-layouts  1.54 us (3%)
  between operations  0.81 us (2%)
    pallas_call x4, Pallas kernels, back_plane(): pl.pallas_call(functools.partial(back_kernel, z, len(above) > 0, fresh, a...  13.2 us
    ppermute x3, starting transfers between devices, all_sum(): got = lax.ppermute(value, axis, [(i, i ^ step) for i in range(peers)])  7.23 us
    pallas_call x1, Pallas kernels, shards(): pl.pallas_call(upper_kernel, in_specs=[ANY, VMEM, VMEM, VMEM, ANY], out_s...  6.45 us
    pallas_call x1, Pallas kernels, shards(): pl.pallas_call(lower_kernel, in_specs=[ANY, ANY, VMEM, ANY], out_specs=[V...  4.92 us
    ppermute x3, waiting for transfers between devices, all_sum(): got = lax.ppermute(value, axis, [(i, i ^ step) for i in range(peers)])  4.28 us
    ppermute x2, starting transfers between devices, shifted(): return lax.ppermute(x, axis, pairs)  3.91 us
    ppermute x1, starting transfers between devices, all_sum(): got = lax.ppermute(sent, axis, swap)  3.31 us
    pallas_call x1, Pallas kernels, shards(): pl.pallas_call(terms_kernel, in_specs=[VMEM] * 4, out_specs=[VMEM] * 2, o...  1.81 us
  transfers between devices with their start and end apart: 7, of which 3 were waited for; matrix products, arithmetic and copies ran while one was open for 0% of the time, Pallas kernels for 51%

profile of v5, /device:TPU:0, one launch (start us, length us, event | category | flops | bytes accessed | tf_op | source)
XLA Modules:
  0.0 51.6 jit_solution(16596833791364583625)
XLA Ops:
  0.6 0.0 copy-start
  0.6 0.0 copy-start.2
  0.7 0.0 copy-start.1
  0.7 1.5 %slice.3 = bf16[32,1,80,256]{3,2,1,0:T(8,128)(2,1)S(1)} slice(bf16[32,4,80,256]{3,2,1,0:T(8,128)(2,1)} %volume.3), slice={[0:32], [3:4], [0:80], [0:256]} | slice | bytes 2621440 | tf_op jit(solution)/shard_map/slice | solution.py:392
  2.2 2.4 %collective-permute-start = (bf16[32,1,80,256]{3,2,1,0:T(8,128)(2,1)S(1)}, bf16[32,1,80,256]{3,2,1,0:T(8,128)(2,1)S(1)}, u32[]{:S(2)}, u32[]{:S(2)}) collective-permute-start(bf16[32,1,80,256]{3,2,1,0:T(8,128)(2,1)S(1)} %slice.3), channel_id=1, source_target_pairs={{0,1},{1,2},{2,3},{3,4},{4,5},{5,6},{6,7},{7,8},{8,9},{9,10},{10,1... | collective-permute-start | bytes 3932168 | tf_op jit(solution)/shard_map/ppermute | solution.py:384
  4.6 0.0 copy-done
  4.6 0.0 copy-done.2
  4.7 0.0 copy-done.1
  4.7 4.9 %shard_map.67 = (bf16[2,81,96,128]{3,2,1,0:T(8,128)(2,1)S(1)}, f32[40,64,128]{2,1,0:T(8,128)S(1)}, bf16[40,64,128]{2,1,0:T(8,128)(2,1)S(1)}, bf16[64,864]{1,0:T(8,128)(2,1)S(1)}, bf16[3,128,256]{2,1,0:T(8,128)(2,1)S(1)}) custom-call(bf16[32,4,80,256]{3,2,1,0:T(8,128)(2,1)} %volume.3, bf16[3,3,3,32,64]{4,3,2,1,0:T(8,128)(2,1)S(1)} %copy-done.1, ...), custom_call_target="tpu_custom_call" | custom-call | flops 5000000000 | bytes 10485760 | tf_op jit(solution)/shard_map/pallas_call | solution.py:397
  9.6 6.4 %shard_map.68 = (bf16[41,128,128]{2,1,0:T(8,128)(2,1)S(1)}, f32[592,128]{1,0:T(8,128)S(1)}) custom-call(bf16[32,4,80,256]{3,2,1,0:T(8,128)(2,1)} %volume.3, bf16[2,81,96,128]{3,2,1,0:T(8,128)(2,1)S(1)} %get-tuple-element.38.lines, bf16[64,864]{1,0:T(8,128)(2,1)S(1)} %get-tuple-element.39.full, f32[1,64]{1,0:T(1,128)S(1)} %bitcast.4, ...), custom_call_target="tpu_custom_call" | custom-call | flops 6000000000 | bytes 10485760 | tf_op jit(solution)/shard_map/pallas_call | solution.py:417
  16.0 3.0 %shard_map.69.refs_0_ = bf16[32,4,80,256]{3,2,1,0:T(8,128)(2,1)} custom-call(bf16[3,128,256]{2,1,0:T(8,128)(2,1)S(1)} %get-tuple-element.37.refs_0_.refs_1_, bf16[41,128,128]{2,1,0:T(8,128)(2,1)S(1)} %get-tuple-element.40.refs_1_.refs_3_.refs_2_), custom_call_target="tpu_custom_call" | custom-call | flops 1000000 | bytes 1000 | tf_op jit(solution)/shard_map/pallas_call | solution.py:341
  19.1 0.0 collective-permute-done.halo
  19.1 1.8 %shard_map.70 = (bf16[41,128,128]{2,1,0:T(8,128)(2,1)S(1)}, bf16[40,64,128]{2,1,0:T(8,128)(2,1)S(1)}, bf16[81,96,128]{2,1,0:T(8,128)(2,1)S(1)}) custom-call(bf16[32,1,80,256]{3,2,1,0:T(8,128)(2,1)S(1)} %collective-permute-done.halo, f32[40,64,128]{2,1,0:T(8,128)S(1)} %get-tuple-element.42.pre, bf16[40,64,128]{2,1,0:T(8,128)(2,1)S(1)} %get-tuple-element.43.upstream, ...), custom_call_target="tpu_custom_call" | custom-call | flops 3000000000 | bytes 6291456 | tf_op jit(solution)/shard_map/pallas_call | solution.py:437
  20.8 1.5 %collective-permute-start.3 = (bf16[40,64,128]{2,1,0:T(8,128)(2,1)S(1)}, bf16[40,64,128]{2,1,0:T(8,128)(2,1)S(1)}, u32[]{:S(2)}, u32[]{:S(2)}) collective-permute-start(bf16[40,64,128]{2,1,0:T(8,128)(2,1)S(1)} %get-tuple-element.57), channel_id=1, source_target_pairs={{1,0},{2,1},{3,2},{4,3},{5,4},{6,5},{7,6},{8,7},{9,8},{10,9},{11,1... | collective-permute-start | bytes 1966088 | tf_op jit(solution)/shard_map/ppermute | solution.py:384
  22.3 1.8 %shard_map.71 = (f32[224,128]{1,0:T(8,128)S(1)}, f32[224,128]{1,0:T(8,128)S(1)}) custom-call(bf16[81,96,128]{2,1,0:T(8,128)(2,1)S(1)} %get-tuple-element.44.below, bf16[2,81,96,128]{3,2,1,0:T(8,128)(2,1)S(1)} %get-tuple-element.38.lines, bf16[41,128,128]{2,1,0:T(8,128)(2,1)S(1)} %get-tuple-element.45.grads.refs_2_, f32[592,128]{1,0:T(8,128)S(1)} %get-tuple-element.46.terms_in), custom_call_target="tpu_custom_call" | custom-call | flops 100000000 | bytes 100000 | tf_op jit(solution)/shard_map/pallas_call | solution.py:448
  24.1 3.3 %collective-permute-start.1 = (f32[224,128]{1,0:T(8,128)S(1)}, f32[224,128]{1,0:T(8,128)S(1)}, u32[]{:S(2)}, u32[]{:S(2)}) collective-permute-start(f32[224,128]{1,0:T(8,128)S(1)} %get-tuple-element.51), channel_id=1, source_target_pairs={{0,1},{1,0},{2,3},{3,2},{4,5},{5,4},{6,7},{7,6},{8,9},{9,8},{10,11... | collective-permute-start | bytes 344072 | tf_op jit(solution)/shard_map/ppermute | solution.py:363
  27.4 3.0 %shard_map.72.refs_0_ = bf16[32,4,80,256]{3,2,1,0:T(8,128)(2,1)} custom-call(bf16[32,4,80,256]{3,2,1,0:T(8,128)(2,1)} %shard_map.69.refs_0_, bf16[3,128,256]{2,1,0:T(8,128)(2,1)S(1)} %get-tuple-element.37.refs_0_.refs_1_, bf16[41,128,128]{2,1,0:T(8,128)(2,1)S(1)} %get-tuple-element.45.grads.refs_2_), custom_call_target="tpu_custom_call", output_to_operand_aliasing={{}: (0, {})} | custom-call | flops 1000000 | bytes 1000 | tf_op jit(solution)/shard_map/pallas_call | solution.py:341
  30.4 0.0 collective-permute-done.1
  30.5 2.9 %collective-permute-start.2 = (f32[224,128]{1,0:T(8,128)S(1)}, f32[224,128]{1,0:T(8,128)S(1)}, u32[]{:S(2)}, u32[]{:S(2)}) collective-permute-start(f32[224,128]{1,0:T(8,128)S(1)} %add.12), channel_id=1, source_target_pairs={{0,2},{1,3},{2,0},{3,1},{4,6},{5,7},{6,4},{7,5},{8,10},{9,11},{10,... | collective-permute-start | bytes 344072 | tf_op jit(solution)/shard_map/ppermute | solution.py:370
  33.4 3.5 %shard_map.73.refs_0_ = bf16[32,4,80,256]{3,2,1,0:T(8,128)(2,1)} custom-call(bf16[32,4,80,256]{3,2,1,0:T(8,128)(2,1)} %shard_map.72.refs_0_, bf16[3,128,256]{2,1,0:T(8,128)(2,1)S(1)} %get-tuple-element.37.refs_0_.refs_1_, bf16[41,128,128]{2,1,0:T(8,128)(2,1)S(1)} %get-tuple-element.45.grads.refs_2_, ...), custom_call_target="tpu_custom_call", output_to_operand_aliasing={{}: (0, {})} | custom-call | flops 1000000 | bytes 1000 | tf_op jit(solution)/shard_map/pallas_call | solution.py:341
  37.0 1.8 %collective-permute-done.2 = f32[224,128]{1,0:T(8,128)S(1)} collective-permute-done((f32[224,128]{1,0:T(8,128)S(1)}, f32[224,128]{1,0:T(8,128)S(1)}, u32[]{:S(2)}, u32[]{:S(2)}) %collective-permute-start.2) | collective-permute-done | bytes 114720 | tf_op jit(solution)/shard_map/ppermute | solution.py:370
  38.8 0.0 collective-permute-done.3.refs_3_
  38.8 1.6 %collective-permute-start.4 = (f32[224,128]{1,0:T(8,128)S(1)}, f32[224,128]{1,0:T(8,128)S(1)}, u32[]{:S(2)}, u32[]{:S(2)}) collective-permute-start(f32[224,128]{1,0:T(8,128)S(1)} %add.13), channel_id=1, source_target_pairs={{0,4},{1,5},{2,6},{3,7},{4,0},{5,1},{6,2},{7,3},{8,12},{9,13},{10,... | collective-permute-start | bytes 344072 | tf_op jit(solution)/shard_map/ppermute | solution.py:370
  40.4 3.7 %shard_map.74 = bf16[32,4,80,256]{3,2,1,0:T(8,128)(2,1)} custom-call(bf16[32,4,80,256]{3,2,1,0:T(8,128)(2,1)} %shard_map.73.refs_0_, bf16[3,128,256]{2,1,0:T(8,128)(2,1)S(1)} %get-tuple-element.37.refs_0_.refs_1_, bf16[41,128,128]{2,1,0:T(8,128)(2,1)S(1)} %get-tuple-element.40.refs_1_.refs_3_.refs_2_, ...), custom_call_target="tpu_custom_call", output_to_operand_aliasing={{}: (0, {})} | custom-call | flops 1000000 | bytes 1000 | tf_op jit(solution)/shard_map/pallas_call | solution.py:341
  44.1 0.0 collective-permute-done.4
  44.1 2.7 %collective-permute-start.5 = (bf16[224,128]{1,0:T(8,128)(2,1)S(1)}, bf16[224,128]{1,0:T(8,128)(2,1)S(1)}, u32[]{:S(2)}, u32[]{:S(2)}) collective-permute-start(bf16[224,128]{1,0:T(8,128)(2,1)S(1)} %add_convert_fusion), channel_id=1, source_target_pairs={{0,8},{1,9},{2,10},{3,11},{4,12},{5,13},{6,14},{7,15},{8,0},{9,1},... | collective-permute-start | bytes 172040 | tf_op jit(solution)/shard_map/ppermute | solution.py:370
  46.8 2.5 %collective-permute-done.5 = bf16[224,128]{1,0:T(8,128)(2,1)S(1)} collective-permute-done((bf16[224,128]{1,0:T(8,128)(2,1)S(1)}, bf16[224,128]{1,0:T(8,128)(2,1)S(1)}, u32[]{:S(2)}, u32[]{:S(2)}) %collective-permute-start.5) | collective-permute-done | bytes 57376 | tf_op jit(solution)/shard_map/ppermute | solution.py:370
  49.3 0.1 collective-permute-start.6
  49.4 1.3 %collective-permute-done.6.got = f32[224,128]{1,0:T(8,128)S(1)} collective-permute-done((f32[224,128]{1,0:T(8,128)S(1)}, f32[224,128]{1,0:T(8,128)S(1)}, u32[]{:S(2)}, u32[]{:S(2)}) %collective-permute-start.6) | collective-permute-done | bytes 114720 | tf_op jit(solution)/shard_map/ppermute | solution.py:378
  50.7 0.9 %shard_map.75 = (f32[3,3,96,64]{3,2,1,0:T(8,128)}, f32[1,64]{1,0:T(1,128)}) custom-call(f32[224,128]{1,0:T(8,128)S(1)} %convert_add_fusion.mine, f32[224,128]{1,0:T(8,128)S(1)} %collective-permute-done.6.got), custom_call_target="tpu_custom_call" | custom-call | tf_op jit(solution)/shard_map/pallas_call | solution.py:470
  (4 shorter events, 0.1 us)
Async XLA Ops:
  0.6 4.0 %copy-start = (bf16[64,2,40,128]{3,2,1,0:T(8,128)(2,1)S(1)}, bf16[64,2,40,128]{3,2,1,0:T(8,128)(2,1)}, u32[]{:S(2)}) copy-start(bf16[64,2,40,128]{3,2,1,0:T(8,128)(2,1)} %upstream.3) | copy-start | bytes 3932164
  0.6 4.0 %copy-start.2 = (f32[64]{0:T(128)S(1)}, f32[64]{0:T(128)}, u32[]{:S(2)}) copy-start(f32[64]{0:T(128)} %param.6) | copy-start | bytes 772
  0.7 4.0 %copy-start.1 = (bf16[3,3,3,32,64]{4,3,2,1,0:T(8,128)(2,1)S(1)}, bf16[3,3,3,32,64]{4,3,2,1,0:T(8,128)(2,1)}, u32[]{:S(2)}) copy-start(bf16[3,3,3,32,64]{4,3,2,1,0:T(8,128)(2,1)} %weights_in.1) | copy-start | bytes 331780
  2.2 16.9 %collective-permute-start = (bf16[32,1,80,256]{3,2,1,0:T(8,128)(2,1)S(1)}, bf16[32,1,80,256]{3,2,1,0:T(8,128)(2,1)S(1)}, u32[]{:S(2)}, u32[]{:S(2)}) collective-permute-start(bf16[32,1,80,256]{3,2,1,0:T(8,128)(2,1)S(1)} %slice.3), channel_id=1, source_target_pairs={{0,1},{1,2},{2,3},{3,4},{4,5},{5,6},{6,7},{7,8},{8,9},{9,10},{10,1... | collective-permute-start | bytes 3932168 | tf_op jit(solution)/shard_map/ppermute | solution.py:384
  20.8 17.9 %collective-permute-start.3 = (bf16[40,64,128]{2,1,0:T(8,128)(2,1)S(1)}, bf16[40,64,128]{2,1,0:T(8,128)(2,1)S(1)}, u32[]{:S(2)}, u32[]{:S(2)}) collective-permute-start(bf16[40,64,128]{2,1,0:T(8,128)(2,1)S(1)} %get-tuple-element.57), channel_id=1, source_target_pairs={{1,0},{2,1},{3,2},{4,3},{5,4},{6,5},{7,6},{8,7},{9,8},{10,9},{11,1... | collective-permute-start | bytes 1966088 | tf_op jit(solution)/shard_map/ppermute | solution.py:384
  24.1 6.3 %collective-permute-start.1 = (f32[224,128]{1,0:T(8,128)S(1)}, f32[224,128]{1,0:T(8,128)S(1)}, u32[]{:S(2)}, u32[]{:S(2)}) collective-permute-start(f32[224,128]{1,0:T(8,128)S(1)} %get-tuple-element.51), channel_id=1, source_target_pairs={{0,1},{1,0},{2,3},{3,2},{4,5},{5,4},{6,7},{7,6},{8,9},{9,8},{10,11... | collective-permute-start | bytes 344072 | tf_op jit(solution)/shard_map/ppermute | solution.py:363
  30.5 8.3 %collective-permute-start.2 = (f32[224,128]{1,0:T(8,128)S(1)}, f32[224,128]{1,0:T(8,128)S(1)}, u32[]{:S(2)}, u32[]{:S(2)}) collective-permute-start(f32[224,128]{1,0:T(8,128)S(1)} %add.12), channel_id=1, source_target_pairs={{0,2},{1,3},{2,0},{3,1},{4,6},{5,7},{6,4},{7,5},{8,10},{9,11},{10,... | collective-permute-start | bytes 344072 | tf_op jit(solution)/shard_map/ppermute | solution.py:370
  38.8 5.3 %collective-permute-start.4 = (f32[224,128]{1,0:T(8,128)S(1)}, f32[224,128]{1,0:T(8,128)S(1)}, u32[]{:S(2)}, u32[]{:S(2)}) collective-permute-start(f32[224,128]{1,0:T(8,128)S(1)} %add.13), channel_id=1, source_target_pairs={{0,4},{1,5},{2,6},{3,7},{4,0},{5,1},{6,2},{7,3},{8,12},{9,13},{10,... | collective-permute-start | bytes 344072 | tf_op jit(solution)/shard_map/ppermute | solution.py:370
  44.1 5.1 %collective-permute-start.5 = (bf16[224,128]{1,0:T(8,128)(2,1)S(1)}, bf16[224,128]{1,0:T(8,128)(2,1)S(1)}, u32[]{:S(2)}, u32[]{:S(2)}) collective-permute-start(bf16[224,128]{1,0:T(8,128)(2,1)S(1)} %add_convert_fusion), channel_id=1, source_target_pairs={{0,8},{1,9},{2,10},{3,11},{4,12},{5,13},{6,14},{7,15},{8,0},{9,1},... | collective-permute-start | bytes 172040 | tf_op jit(solution)/shard_map/ppermute | solution.py:370
  49.3 1.4 %collective-permute-start.6 = (f32[224,128]{1,0:T(8,128)S(1)}, f32[224,128]{1,0:T(8,128)S(1)}, u32[]{:S(2)}, u32[]{:S(2)}) collective-permute-start(f32[224,128]{1,0:T(8,128)S(1)} %convert_add_fusion.mine), channel_id=1, source_target_pairs={{0,1},{1,0},{2,3},{3,2},{4,5},{5,4},{6,7},{7,6},{8,9},{9,8},{10,11... | collective-permute-start | bytes 344072 | tf_op jit(solution)/shard_map/ppermute | solution.py:378

commit v6 on v5

--- a/solution.py
+++ b/solution.py
@@ -116,6 +116,14 @@
 
 def spans(total, size):
     return [(at, min(at + size, total)) for at in range(0, total, size)]
+
+
+def edge_kernel(volume, edge, semaphores):
+    copies = Copies(semaphores)
+    top = volume.shape[1] - 1
+    for lo, hi in spans(volume.shape[0], volume.shape[0] // 4):
+        copies.start(volume.at[lo:hi, top], edge.at[lo:hi, 0])
+    copies.wait()
 
 
 def column(bias):
@@ -279,20 +287,13 @@
 
 def back_kernel(z, odd, fresh, aliased, *refs):
     refs = refs[1:] if aliased else refs
-    back, grads_in = refs[:2]
+    back, grads = refs[:2]
     above_in = refs[2 : 2 + odd]
-    refs = refs[2 + len(above_in) :]
-    total, grads, above, plane, semaphores = refs[:5]
+    total, plane, shifted_above, semaphores = refs[2 + len(above_in) :]
     ny = grads.shape[0] - 1
     cout = grads.shape[1] // 2
     copies = Copies(semaphores)
-    loads = []
-    for lo, hi in spans(ny, 8):
-        top = ny + 1 if hi == ny else hi
-        part = [copies.start(grads_in.at[lo:top], grads.at[lo:top])]
-        if odd and not fresh:
-            part.append(copies.start(above_in[0].at[lo:top], above.at[lo:top]))
-        loads.append(part)
+    above = shifted_above if fresh else above_in[0] if odd else None
     if fresh:
         for j in range(ny):
             value = above_in[0][j]
@@ -303,10 +304,7 @@
     cin = plane.shape[0]
     half = plane.shape[2] // 2
     table = picks(half, True)
-    copies.wait(*loads[0])
-    for n, (lo, hi) in enumerate(spans(ny, 8)):
-        if n + 1 < len(loads):
-            copies.wait(*loads[n + 1])
+    for lo, hi in spans(ny, 8):
         columns = []
         for j in range(lo, hi):
             parts = [grads[j : j + 2].reshape(-1, half)]
@@ -333,7 +331,7 @@
     cin, depth, height, width = full
     fresh = len(above) > 0 and above[0].shape != grads.shape
     args = [back, grads, *above]
-    specs = [VMEM, ANY] + [VMEM if fresh else ANY] * len(above)
+    specs = [VMEM] * len(args)
     aliased = total is not None
     if aliased:
         args = [total] + args
@@ -344,10 +342,9 @@
         out_specs=ANY,
         out_shape=shape(*full),
         scratch_shapes=[
-            pltpu.VMEM(grads.shape, BF),
-            pltpu.VMEM(grads.shape if above else (16, 128), BF),
             pltpu.VMEM((cin, height, width), BF),
-            pltpu.SemaphoreType.DMA((3 * (height // 16),)),
+            pltpu.VMEM(grads.shape if fresh else (16, 128), BF),
+            pltpu.SemaphoreType.DMA((height // 16,)),
         ],
         input_output_aliases={0: 0} if aliased else {},
         compiler_params=PARAMS,
@@ -389,11 +386,20 @@
     cout = bias.shape[0]
     ny, half = height // 2, width // 2
     rows, count = height + 1, 3 * cin
-    halo = shifted(volume[:, depth - 1 :], "slab", 1)
+    pinned = pltpu.with_memory_space_constraint(volume, pltpu.HBM)
+    edge = pl.pallas_call(
+        edge_kernel,
+        in_specs=[ANY],
+        out_specs=VMEM,
+        out_shape=shape(cin, 1, height, width),
+        scratch_shapes=[pltpu.SemaphoreType.DMA((4,))],
+        compiler_params=PARAMS,
+        cost_estimate=cost(0, 3 * 2**20),
+    )(pinned)
+    halo = shifted(edge, "slab", 1)
     grads_shape = (ny + 1, 2 * cout, half)
     terms_shape = (6 * count + 16, 2 * cout)
     bias = bias.reshape(1, cout)
-    pinned = pltpu.with_memory_space_constraint(volume, pltpu.HBM)
     lines, pre, late, taps, back = pl.pallas_call(
         lower_kernel,
         in_specs=[ANY, ANY, VMEM, ANY],

time: 51.8 us -> 51.5 us (level)
  waiting for transfers between devices: 5.6 us -> 8.66 us
  Pallas kernels: 29 us -> 26.2 us
  local copies, waits for them, and re-layouts: 1.54 us -> 0.01 us
  starting transfers between devices: 14.5 us -> 15.5 us
    pallas_call x4, Pallas kernels: 13.2 us -> 8.92 us  [back_plane(): pl.pallas_call(functools.partial(back_kernel, z, len(above) > 0, fresh, a...]
    ppermute x3, waiting for transfers between devices: 4.28 us -> 7.34 us  [all_sum(): got = lax.ppermute(value, axis, [(i, i ^ step) for i in range(peers)])]
    slice x1 -> x0, local copies, waits for them, and re-layouts: 1.52 us -> none  [shards(): halo = shifted(volume[:, depth - 1:], 'slab', 1)]
    pallas_call x0 -> x1, Pallas kernels: none -> 1.42 us  [shards(): pl.pallas_call(edge_kernel, in_specs=[ANY], out_specs=VMEM, out_shape=sha...]
    ppermute x1, starting transfers between devices: 3.31 us -> 4.31 us  [all_sum(): got = lax.ppermute(sent, axis, swap)]
  transfers between devices with their start and end apart: 7 -> 7, of which waited for: 3 -> 4; matrix products, arithmetic and copies ran while one was open for 0% -> 0% of each run, Pallas kernels for 51% -> 43%
where the time goes in v6:
time: 51.5 us; the launch traced here: 51.2 us
  Pallas kernels  26.2 us (51%)
  starting transfers between devices  15.5 us (30%)
  waiting for transfers between devices  8.66 us (17%)
  between operations  0.8 us (2%)
    pallas_call x4, Pallas kernels, back_plane(): pl.pallas_call(functools.partial(back_kernel, z, len(above) > 0, fresh, a...  8.92 us
    ppermute x3, waiting for transfers between devices, all_sum(): got = lax.ppermute(value, axis, [(i, i ^ step) for i in range(peers)])  7.34 us
    ppermute x3, starting transfers between devices, all_sum(): got = lax.ppermute(value, axis, [(i, i ^ step) for i in range(peers)])  7.23 us
    pallas_call x1, Pallas kernels, shards(): pl.pallas_call(upper_kernel, in_specs=[ANY, VMEM, VMEM, VMEM, ANY], out_s...  6.45 us
    pallas_call x1, Pallas kernels, shards(): pl.pallas_call(lower_kernel, in_specs=[ANY, ANY, VMEM, ANY], out_specs=[V...  4.92 us
    ppermute x1, starting transfers between devices, all_sum(): got = lax.ppermute(sent, axis, swap)  4.31 us
    ppermute x2, starting transfers between devices, shifted(): return lax.ppermute(x, axis, pairs)  3.91 us
    pallas_call x1, Pallas kernels, shards(): pl.pallas_call(terms_kernel, in_specs=[VMEM] * 4, out_specs=[VMEM] * 2, o...  1.81 us
  transfers between devices with their start and end apart: 7, of which 4 were waited for; matrix products, arithmetic and copies ran while one was open for 0% of the time, Pallas kernels for 43%

profile of v6, /device:TPU:0, one launch (start us, length us, event | category | flops | bytes accessed | tf_op | source)
XLA Modules:
  0.0 51.2 jit_solution(901088297084414021)
XLA Ops:
  0.6 0.0 copy-start
  0.6 0.0 copy-start.2
  0.7 0.0 copy-start.1
  0.7 1.4 %shard_map.70 = bf16[32,1,80,256]{3,2,1,0:T(8,128)(2,1)S(1)} custom-call(bf16[32,4,80,256]{3,2,1,0:T(8,128)(2,1)} %volume.5), custom_call_target="tpu_custom_call" | custom-call | bytes 3145728 | tf_op jit(solution)/shard_map/pallas_call | solution.py:390
  2.1 2.4 %collective-permute-start = (bf16[32,1,80,256]{3,2,1,0:T(8,128)(2,1)S(1)}, bf16[32,1,80,256]{3,2,1,0:T(8,128)(2,1)S(1)}, u32[]{:S(2)}, u32[]{:S(2)}) collective-permute-start(bf16[32,1,80,256]{3,2,1,0:T(8,128)(2,1)S(1)} %shard_map.70), channel_id=1, source_target_pairs={{0,1},{1,2},{2,3},{3,4},{4,5},{5,6},{6,7},{7,8},{8,9},{9,10},{10,1... | collective-permute-start | bytes 3932168 | tf_op jit(solution)/shard_map/ppermute | solution.py:381
  4.5 0.0 copy-done
  4.5 0.0 copy-done.2
  4.6 0.0 copy-done.1
  4.6 4.9 %shard_map.67 = (bf16[2,81,96,128]{3,2,1,0:T(8,128)(2,1)S(1)}, f32[40,64,128]{2,1,0:T(8,128)S(1)}, bf16[40,64,128]{2,1,0:T(8,128)(2,1)S(1)}, bf16[64,864]{1,0:T(8,128)(2,1)S(1)}, bf16[3,128,256]{2,1,0:T(8,128)(2,1)S(1)}) custom-call(bf16[32,4,80,256]{3,2,1,0:T(8,128)(2,1)} %volume.5, bf16[3,3,3,32,64]{4,3,2,1,0:T(8,128)(2,1)S(1)} %copy-done.1, ...), custom_call_target="tpu_custom_call" | custom-call | flops 5000000000 | bytes 10485760 | tf_op jit(solution)/shard_map/pallas_call | solution.py:403
  9.5 6.4 %shard_map.68 = (bf16[41,128,128]{2,1,0:T(8,128)(2,1)S(1)}, f32[592,128]{1,0:T(8,128)S(1)}) custom-call(bf16[32,4,80,256]{3,2,1,0:T(8,128)(2,1)} %volume.5, bf16[2,81,96,128]{3,2,1,0:T(8,128)(2,1)S(1)} %get-tuple-element.38.lines, bf16[64,864]{1,0:T(8,128)(2,1)S(1)} %get-tuple-element.39.full, f32[1,64]{1,0:T(1,128)S(1)} %bitcast.4, ...), custom_call_target="tpu_custom_call" | custom-call | flops 6000000000 | bytes 10485760 | tf_op jit(solution)/shard_map/pallas_call | solution.py:423
  15.9 2.0 %shard_map.69.refs_0_ = bf16[32,4,80,256]{3,2,1,0:T(8,128)(2,1)} custom-call(bf16[3,128,256]{2,1,0:T(8,128)(2,1)S(1)} %get-tuple-element.37.refs_0_.refs_1_, bf16[41,128,128]{2,1,0:T(8,128)(2,1)S(1)} %get-tuple-element.40.refs_1_.refs_3_.refs_2_), custom_call_target="tpu_custom_call" | custom-call | flops 1000000 | bytes 1000 | tf_op jit(solution)/shard_map/pallas_call | solution.py:339
  18.0 0.0 collective-permute-done.halo
  18.0 1.8 %shard_map.71 = (bf16[41,128,128]{2,1,0:T(8,128)(2,1)S(1)}, bf16[40,64,128]{2,1,0:T(8,128)(2,1)S(1)}, bf16[81,96,128]{2,1,0:T(8,128)(2,1)S(1)}) custom-call(bf16[32,1,80,256]{3,2,1,0:T(8,128)(2,1)S(1)} %collective-permute-done.halo, f32[40,64,128]{2,1,0:T(8,128)S(1)} %get-tuple-element.42.pre, bf16[40,64,128]{2,1,0:T(8,128)(2,1)S(1)} %get-tuple-element.43.upstream, ...), custom_call_target="tpu_custom_call" | custom-call | flops 3000000000 | bytes 6291456 | tf_op jit(solution)/shard_map/pallas_call | solution.py:443
  19.7 1.5 %collective-permute-start.3 = (bf16[40,64,128]{2,1,0:T(8,128)(2,1)S(1)}, bf16[40,64,128]{2,1,0:T(8,128)(2,1)S(1)}, u32[]{:S(2)}, u32[]{:S(2)}) collective-permute-start(bf16[40,64,128]{2,1,0:T(8,128)(2,1)S(1)} %get-tuple-element.57), channel_id=1, source_target_pairs={{1,0},{2,1},{3,2},{4,3},{5,4},{6,5},{7,6},{8,7},{9,8},{10,9},{11,1... | collective-permute-start | bytes 1966088 | tf_op jit(solution)/shard_map/ppermute | solution.py:381
  21.2 1.8 %shard_map.72 = (f32[224,128]{1,0:T(8,128)S(1)}, f32[224,128]{1,0:T(8,128)S(1)}) custom-call(bf16[81,96,128]{2,1,0:T(8,128)(2,1)S(1)} %get-tuple-element.44.below, bf16[2,81,96,128]{3,2,1,0:T(8,128)(2,1)S(1)} %get-tuple-element.38.lines, bf16[41,128,128]{2,1,0:T(8,128)(2,1)S(1)} %get-tuple-element.45.grads.refs_2_, f32[592,128]{1,0:T(8,128)S(1)} %get-tuple-element.46.terms_in), custom_call_target="tpu_custom_call" | custom-call | flops 100000000 | bytes 100000 | tf_op jit(solution)/shard_map/pallas_call | solution.py:454
  23.0 4.3 %collective-permute-start.1 = (f32[224,128]{1,0:T(8,128)S(1)}, f32[224,128]{1,0:T(8,128)S(1)}, u32[]{:S(2)}, u32[]{:S(2)}) collective-permute-start(f32[224,128]{1,0:T(8,128)S(1)} %get-tuple-element.51), channel_id=1, source_target_pairs={{0,1},{1,0},{2,3},{3,2},{4,5},{5,4},{6,7},{7,6},{8,9},{9,8},{10,11... | collective-permute-start | bytes 344072 | tf_op jit(solution)/shard_map/ppermute | solution.py:360
  27.3 2.0 %shard_map.73.refs_0_ = bf16[32,4,80,256]{3,2,1,0:T(8,128)(2,1)} custom-call(bf16[32,4,80,256]{3,2,1,0:T(8,128)(2,1)} %shard_map.69.refs_0_, bf16[3,128,256]{2,1,0:T(8,128)(2,1)S(1)} %get-tuple-element.37.refs_0_.refs_1_, bf16[41,128,128]{2,1,0:T(8,128)(2,1)S(1)} %get-tuple-element.45.grads.refs_2_), custom_call_target="tpu_custom_call", output_to_operand_aliasing={{}: (0, {})} | custom-call | flops 1000000 | bytes 1000 | tf_op jit(solution)/shard_map/pallas_call | solution.py:339
  29.3 0.0 collective-permute-done.1
  29.4 2.9 %collective-permute-start.2 = (f32[224,128]{1,0:T(8,128)S(1)}, f32[224,128]{1,0:T(8,128)S(1)}, u32[]{:S(2)}, u32[]{:S(2)}) collective-permute-start(f32[224,128]{1,0:T(8,128)S(1)} %add.12), channel_id=1, source_target_pairs={{0,2},{1,3},{2,0},{3,1},{4,6},{5,7},{6,4},{7,5},{8,10},{9,11},{10,... | collective-permute-start | bytes 344072 | tf_op jit(solution)/shard_map/ppermute | solution.py:367
  32.3 2.4 %shard_map.74.refs_0_ = bf16[32,4,80,256]{3,2,1,0:T(8,128)(2,1)} custom-call(bf16[32,4,80,256]{3,2,1,0:T(8,128)(2,1)} %shard_map.73.refs_0_, bf16[3,128,256]{2,1,0:T(8,128)(2,1)S(1)} %get-tuple-element.37.refs_0_.refs_1_, bf16[41,128,128]{2,1,0:T(8,128)(2,1)S(1)} %get-tuple-element.45.grads.refs_2_, ...), custom_call_target="tpu_custom_call", output_to_operand_aliasing={{}: (0, {})} | custom-call | flops 1000000 | bytes 1000 | tf_op jit(solution)/shard_map/pallas_call | solution.py:339
  34.7 3.9 %collective-permute-done.2 = f32[224,128]{1,0:T(8,128)S(1)} collective-permute-done((f32[224,128]{1,0:T(8,128)S(1)}, f32[224,128]{1,0:T(8,128)S(1)}, u32[]{:S(2)}, u32[]{:S(2)}) %collective-permute-start.2) | collective-permute-done | bytes 114720 | tf_op jit(solution)/shard_map/ppermute | solution.py:367
  38.7 0.0 collective-permute-done.3.refs_3_
  38.7 1.6 %collective-permute-start.4 = (f32[224,128]{1,0:T(8,128)S(1)}, f32[224,128]{1,0:T(8,128)S(1)}, u32[]{:S(2)}, u32[]{:S(2)}) collective-permute-start(f32[224,128]{1,0:T(8,128)S(1)} %add.13), channel_id=1, source_target_pairs={{0,4},{1,5},{2,6},{3,7},{4,0},{5,1},{6,2},{7,3},{8,12},{9,13},{10,... | collective-permute-start | bytes 344072 | tf_op jit(solution)/shard_map/ppermute | solution.py:367
  40.3 2.5 %shard_map.75 = bf16[32,4,80,256]{3,2,1,0:T(8,128)(2,1)} custom-call(bf16[32,4,80,256]{3,2,1,0:T(8,128)(2,1)} %shard_map.74.refs_0_, bf16[3,128,256]{2,1,0:T(8,128)(2,1)S(1)} %get-tuple-element.37.refs_0_.refs_1_, bf16[41,128,128]{2,1,0:T(8,128)(2,1)S(1)} %get-tuple-element.40.refs_1_.refs_3_.refs_2_, ...), custom_call_target="tpu_custom_call", output_to_operand_aliasing={{}: (0, {})} | custom-call | flops 1000000 | bytes 1000 | tf_op jit(solution)/shard_map/pallas_call | solution.py:339
  42.8 0.9 %collective-permute-done.4 = f32[224,128]{1,0:T(8,128)S(1)} collective-permute-done((f32[224,128]{1,0:T(8,128)S(1)}, f32[224,128]{1,0:T(8,128)S(1)}, u32[]{:S(2)}, u32[]{:S(2)}) %collective-permute-start.4) | collective-permute-done | bytes 114720 | tf_op jit(solution)/shard_map/ppermute | solution.py:367
  43.8 2.7 %collective-permute-start.5 = (bf16[224,128]{1,0:T(8,128)(2,1)S(1)}, bf16[224,128]{1,0:T(8,128)(2,1)S(1)}, u32[]{:S(2)}, u32[]{:S(2)}) collective-permute-start(bf16[224,128]{1,0:T(8,128)(2,1)S(1)} %add_convert_fusion), channel_id=1, source_target_pairs={{0,8},{1,9},{2,10},{3,11},{4,12},{5,13},{6,14},{7,15},{8,0},{9,1},... | collective-permute-start | bytes 172040 | tf_op jit(solution)/shard_map/ppermute | solution.py:367
  46.4 2.5 %collective-permute-done.5 = bf16[224,128]{1,0:T(8,128)(2,1)S(1)} collective-permute-done((bf16[224,128]{1,0:T(8,128)(2,1)S(1)}, bf16[224,128]{1,0:T(8,128)(2,1)S(1)}, u32[]{:S(2)}, u32[]{:S(2)}) %collective-permute-start.5) | collective-permute-done | bytes 57376 | tf_op jit(solution)/shard_map/ppermute | solution.py:367
  48.9 0.1 collective-permute-start.6
  49.0 1.3 %collective-permute-done.6.got = f32[224,128]{1,0:T(8,128)S(1)} collective-permute-done((f32[224,128]{1,0:T(8,128)S(1)}, f32[224,128]{1,0:T(8,128)S(1)}, u32[]{:S(2)}, u32[]{:S(2)}) %collective-permute-start.6) | collective-permute-done | bytes 114720 | tf_op jit(solution)/shard_map/ppermute | solution.py:375
  50.3 0.9 %shard_map.76 = (f32[3,3,96,64]{3,2,1,0:T(8,128)}, f32[1,64]{1,0:T(1,128)}) custom-call(f32[224,128]{1,0:T(8,128)S(1)} %convert_add_fusion.mine, f32[224,128]{1,0:T(8,128)S(1)} %collective-permute-done.6.got), custom_call_target="tpu_custom_call" | custom-call | tf_op jit(solution)/shard_map/pallas_call | solution.py:476
  (4 shorter events, 0.1 us)
Async XLA Ops:
  0.6 3.9 %copy-start = (bf16[64,2,40,128]{3,2,1,0:T(8,128)(2,1)S(1)}, bf16[64,2,40,128]{3,2,1,0:T(8,128)(2,1)}, u32[]{:S(2)}) copy-start(bf16[64,2,40,128]{3,2,1,0:T(8,128)(2,1)} %upstream.3) | copy-start | bytes 3932164
  0.6 3.9 %copy-start.2 = (f32[64]{0:T(128)S(1)}, f32[64]{0:T(128)}, u32[]{:S(2)}) copy-start(f32[64]{0:T(128)} %param.6) | copy-start | bytes 772
  0.7 3.9 %copy-start.1 = (bf16[3,3,3,32,64]{4,3,2,1,0:T(8,128)(2,1)S(1)}, bf16[3,3,3,32,64]{4,3,2,1,0:T(8,128)(2,1)}, u32[]{:S(2)}) copy-start(bf16[3,3,3,32,64]{4,3,2,1,0:T(8,128)(2,1)} %weights_in.1) | copy-start | bytes 331780
  2.1 15.9 %collective-permute-start = (bf16[32,1,80,256]{3,2,1,0:T(8,128)(2,1)S(1)}, bf16[32,1,80,256]{3,2,1,0:T(8,128)(2,1)S(1)}, u32[]{:S(2)}, u32[]{:S(2)}) collective-permute-start(bf16[32,1,80,256]{3,2,1,0:T(8,128)(2,1)S(1)} %shard_map.70), channel_id=1, source_target_pairs={{0,1},{1,2},{2,3},{3,4},{4,5},{5,6},{6,7},{7,8},{8,9},{9,10},{10,1... | collective-permute-start | bytes 3932168 | tf_op jit(solution)/shard_map/ppermute | solution.py:381
  19.7 18.9 %collective-permute-start.3 = (bf16[40,64,128]{2,1,0:T(8,128)(2,1)S(1)}, bf16[40,64,128]{2,1,0:T(8,128)(2,1)S(1)}, u32[]{:S(2)}, u32[]{:S(2)}) collective-permute-start(bf16[40,64,128]{2,1,0:T(8,128)(2,1)S(1)} %get-tuple-element.57), channel_id=1, source_target_pairs={{1,0},{2,1},{3,2},{4,3},{5,4},{6,5},{7,6},{8,7},{9,8},{10,9},{11,1... | collective-permute-start | bytes 1966088 | tf_op jit(solution)/shard_map/ppermute | solution.py:381
  23.0 6.3 %collective-permute-start.1 = (f32[224,128]{1,0:T(8,128)S(1)}, f32[224,128]{1,0:T(8,128)S(1)}, u32[]{:S(2)}, u32[]{:S(2)}) collective-permute-start(f32[224,128]{1,0:T(8,128)S(1)} %get-tuple-element.51), channel_id=1, source_target_pairs={{0,1},{1,0},{2,3},{3,2},{4,5},{5,4},{6,7},{7,6},{8,9},{9,8},{10,11... | collective-permute-start | bytes 344072 | tf_op jit(solution)/shard_map/ppermute | solution.py:360
  29.4 9.3 %collective-permute-start.2 = (f32[224,128]{1,0:T(8,128)S(1)}, f32[224,128]{1,0:T(8,128)S(1)}, u32[]{:S(2)}, u32[]{:S(2)}) collective-permute-start(f32[224,128]{1,0:T(8,128)S(1)} %add.12), channel_id=1, source_target_pairs={{0,2},{1,3},{2,0},{3,1},{4,6},{5,7},{6,4},{7,5},{8,10},{9,11},{10,... | collective-permute-start | bytes 344072 | tf_op jit(solution)/shard_map/ppermute | solution.py:367
  38.7 5.1 %collective-permute-start.4 = (f32[224,128]{1,0:T(8,128)S(1)}, f32[224,128]{1,0:T(8,128)S(1)}, u32[]{:S(2)}, u32[]{:S(2)}) collective-permute-start(f32[224,128]{1,0:T(8,128)S(1)} %add.13), channel_id=1, source_target_pairs={{0,4},{1,5},{2,6},{3,7},{4,0},{5,1},{6,2},{7,3},{8,12},{9,13},{10,... | collective-permute-start | bytes 344072 | tf_op jit(solution)/shard_map/ppermute | solution.py:367
  43.8 5.1 %collective-permute-start.5 = (bf16[224,128]{1,0:T(8,128)(2,1)S(1)}, bf16[224,128]{1,0:T(8,128)(2,1)S(1)}, u32[]{:S(2)}, u32[]{:S(2)}) collective-permute-start(bf16[224,128]{1,0:T(8,128)(2,1)S(1)} %add_convert_fusion), channel_id=1, source_target_pairs={{0,8},{1,9},{2,10},{3,11},{4,12},{5,13},{6,14},{7,15},{8,0},{9,1},... | collective-permute-start | bytes 172040 | tf_op jit(solution)/shard_map/ppermute | solution.py:367
  48.9 1.4 %collective-permute-start.6 = (f32[224,128]{1,0:T(8,128)S(1)}, f32[224,128]{1,0:T(8,128)S(1)}, u32[]{:S(2)}, u32[]{:S(2)}) collective-permute-start(f32[224,128]{1,0:T(8,128)S(1)} %convert_add_fusion.mine), channel_id=1, source_target_pairs={{0,1},{1,0},{2,3},{3,2},{4,5},{5,4},{6,7},{7,6},{8,9},{9,8},{10,11... | collective-permute-start | bytes 344072 | tf_op jit(solution)/shard_map/ppermute | solution.py:375

commit v7 on v6

--- a/solution.py
+++ b/solution.py
@@ -363,7 +363,7 @@
     value = kept + got
     step = 2
     while step < peers:
-        value, total = lax.optimization_barrier((value.astype((BF if 2 * step == peers else F32)), total))
+        value, total = lax.optimization_barrier((value.astype((BF if 4 * step >= peers else F32)), total))
         got = lax.ppermute(value, axis, [(i, i ^ step) for i in range(peers)])
         if works:
             total, above = works.pop(0)(total, above)

time: 51.5 us -> 50.6 us (0.983)
  waiting for transfers between devices: 8.66 us -> 7.83 us
    ppermute x3, waiting for transfers between devices: 7.34 us -> 6.52 us  [all_sum(): got = lax.ppermute(value, axis, [(i, i ^ step) for i in range(peers)])]
  transfers between devices with their start and end apart: 7 -> 7, of which waited for: 4 -> 4; matrix products, arithmetic and copies ran while one was open for 0% -> 0% of each run, Pallas kernels for 43% -> 44%
where the time goes in v7:
time: 50.6 us; the launch traced here: 50.4 us
  Pallas kernels  26.2 us (52%)
  starting transfers between devices  15.5 us (31%)
  waiting for transfers between devices  7.83 us (15%)
  between operations  0.8 us (2%)
    pallas_call x4, Pallas kernels, back_plane(): pl.pallas_call(functools.partial(back_kernel, z, len(above) > 0, fresh, a...  8.93 us
    ppermute x3, starting transfers between devices, all_sum(): got = lax.ppermute(value, axis, [(i, i ^ step) for i in range(peers)])  7.22 us
    ppermute x3, waiting for transfers between devices, all_sum(): got = lax.ppermute(value, axis, [(i, i ^ step) for i in range(peers)])  6.52 us
    pallas_call x1, Pallas kernels, shards(): pl.pallas_call(upper_kernel, in_specs=[ANY, VMEM, VMEM, VMEM, ANY], out_s...  6.45 us
    pallas_call x1, Pallas kernels, shards(): pl.pallas_call(lower_kernel, in_specs=[ANY, ANY, VMEM, ANY], out_specs=[V...  4.92 us
    ppermute x1, starting transfers between devices, all_sum(): got = lax.ppermute(sent, axis, swap)  4.31 us
    ppermute x2, starting transfers between devices, shifted(): return lax.ppermute(x, axis, pairs)  3.91 us
    pallas_call x1, Pallas kernels, shards(): pl.pallas_call(terms_kernel, in_specs=[VMEM] * 4, out_specs=[VMEM] * 2, o...  1.81 us
  transfers between devices with their start and end apart: 7, of which 4 were waited for; matrix products, arithmetic and copies ran while one was open for 0% of the time, Pallas kernels for 44%

profile of v7, /device:TPU:0, one launch (start us, length us, event | category | flops | bytes accessed | tf_op | source)
XLA Modules:
  0.0 50.4 jit_solution(6293496868882330934)
XLA Ops:
  0.6 0.0 copy-start
  0.6 0.0 copy-start.2
  0.7 0.0 copy-start.1
  0.7 1.4 %shard_map.70 = bf16[32,1,80,256]{3,2,1,0:T(8,128)(2,1)S(1)} custom-call(bf16[32,4,80,256]{3,2,1,0:T(8,128)(2,1)} %volume.5), custom_call_target="tpu_custom_call" | custom-call | bytes 3145728 | tf_op jit(solution)/shard_map/pallas_call | solution.py:390
  2.1 2.4 %collective-permute-start = (bf16[32,1,80,256]{3,2,1,0:T(8,128)(2,1)S(1)}, bf16[32,1,80,256]{3,2,1,0:T(8,128)(2,1)S(1)}, u32[]{:S(2)}, u32[]{:S(2)}) collective-permute-start(bf16[32,1,80,256]{3,2,1,0:T(8,128)(2,1)S(1)} %shard_map.70), channel_id=1, source_target_pairs={{0,1},{1,2},{2,3},{3,4},{4,5},{5,6},{6,7},{7,8},{8,9},{9,10},{10,1... | collective-permute-start | bytes 3932168 | tf_op jit(solution)/shard_map/ppermute | solution.py:381
  4.5 0.0 copy-done
  4.5 0.0 copy-done.2
  4.6 0.0 copy-done.1
  4.6 4.9 %shard_map.67 = (bf16[2,81,96,128]{3,2,1,0:T(8,128)(2,1)S(1)}, f32[40,64,128]{2,1,0:T(8,128)S(1)}, bf16[40,64,128]{2,1,0:T(8,128)(2,1)S(1)}, bf16[64,864]{1,0:T(8,128)(2,1)S(1)}, bf16[3,128,256]{2,1,0:T(8,128)(2,1)S(1)}) custom-call(bf16[32,4,80,256]{3,2,1,0:T(8,128)(2,1)} %volume.5, bf16[3,3,3,32,64]{4,3,2,1,0:T(8,128)(2,1)S(1)} %copy-done.1, ...), custom_call_target="tpu_custom_call" | custom-call | flops 5000000000 | bytes 10485760 | tf_op jit(solution)/shard_map/pallas_call | solution.py:403
  9.5 6.4 %shard_map.68 = (bf16[41,128,128]{2,1,0:T(8,128)(2,1)S(1)}, f32[592,128]{1,0:T(8,128)S(1)}) custom-call(bf16[32,4,80,256]{3,2,1,0:T(8,128)(2,1)} %volume.5, bf16[2,81,96,128]{3,2,1,0:T(8,128)(2,1)S(1)} %get-tuple-element.38.lines, bf16[64,864]{1,0:T(8,128)(2,1)S(1)} %get-tuple-element.39.full, f32[1,64]{1,0:T(1,128)S(1)} %bitcast.4, ...), custom_call_target="tpu_custom_call" | custom-call | flops 6000000000 | bytes 10485760 | tf_op jit(solution)/shard_map/pallas_call | solution.py:423
  15.9 2.0 %shard_map.69.refs_0_ = bf16[32,4,80,256]{3,2,1,0:T(8,128)(2,1)} custom-call(bf16[3,128,256]{2,1,0:T(8,128)(2,1)S(1)} %get-tuple-element.37.refs_0_.refs_1_, bf16[41,128,128]{2,1,0:T(8,128)(2,1)S(1)} %get-tuple-element.40.refs_1_.refs_3_.refs_2_), custom_call_target="tpu_custom_call" | custom-call | flops 1000000 | bytes 1000 | tf_op jit(solution)/shard_map/pallas_call | solution.py:339
  18.0 0.0 collective-permute-done.halo
  18.0 1.8 %shard_map.71 = (bf16[41,128,128]{2,1,0:T(8,128)(2,1)S(1)}, bf16[40,64,128]{2,1,0:T(8,128)(2,1)S(1)}, bf16[81,96,128]{2,1,0:T(8,128)(2,1)S(1)}) custom-call(bf16[32,1,80,256]{3,2,1,0:T(8,128)(2,1)S(1)} %collective-permute-done.halo, f32[40,64,128]{2,1,0:T(8,128)S(1)} %get-tuple-element.42.pre, bf16[40,64,128]{2,1,0:T(8,128)(2,1)S(1)} %get-tuple-element.43.upstream, ...), custom_call_target="tpu_custom_call" | custom-call | flops 3000000000 | bytes 6291456 | tf_op jit(solution)/shard_map/pallas_call | solution.py:443
  19.7 1.5 %collective-permute-start.3 = (bf16[40,64,128]{2,1,0:T(8,128)(2,1)S(1)}, bf16[40,64,128]{2,1,0:T(8,128)(2,1)S(1)}, u32[]{:S(2)}, u32[]{:S(2)}) collective-permute-start(bf16[40,64,128]{2,1,0:T(8,128)(2,1)S(1)} %get-tuple-element.57), channel_id=1, source_target_pairs={{1,0},{2,1},{3,2},{4,3},{5,4},{6,5},{7,6},{8,7},{9,8},{10,9},{11,1... | collective-permute-start | bytes 1966088 | tf_op jit(solution)/shard_map/ppermute | solution.py:381
  21.2 1.8 %shard_map.72 = (f32[224,128]{1,0:T(8,128)S(1)}, f32[224,128]{1,0:T(8,128)S(1)}) custom-call(bf16[81,96,128]{2,1,0:T(8,128)(2,1)S(1)} %get-tuple-element.44.below, bf16[2,81,96,128]{3,2,1,0:T(8,128)(2,1)S(1)} %get-tuple-element.38.lines, bf16[41,128,128]{2,1,0:T(8,128)(2,1)S(1)} %get-tuple-element.45.grads.refs_2_, f32[592,128]{1,0:T(8,128)S(1)} %get-tuple-element.46.terms_in), custom_call_target="tpu_custom_call" | custom-call | flops 100000000 | bytes 100000 | tf_op jit(solution)/shard_map/pallas_call | solution.py:454
  23.0 4.3 %collective-permute-start.1 = (f32[224,128]{1,0:T(8,128)S(1)}, f32[224,128]{1,0:T(8,128)S(1)}, u32[]{:S(2)}, u32[]{:S(2)}) collective-permute-start(f32[224,128]{1,0:T(8,128)S(1)} %get-tuple-element.51), channel_id=1, source_target_pairs={{0,1},{1,0},{2,3},{3,2},{4,5},{5,4},{6,7},{7,6},{8,9},{9,8},{10,11... | collective-permute-start | bytes 344072 | tf_op jit(solution)/shard_map/ppermute | solution.py:360
  27.3 2.0 %shard_map.73.refs_0_ = bf16[32,4,80,256]{3,2,1,0:T(8,128)(2,1)} custom-call(bf16[32,4,80,256]{3,2,1,0:T(8,128)(2,1)} %shard_map.69.refs_0_, bf16[3,128,256]{2,1,0:T(8,128)(2,1)S(1)} %get-tuple-element.37.refs_0_.refs_1_, bf16[41,128,128]{2,1,0:T(8,128)(2,1)S(1)} %get-tuple-element.45.grads.refs_2_), custom_call_target="tpu_custom_call", output_to_operand_aliasing={{}: (0, {})} | custom-call | flops 1000000 | bytes 1000 | tf_op jit(solution)/shard_map/pallas_call | solution.py:339
  29.3 0.0 collective-permute-done.1
  29.4 2.9 %collective-permute-start.2 = (f32[224,128]{1,0:T(8,128)S(1)}, f32[224,128]{1,0:T(8,128)S(1)}, u32[]{:S(2)}, u32[]{:S(2)}) collective-permute-start(f32[224,128]{1,0:T(8,128)S(1)} %add.12), channel_id=1, source_target_pairs={{0,2},{1,3},{2,0},{3,1},{4,6},{5,7},{6,4},{7,5},{8,10},{9,11},{10,... | collective-permute-start | bytes 344072 | tf_op jit(solution)/shard_map/ppermute | solution.py:367
  32.3 2.4 %shard_map.74.refs_0_ = bf16[32,4,80,256]{3,2,1,0:T(8,128)(2,1)} custom-call(bf16[32,4,80,256]{3,2,1,0:T(8,128)(2,1)} %shard_map.73.refs_0_, bf16[3,128,256]{2,1,0:T(8,128)(2,1)S(1)} %get-tuple-element.37.refs_0_.refs_1_, bf16[41,128,128]{2,1,0:T(8,128)(2,1)S(1)} %get-tuple-element.45.grads.refs_2_, ...), custom_call_target="tpu_custom_call", output_to_operand_aliasing={{}: (0, {})} | custom-call | flops 1000000 | bytes 1000 | tf_op jit(solution)/shard_map/pallas_call | solution.py:339
  34.7 3.9 %collective-permute-done.2 = f32[224,128]{1,0:T(8,128)S(1)} collective-permute-done((f32[224,128]{1,0:T(8,128)S(1)}, f32[224,128]{1,0:T(8,128)S(1)}, u32[]{:S(2)}, u32[]{:S(2)}) %collective-permute-start.2) | collective-permute-done | bytes 114720 | tf_op jit(solution)/shard_map/ppermute | solution.py:367
  38.7 0.0 collective-permute-done.3.refs_3_
  38.7 1.6 %collective-permute-start.4 = (bf16[224,128]{1,0:T(8,128)(2,1)S(1)}, bf16[224,128]{1,0:T(8,128)(2,1)S(1)}, u32[]{:S(2)}, u32[]{:S(2)}) collective-permute-start(bf16[224,128]{1,0:T(8,128)(2,1)S(1)} %add_convert_fusion.1), channel_id=1, source_target_pairs={{0,4},{1,5},{2,6},{3,7},{4,0},{5,1},{6,2},{7,3},{8,12},{9,13},{10,... | collective-permute-start | bytes 172040 | tf_op jit(solution)/shard_map/ppermute | solution.py:367
  40.3 2.5 %shard_map.75 = bf16[32,4,80,256]{3,2,1,0:T(8,128)(2,1)} custom-call(bf16[32,4,80,256]{3,2,1,0:T(8,128)(2,1)} %shard_map.74.refs_0_, bf16[3,128,256]{2,1,0:T(8,128)(2,1)S(1)} %get-tuple-element.37.refs_0_.refs_1_, bf16[41,128,128]{2,1,0:T(8,128)(2,1)S(1)} %get-tuple-element.40.refs_1_.refs_3_.refs_2_, ...), custom_call_target="tpu_custom_call", output_to_operand_aliasing={{}: (0, {})} | custom-call | flops 1000000 | bytes 1000 | tf_op jit(solution)/shard_map/pallas_call | solution.py:339
  42.8 0.1 collective-permute-done.4
  43.0 2.6 %collective-permute-start.5 = (bf16[224,128]{1,0:T(8,128)(2,1)S(1)}, bf16[224,128]{1,0:T(8,128)(2,1)S(1)}, u32[]{:S(2)}, u32[]{:S(2)}) collective-permute-start(bf16[224,128]{1,0:T(8,128)(2,1)S(1)} %add_convert_fusion), channel_id=1, source_target_pairs={{0,8},{1,9},{2,10},{3,11},{4,12},{5,13},{6,14},{7,15},{8,0},{9,1},... | collective-permute-start | bytes 172040 | tf_op jit(solution)/shard_map/ppermute | solution.py:367
  45.6 2.5 %collective-permute-done.5 = bf16[224,128]{1,0:T(8,128)(2,1)S(1)} collective-permute-done((bf16[224,128]{1,0:T(8,128)(2,1)S(1)}, bf16[224,128]{1,0:T(8,128)(2,1)S(1)}, u32[]{:S(2)}, u32[]{:S(2)}) %collective-permute-start.5) | collective-permute-done | bytes 57376 | tf_op jit(solution)/shard_map/ppermute | solution.py:367
  48.1 0.1 collective-permute-start.6
  48.2 1.3 %collective-permute-done.6.got = f32[224,128]{1,0:T(8,128)S(1)} collective-permute-done((f32[224,128]{1,0:T(8,128)S(1)}, f32[224,128]{1,0:T(8,128)S(1)}, u32[]{:S(2)}, u32[]{:S(2)}) %collective-permute-start.6) | collective-permute-done | bytes 114720 | tf_op jit(solution)/shard_map/ppermute | solution.py:375
  49.5 0.9 %shard_map.76 = (f32[3,3,96,64]{3,2,1,0:T(8,128)}, f32[1,64]{1,0:T(1,128)}) custom-call(f32[224,128]{1,0:T(8,128)S(1)} %convert_add_fusion.mine, f32[224,128]{1,0:T(8,128)S(1)} %collective-permute-done.6.got), custom_call_target="tpu_custom_call" | custom-call | tf_op jit(solution)/shard_map/pallas_call | solution.py:476
  (4 shorter events, 0.1 us)
Async XLA Ops:
  0.6 3.9 %copy-start = (bf16[64,2,40,128]{3,2,1,0:T(8,128)(2,1)S(1)}, bf16[64,2,40,128]{3,2,1,0:T(8,128)(2,1)}, u32[]{:S(2)}) copy-start(bf16[64,2,40,128]{3,2,1,0:T(8,128)(2,1)} %upstream.3) | copy-start | bytes 3932164
  0.6 3.9 %copy-start.2 = (f32[64]{0:T(128)S(1)}, f32[64]{0:T(128)}, u32[]{:S(2)}) copy-start(f32[64]{0:T(128)} %param.6) | copy-start | bytes 772
  0.7 3.9 %copy-start.1 = (bf16[3,3,3,32,64]{4,3,2,1,0:T(8,128)(2,1)S(1)}, bf16[3,3,3,32,64]{4,3,2,1,0:T(8,128)(2,1)}, u32[]{:S(2)}) copy-start(bf16[3,3,3,32,64]{4,3,2,1,0:T(8,128)(2,1)} %weights_in.1) | copy-start | bytes 331780
  2.1 15.9 %collective-permute-start = (bf16[32,1,80,256]{3,2,1,0:T(8,128)(2,1)S(1)}, bf16[32,1,80,256]{3,2,1,0:T(8,128)(2,1)S(1)}, u32[]{:S(2)}, u32[]{:S(2)}) collective-permute-start(bf16[32,1,80,256]{3,2,1,0:T(8,128)(2,1)S(1)} %shard_map.70), channel_id=1, source_target_pairs={{0,1},{1,2},{2,3},{3,4},{4,5},{5,6},{6,7},{7,8},{8,9},{9,10},{10,1... | collective-permute-start | bytes 3932168 | tf_op jit(solution)/shard_map/ppermute | solution.py:381
  19.7 18.9 %collective-permute-start.3 = (bf16[40,64,128]{2,1,0:T(8,128)(2,1)S(1)}, bf16[40,64,128]{2,1,0:T(8,128)(2,1)S(1)}, u32[]{:S(2)}, u32[]{:S(2)}) collective-permute-start(bf16[40,64,128]{2,1,0:T(8,128)(2,1)S(1)} %get-tuple-element.57), channel_id=1, source_target_pairs={{1,0},{2,1},{3,2},{4,3},{5,4},{6,5},{7,6},{8,7},{9,8},{10,9},{11,1... | collective-permute-start | bytes 1966088 | tf_op jit(solution)/shard_map/ppermute | solution.py:381
  23.0 6.3 %collective-permute-start.1 = (f32[224,128]{1,0:T(8,128)S(1)}, f32[224,128]{1,0:T(8,128)S(1)}, u32[]{:S(2)}, u32[]{:S(2)}) collective-permute-start(f32[224,128]{1,0:T(8,128)S(1)} %get-tuple-element.51), channel_id=1, source_target_pairs={{0,1},{1,0},{2,3},{3,2},{4,5},{5,4},{6,7},{7,6},{8,9},{9,8},{10,11... | collective-permute-start | bytes 344072 | tf_op jit(solution)/shard_map/ppermute | solution.py:360
  29.4 9.3 %collective-permute-start.2 = (f32[224,128]{1,0:T(8,128)S(1)}, f32[224,128]{1,0:T(8,128)S(1)}, u32[]{:S(2)}, u32[]{:S(2)}) collective-permute-start(f32[224,128]{1,0:T(8,128)S(1)} %add.12), channel_id=1, source_target_pairs={{0,2},{1,3},{2,0},{3,1},{4,6},{5,7},{6,4},{7,5},{8,10},{9,11},{10,... | collective-permute-start | bytes 344072 | tf_op jit(solution)/shard_map/ppermute | solution.py:367
  38.7 4.2 %collective-permute-start.4 = (bf16[224,128]{1,0:T(8,128)(2,1)S(1)}, bf16[224,128]{1,0:T(8,128)(2,1)S(1)}, u32[]{:S(2)}, u32[]{:S(2)}) collective-permute-start(bf16[224,128]{1,0:T(8,128)(2,1)S(1)} %add_convert_fusion.1), channel_id=1, source_target_pairs={{0,4},{1,5},{2,6},{3,7},{4,0},{5,1},{6,2},{7,3},{8,12},{9,13},{10,... | collective-permute-start | bytes 172040 | tf_op jit(solution)/shard_map/ppermute | solution.py:367
  43.0 5.1 %collective-permute-start.5 = (bf16[224,128]{1,0:T(8,128)(2,1)S(1)}, bf16[224,128]{1,0:T(8,128)(2,1)S(1)}, u32[]{:S(2)}, u32[]{:S(2)}) collective-permute-start(bf16[224,128]{1,0:T(8,128)(2,1)S(1)} %add_convert_fusion), channel_id=1, source_target_pairs={{0,8},{1,9},{2,10},{3,11},{4,12},{5,13},{6,14},{7,15},{8,0},{9,1},... | collective-permute-start | bytes 172040 | tf_op jit(solution)/shard_map/ppermute | solution.py:367
  48.1 1.4 %collective-permute-start.6 = (f32[224,128]{1,0:T(8,128)S(1)}, f32[224,128]{1,0:T(8,128)S(1)}, u32[]{:S(2)}, u32[]{:S(2)}) collective-permute-start(f32[224,128]{1,0:T(8,128)S(1)} %convert_add_fusion.mine), channel_id=1, source_target_pairs={{0,1},{1,0},{2,3},{3,2},{4,5},{5,4},{6,7},{7,6},{8,9},{9,8},{10,11... | collective-permute-start | bytes 344072 | tf_op jit(solution)/shard_map/ppermute | solution.py:375
